TPU v7x, 256 devices: a whole 4x4x8 slice. The times are simulated.
256 devices in a mesh: row: 32 (over z, y), col: 8 (over x, core).
Axes of the slice: x: 4, y: 4, z: 8, core: 2. Of those that a mesh axis runs over, the one named last changes fastest.
Arguments:
- blocks: bfloat16 [32, 8, 224, 128, 128], P('row', 'col'), may hold values from -0.125 to 0.125
- block_rows: int32 [32, 8, 224], P('row', 'col'), may hold values from 0 to 15, as said below
- block_cols: int32 [32, 8, 224], P('row', 'col'), may hold values from 0 to 63, as said below
- live_counts: int32 [32, 8], P('row', 'col'), may hold values from 64 to 224, as said below
- omega: bfloat16 [65536, 256], P(('col', 'row')), may hold values from -6 to 6
- row_scale: float32 [65536], P(('row', 'col')), may hold values from 0.1 to 12
Outputs:
- basis: float32 [65536, 256], P(('row', 'col'))
- factor: float32 [256, 256], replicated
Inputs may be any that keep to these rules, and one draw needn't show every extreme that they name: `block_rows`: local row block of each slot; in each device's first 16 slots every local row block stands once. `block_cols`: local column block of each slot; in each device's first 64 slots every local column block stands once. `live_counts`: at least max(16, 64) on every device; some device has all 224 slots live.
All inputs are finite; a program needn't handle non-finite values.
Results may differ from a plain program's by a relative error of at most 0.0085.
Values may be sent and summed in bfloat16 or wider, within the bound.
No kernel may reach another device: no remote copies, remote signals or barrier semaphores. Data moves between devices by JAX's collectives and lax.ppermute only.
A program may use at most 128 MiB of HBM per device.

v0:
```python
import math

import jax
import jax.numpy as jnp
from jax import lax
from jax.sharding import PartitionSpec as P


def shards(blocks, block_rows, block_cols, live_counts, omega, row_scale):
    slot_total = blocks.shape[2]
    block_size = blocks.shape[3]
    width = omega.shape[1]
    own_rows = omega.shape[0]
    col_count = lax.axis_size("col")
    row_blocks = own_rows * col_count // block_size
    values = blocks[0, 0]
    rows_here = block_rows[0, 0]
    cols_here = block_cols[0, 0]
    count_here = live_counts[0, 0]
    gathered = lax.all_gather(omega, "row", axis=0, tiled=True)
    omega_blocks = gathered.reshape(-1, block_size, width)
    group = 16

    def add_group(index, total):
        start = index * group
        block_group = lax.dynamic_slice_in_dim(values, start, group, 0)
        row_group = lax.dynamic_slice_in_dim(rows_here, start, group, 0)
        col_group = lax.dynamic_slice_in_dim(cols_here, start, group, 0)
        chosen = jnp.take(omega_blocks, col_group, axis=0)
        products = jnp.einsum(
            "nij,njk->nik", block_group, chosen, preferred_element_type=jnp.float32
        )
        live = start + jnp.arange(group, dtype=jnp.int32) < count_here
        onehot = (
            (row_group[None, :] == jnp.arange(row_blocks, dtype=jnp.int32)[:, None]) & live[None, :]
        ).astype(jnp.float32)
        return total + jnp.einsum("rn,nik->rik", onehot, products, precision=lax.Precision.HIGHEST)

    partial_sum = lax.fori_loop(
        0, slot_total // group, add_group, jnp.zeros((row_blocks, block_size, width), jnp.float32)
    )
    partial_sum = partial_sum.reshape(row_blocks * block_size, width)
    summed = lax.psum(partial_sum, "col")
    mine = lax.dynamic_slice_in_dim(summed, lax.axis_index("col") * own_rows, own_rows, 0)
    sketch = mine * row_scale[:, None]
    local_gram = jnp.dot(
        sketch.T, sketch, precision=lax.Precision.HIGHEST, preferred_element_type=jnp.float32
    )
    gram = lax.psum(local_gram, ("row", "col"))
    lower = jnp.linalg.cholesky(gram)
    vertex_total = own_rows * col_count * lax.axis_size("row")
    solved = jax.scipy.linalg.solve_triangular(lower, sketch.T, lower=True)
    basis = solved.T * math.sqrt(vertex_total)
    factor = lower.T / math.sqrt(vertex_total)
    return (basis, factor)


def solution(mesh):
    placed = (
        P("row", "col", None, None, None),
        P("row", "col", None),
        P("row", "col", None),
        P("row", "col"),
        P(("col", "row"), None),
        P(("row", "col")),
    )
    return jax.shard_map(
        shards,
        mesh=mesh,
        in_specs=placed,
        out_specs=(P(("row", "col"), None), P()),
        check_vma=False,
    )
```

profile of v0, /device:TPU:2, one launch (start us, length us, event | category | flops | bytes accessed | tf_op | source)
XLA Modules:
  0.0 649.7 jit_solution(9414910297340598209)
XLA Ops:
  8.0 87.5 %all-gather.2.cloned.1.call-done = bf16[8192,256]{1,0:T(8,128)(2,1)} async-done(((bf16[256,256]{1,0:T(8,128)(2,1)}), bf16[8192,256]{1,0:T(8,128)(2,1)}) %all-gather.2.cloned.1.call-update) | async-done | bytes 4194320 | tf_op jit(solution)/shard_map/all_gather | solution.py:20
  95.4 155.0 %while.16 = (s32[]{:T(128)}, f32[16,128,256]{2,0,1:T(8,128)}, s32[224]{0:T(256)}, s32[]{:T(128)}, bf16[224,128,128]{2,1,0:T(8,128)(2,1)}, /*index=5*/s32[224]{0:...) while((s32[]{:T(128)}, f32[16,128,256]{2,0,1:T(8,128)}, ...), condition=%wide.region_1.0_spmd.clone, body=%wide.region_0.1_spmd.clone.sunk | while | flops 236455552 | bytes 12067037 | solution.py:39
  96.8 2.8 gather_fusion
  99.6 1.6 fusion.46
  101.3 3.7 select_add_fusion.2
  106.4 2.8 gather_fusion
  110.9 5.3 select_add_fusion.2
  117.6 2.8 gather_fusion
  120.4 1.6 fusion.46
  122.1 5.3 select_add_fusion.2
  128.8 2.8 gather_fusion
  131.6 1.6 fusion.46
  133.3 5.3 select_add_fusion.2
  140.0 2.8 gather_fusion
  142.8 1.6 fusion.46
  144.4 5.3 select_add_fusion.2
  151.1 2.8 gather_fusion
  155.6 5.3 select_add_fusion.2
  162.3 2.8 gather_fusion
  165.1 1.6 fusion.46
  166.8 5.3 select_add_fusion.2
  173.5 2.8 gather_fusion
  178.0 5.3 select_add_fusion.2
  184.7 2.8 gather_fusion
  189.2 5.3 select_add_fusion.2
  195.9 2.8 gather_fusion
  198.7 1.6 fusion.46
  200.3 5.3 select_add_fusion.2
  207.1 2.8 gather_fusion
  209.9 1.6 fusion.46
  211.5 5.3 select_add_fusion.2
  218.2 2.8 gather_fusion
  222.7 5.3 select_add_fusion.2
  229.4 2.8 gather_fusion
  232.2 1.6 fusion.46
  233.9 5.3 select_add_fusion.2
  240.6 2.8 gather_fusion
  243.4 1.6 fusion.46
  245.1 5.3 select_add_fusion.2
  250.4 4.1 copy.12
  254.8 65.5 %all-reduce.4.cloned.1.call-done = f32[2048,256]{1,0:T(8,128)} async-done(((f32[2048,256]{1,0:T(8,128)}), f32[2048,256]{1,0:T(8,128)}) %all-reduce.4.cloned.1.call-update) | async-done | bytes 2097168 | tf_op jit(solution)/shard_map/psum | solution.py:43
  320.3 2.4 fusion.20
  323.8 254.8 %all-reduce.6.cloned.1.call-done = f32[256,256]{0,1:T(8,128)} async-done(((f32[256,256]{0,1:T(8,128)}), f32[256,256]{0,1:T(8,128)}) %all-reduce.6.cloned.1.call-update) | async-done | bytes 262160 | tf_op jit(solution)/shard_map/psum | solution.py:49
  580.7 11.7 %cholesky.50 = f32[128,128]{1,0:T(8,128)S(1)} custom-call(f32[128,128]{1,0:T(8,128)S(1)} %cholesky.118), custom_call_target="Cholesky" | custom-call | tf_op jit(solution)/shard_map/jit(cholesky)/cholesky | solution.py:50
  592.4 9.8 %custom-call.15 = f32[1,128,128]{1,2,0:T(8,128)S(1)} custom-call(f32[1,128,128]{2,1,0:T(8,128)S(1)} %get-tuple-element.195), custom_call_target="InvertDiagBlocksLowerTriangular" | custom-call | tf_op jit(solution)/shard_map/jit(cholesky)/cholesky | solution.py:50
  602.7 11.7 %cholesky.105 = f32[128,128]{1,0:T(8,128)S(1)} custom-call(f32[128,128]{1,0:T(8,128)S(1)} %convolution_subtract_fusion.1), custom_call_target="Cholesky" | custom-call | tf_op jit(solution)/shard_map/jit(cholesky)/cholesky | solution.py:50
  616.6 4.1 while.15
  620.7 19.7 %custom-call.16 = f32[2,128,128]{1,2,0:T(8,128)S(1)} custom-call(f32[2,128,128]{2,1,0:T(8,128)S(1)} %get-tuple-element.134), custom_call_target="InvertDiagBlocksLowerTriangular" | custom-call | tf_op jit(solution)/shard_map/jit(_solve_triangular)/triangular_solve | solution.py:52
  (110 shorter events, 40.8 us)
Async XLA Ops:
  7.2 88.2 %all-gather.2.cloned.1.call-start = ((), (), s32[]{:S(2)}) async-start(), calls=%async_computation | async-start | bytes 4325376 | tf_op jit(solution)/shard_map/all_gather | solution.py:20
  7.9 312.4 %all-reduce.4.cloned.1.call-start = ((), (), s32[]{:S(2)}) async-start(), calls=%async_computation.1 | async-start | bytes 4194304 | tf_op jit(solution)/shard_map/psum | solution.py:43
  99.6 1.6 copy-start.1
  109.2 1.6 copy-start.1
  120.4 1.6 copy-start.1
  131.6 1.6 copy-start.1
  142.8 1.6 copy-start.1
  154.0 1.6 copy-start.1
  165.1 1.6 copy-start.1
  176.3 1.6 copy-start.1
  187.5 1.6 copy-start.1
  198.7 1.6 copy-start.1
  209.9 1.6 copy-start.1
  221.0 1.6 copy-start.1
  232.2 1.6 copy-start.1
  243.4 1.6 copy-start.1
  254.5 65.8 %copy-start = (f32[256]{0:T(256)S(1)}, f32[256]{0:T(256)}, u32[]{:S(2)}) copy-start(f32[256]{0:T(256)} %param.13) | copy-start | bytes 3076
  254.5 324.1 %all-reduce.6.cloned.1.call-start = ((), (), s32[]{:S(2)}) async-start(), calls=%async_computation.2 | async-start | bytes 524288 | tf_op jit(solution)/shard_map/psum | solution.py:49
Sparse Core Ops, SparseCore 0:
  10.6 84.7 all-gather.1
  254.6 65.5 all-reduce.3
  326.3 252.2 all-reduce.5
where the time goes:
time: 652 us; the launch traced here: 650 us
  waiting for transfers between devices  408 us (63%)
  matrix products  98.2 us (15%)
  other arithmetic  75.5 us (12%)
  local copies, waits for them, and re-layouts  51.3 us (8%)
  between operations  15.2 us (2%)
    psum x1, waiting for transfers between devices, shards(): gram = lax.psum(local_gram, ('row', 'col'))  255 us
    all_gather x1, waiting for transfers between devices, shards(): gathered = lax.all_gather(omega, 'row', axis=0, tiled=True)  87.5 us
    dot_general x14, matrix products, add_group(): jnp.einsum('rn,nik->rik', onehot, products, precision=lax.Precision.HIGHEST)  72.5 us
    psum x1, waiting for transfers between devices, shards(): summed = lax.psum(partial_sum, 'col')  65.5 us
    gather x14, local copies, waits for them, and re-layouts, add_group(): chosen = jnp.take(omega_blocks, col_group, axis=0)  39.2 us
    another operation x6, other arithmetic, shards(): lower = jnp.linalg.cholesky(gram)  34 us
    dot_general x14, matrix products, add_group(): jnp.einsum('nij,njk->nik', block_group, chosen, preferred_element_type=jn...  21.7 us
    another operation x2, other arithmetic, shards(): solved = jax.scipy.linalg.solve_triangular(lower, sketch.T, lower=True)  19.7 us
  transfers between devices with their start and end apart: 3, of which 3 were waited for; matrix products, arithmetic and copies ran while one was open for 0% of the time, Pallas kernels for 0%

commit v1 on v0

v1 whole, which is shorter than its diff:
```python
import math

import jax
import jax.numpy as jnp
from jax import lax
from jax.experimental import pallas as pl
from jax.experimental.pallas import tpu as pltpu
from jax.sharding import Mesh
from jax.sharding import PartitionSpec as P

f32 = jnp.float32
HIGHEST = lax.Precision.HIGHEST
BS = 128
GROUP = 16
SIZES = {"z": 8, "y": 4, "x": 4, "core": 2}


def shift(value, axis, step):
    size = SIZES[axis]
    return lax.ppermute(value, axis, [(i, (i + step) % size) for i in range(size)])


def spmm_kernel(rows_ref, cols_ref, count_ref, omega_ref, blocks_ref, out_ref, acc_ref):
    step = pl.program_id(0)
    spare = acc_ref.shape[0] - BS

    @pl.when(step == 0)
    def _():
        acc_ref[...] = jnp.zeros_like(acc_ref)

    @pl.when(step * GROUP < count_ref[0])
    def _():
        for index in range(GROUP):
            slot = step * GROUP + index
            row = jnp.where(slot < count_ref[0], rows_ref[slot] * BS, spare)
            row = pl.multiple_of(row, BS)
            col = pl.multiple_of(cols_ref[slot] * BS, BS)
            product = jnp.dot(
                blocks_ref[index], omega_ref[pl.ds(col, BS), :], preferred_element_type=f32
            )
            acc_ref[pl.ds(row, BS), :] += product

    @pl.when(step == pl.num_programs(0) - 1)
    def _():
        out_ref[...] = acc_ref[pl.ds(0, spare), :]


def spmm(rows, cols, count, omega, blocks, row_blocks):
    slots = blocks.shape[0]
    width = omega.shape[1]
    total = row_blocks * BS

    def group_of(step, rows_ref, cols_ref, count_ref):
        return (jnp.minimum(step, (count_ref[0] - 1) // GROUP), 0, 0)

    return pl.pallas_call(
        spmm_kernel,
        grid_spec=pltpu.PrefetchScalarGridSpec(
            num_scalar_prefetch=3,
            grid=(slots // GROUP,),
            in_specs=[
                pl.BlockSpec(omega.shape, lambda *_: (0, 0)),
                pl.BlockSpec((GROUP, BS, BS), group_of),
            ],
            out_specs=pl.BlockSpec((total, width), lambda *_: (0, 0)),
            scratch_shapes=[pltpu.VMEM((total + BS, width), f32)],
        ),
        out_shape=jax.ShapeDtypeStruct((total, width), f32),
        compiler_params=pltpu.CompilerParams(
            dimension_semantics=("arbitrary",), vmem_limit_bytes=40 * 1024 * 1024
        ),
        name="spmm",
    )(rows, cols, count, omega, blocks)


def dot(a, b, contract):
    return lax.dot_general(
        a, b, ((contract[:1], contract[1:]), ((), ())),
        precision=HIGHEST, preferred_element_type=f32,
    )


def eliminate(sym):
    size = sym.shape[0]
    tiles = size // 8
    lane = lax.broadcasted_iota(jnp.int32, (8, size), 1)
    sub = lax.broadcasted_iota(jnp.int32, (8, size), 0)
    upper = [sym[8 * t:8 * t + 8, :] for t in range(tiles)]
    inverse = [(lane == sub + 8 * t).astype(f32) for t in range(tiles)]
    for k in range(size):
        t, j = divmod(k, 8)
        pivot = 1.0 / upper[t][j:j + 1, k:k + 1]
        row = jnp.broadcast_to(upper[t][j:j + 1, :] * pivot, (8, size))
        row_inverse = jnp.broadcast_to(inverse[t][j:j + 1, :] * pivot, (8, size))
        for i in range(t, tiles):
            if i == t and j == 7:
                continue
            column = jnp.broadcast_to(upper[i][:, k:k + 1], (8, size))
            if i == t:
                column = jnp.where(sub > j, column, 0.0)
            upper[i] = upper[i] - column * row
            inverse[i] = inverse[i] - column * row_inverse
    for t in range(tiles):
        diagonal = jnp.sum(jnp.where(lane == sub + 8 * t, upper[t], 0.0), axis=1, keepdims=True)
        scale = 1.0 / jnp.sqrt(diagonal)
        upper[t] = jnp.where(lane >= sub + 8 * t, upper[t] * scale, 0.0)
        inverse[t] = inverse[t] * scale
    return jnp.concatenate(upper, 0), jnp.concatenate(inverse, 0)


def factor_kernel(gram_ref, sketch_ref, factor_ref, basis_ref, *, scale):
    half = gram_ref.shape[0] // 2
    top, bottom = pl.ds(0, half), pl.ds(half, half)
    upper1, inverse1 = eliminate(gram_ref[top, top])
    cross = dot(inverse1, gram_ref[top, bottom], (1, 0))
    upper2, inverse2 = eliminate(gram_ref[bottom, bottom] - dot(cross, cross, (0, 0)))
    factor_ref[top, top] = upper1 * (1.0 / scale)
    factor_ref[top, bottom] = cross * (1.0 / scale)
    factor_ref[bottom, top] = jnp.zeros((half, half), f32)
    factor_ref[bottom, bottom] = upper2 * (1.0 / scale)
    first = dot(sketch_ref[:, top], inverse1, (1, 1))
    rest = sketch_ref[:, bottom] - dot(first, cross, (1, 0))
    basis_ref[:, top] = first * scale
    basis_ref[:, bottom] = dot(rest, inverse2, (1, 1)) * scale


def orthonormalize(gram, sketch, vertex_total):
    return pl.pallas_call(
        lambda *refs: factor_kernel(*refs, scale=math.sqrt(vertex_total)),
        out_shape=(
            jax.ShapeDtypeStruct(gram.shape, f32),
            jax.ShapeDtypeStruct(sketch.shape, f32),
        ),
        compiler_params=pltpu.CompilerParams(vmem_limit_bytes=32 * 1024 * 1024),
        name="orthonormalize",
    )(gram, sketch)


def spread(value, axes, count):
    copies = jnp.broadcast_to(value[None], (count,) + value.shape)
    return lax.all_to_all(copies, axes, 0, 0, tiled=True)


def sum_over_all(gram):
    rows, width = gram.shape
    pieces = gram.reshape(16, rows // 16, width)
    part = lax.all_to_all(pieces, ("y", "x"), 0, 0, tiled=True).sum(0)
    part = spread(part, ("z", "core"), 16).sum(0)
    return spread(part, ("y", "x"), 16).reshape(rows, width)


def shards(blocks, block_rows, block_cols, live_counts, omega, row_scale):
    own_rows, width = omega.shape
    row_blocks = own_rows * 8 // BS
    per = own_rows // BS
    x_here, core_here = lax.axis_index("x"), lax.axis_index("core")
    rows = block_rows[0, 0]
    x_of, core_of, rest = rows // (2 * per), (rows // per) % 2, rows % per
    rows = (
        jnp.where(core_of == core_here, 4 * per, 0) + ((x_of - x_here + 4) % 4) * per + rest
    )
    gathered = lax.all_gather(omega, ("z", "y"), axis=0, tiled=True)
    partial_sum = spmm(rows, block_cols[0, 0], live_counts[0], gathered, blocks[0, 0], row_blocks)
    theirs, ours = partial_sum[:4 * own_rows], partial_sum[4 * own_rows:]
    ours = ours + shift(theirs, "core", 1)
    pieces = ours.reshape(4, own_rows, width)
    arrived = [shift(pieces[k], "x", k) for k in (1, 3, 2)]
    sketch = pieces[0] + arrived[0] + arrived[1] + arrived[2]
    sketch = sketch * row_scale[:, None]
    gram = sum_over_all(dot(sketch, sketch, (0, 0)))
    factor, basis = orthonormalize(gram, sketch, own_rows * 256)
    return (basis, factor)


def solution(mesh):
    fine = Mesh(mesh.devices.reshape(8, 4, 4, 2), ("z", "y", "x", "core"))
    row, col = ("z", "y"), ("x", "core")
    placed = (
        P(row, col, None, None, None),
        P(row, col, None),
        P(row, col, None),
        P(row, col),
        P(col + row, None),
        P(row + col),
    )
    return jax.shard_map(
        shards,
        mesh=fine,
        in_specs=placed,
        out_specs=(P(row + col, None), P()),
        check_vma=False,
    )
```

time: 652 us -> 201 us (0.31)
  waiting for transfers between devices: 408 us -> 101 us
  matrix products: 98.2 us -> 0.59 us
  other arithmetic: 75.5 us -> 0.98 us
  local copies, waits for them, and re-layouts: 51.3 us -> 6.12 us
  blocking collectives: 0 us -> 41.8 us
  Pallas kernels: 0 us -> 28.9 us
    psum x2 -> x0, waiting for transfers between devices: 320 us -> none  [the longest x1 255 us: shards(): gram = lax.psum(local_gram, ('row', 'col'))]
    dot_general x29 -> x1, matrix products: 96.7 us -> 0.59 us  [dot(): lax.dot_general(a, b, ((contract[:1], contract[1:]), ((), ())), precision...]
    another operation x8 -> x0, other arithmetic: 53.7 us -> none  [the longest x6 34 us: shards(): lower = jnp.linalg.cholesky(gram)]
    all_to_all x0 -> x3, blocking collectives: none -> 41.8 us  [the longest x2 29.5 us: spread(): return lax.all_to_all(copies, axes, 0, 0, tiled=True)]
    gather x14 -> x0, local copies, waits for them, and re-layouts: 39.2 us -> none  [add_group(): chosen = jnp.take(omega_blocks, col_group, axis=0)]
    pallas_call x0 -> x2, Pallas kernels: none -> 28.9 us  [the longest x1 23 us: orthonormalize(): pl.pallas_call(lambda *refs: factor_kernel(*refs, scale=math.sqrt(vertex_...]
    and x14 -> x0, other arithmetic: 19.7 us -> none  [add_group(): chosen = jnp.take(omega_blocks, col_group, axis=0)]
    ppermute x0 -> x4, waiting for transfers between devices: none -> 14 us  [shift(): lax.ppermute(value, axis, [(i, (i + step) % size) for i in range(size)])]
  transfers between devices with their start and end apart: 3 -> 5, of which waited for: 3 -> 4; matrix products, arithmetic and copies ran while one was open for 0% -> 0% of each run, Pallas kernels for 0% -> 0%
where the time goes in v1:
time: 201 us; the launch traced here: 199 us
  waiting for transfers between devices  101 us (50%)
  blocking collectives  41.8 us (21%)
  Pallas kernels  28.9 us (14%)
  between operations  14.8 us (7%)
  local copies, waits for them, and re-layouts  6.12 us (3%)
  starting transfers between devices  5.36 us (3%)
    all_gather x1, waiting for transfers between devices, shards(): gathered = lax.all_gather(omega, ('z', 'y'), axis=0, tiled=True)  86.2 us
    all_to_all x2, blocking collectives, spread(): return lax.all_to_all(copies, axes, 0, 0, tiled=True)  29.5 us
    pallas_call x1, Pallas kernels, orthonormalize(): pl.pallas_call(lambda *refs: factor_kernel(*refs, scale=math.sqrt(vertex_...  23 us
    ppermute x4, waiting for transfers between devices, shift(): lax.ppermute(value, axis, [(i, (i + step) % size) for i in range(size)])  14 us
    all_to_all x1, blocking collectives, sum_over_all(): part = lax.all_to_all(pieces, ('y', 'x'), 0, 0, tiled=True).sum(0)  12.2 us
    unnamed x8, local copies, waits for them, and re-layouts  5.95 us
    pallas_call x1, Pallas kernels, spmm(): pl.pallas_call(spmm_kernel, grid_spec=pltpu.PrefetchScalarGridSpec(num_sc...  5.91 us
    ppermute x4, starting transfers between devices, shift(): lax.ppermute(value, axis, [(i, (i + step) % size) for i in range(size)])  5.32 us
  transfers between devices with their start and end apart: 5, of which 4 were waited for; matrix products, arithmetic and copies ran while one was open for 0% of the time, Pallas kernels for 0%

profile of v1, /device:TPU:2, one launch (start us, length us, event | category | flops | bytes accessed | tf_op | source)
XLA Modules:
  0.0 199.3 jit_solution(6316171237208206633)
XLA Ops:
  7.2 0.0 all-gather.2.cloned.1.call-start
  7.2 0.7 all-gather.2.cloned.1.call-update
  8.5 0.7 fusion.4.rows_ref
  9.3 86.2 %all-gather.2.cloned.1.call-done.omega_ref = bf16[8192,256]{1,0:T(8,128)(2,1)} async-done(((bf16[256,256]{1,0:T(8,128)(2,1)}), bf16[8192,256]{1,0:T(8,128)(2,1)}) %all-gather.2.cloned.1.call-update) | async-done | bytes 4194320 | tf_op jit(solution)/shard_map/all_gather | solution.py:162
  95.4 0.0 copy-start
  95.4 3.1 %copy-done = bf16[1,1,224,128,128]{4,3,2,1,0:T(8,128)(2,1)S(1)} copy-done((bf16[1,1,224,128,128]{4,3,2,1,0:T(8,128)(2,1)S(1)}, bf16[1,1,224,128,128]{4,3,2,1,0:T(8,128)(2,1)}, u32[]{:S(2)}) %copy-start) | copy-done | bytes 7340056
  98.5 0.0 copy-start.1
  98.5 2.2 %copy-done.1 = bf16[8192,256]{1,0:T(8,128)(2,1)S(1)} copy-done((bf16[8192,256]{1,0:T(8,128)(2,1)S(1)}, bf16[8192,256]{1,0:T(8,128)(2,1)}, u32[]{:S(2)}) %copy-start.1) | copy-done | bytes 4194328
  100.7 0.0 copy-start.2
  100.7 0.7 copy-done.2
  101.4 5.9 %spmm.1 = f32[2048,256]{1,0:T(8,128)S(1)} custom-call(s32[224]{0:T(256)S(1)} %fusion.4.rows_ref, s32[224]{0:T(256)S(1)} %bitcast.11, s32[1]{0:T(128)} %bitcast.8.count_ref, bf16[8192,256]{1,0:T(8,128)(2,1)S(1)} %copy-done.1, bf16[224,128,128]{2,1,0:T(8,128)(2,1)S(1)} %bitcast.9), custom_call_target="tpu_custom_call" | custom-call | tf_op jit(solution)/shard_map/spmm/pallas_call | solution.py:56
  107.3 0.0 copy-start.3
  107.3 0.1 slice.29
  107.4 0.1 collective-permute-start
  107.5 2.6 %collective-permute-done = f32[1024,256]{1,0:T(8,128)S(1)} collective-permute-done((f32[1024,256]{1,0:T(8,128)S(1)}, f32[1024,256]{1,0:T(8,128)S(1)}, u32[]{:S(2)}, u32[]{:S(2)}) %collective-permute-start) | collective-permute-done | bytes 1048608 | tf_op jit(solution)/shard_map/ppermute | solution.py:20
  110.1 0.1 slice_add_fusion
  110.3 0.1 fusion.8
  110.3 2.4 %collective-permute-start.1 = (f32[256,256]{1,0:T(8,128)S(1)}, f32[256,256]{1,0:T(8,128)S(1)}, u32[]{:S(2)}, u32[]{:S(2)}) collective-permute-start(f32[256,256]{1,0:T(8,128)S(1)} %get-tuple-element.6), channel_id=1, source_target_pairs={{0,2},{2,4},{4,6},{6,0},{1,3},{3,5},{5,7},{7,1},{8,10},{10,12},{12... | collective-permute-start | bytes 786440 | tf_op jit(solution)/shard_map/ppermute | solution.py:20
  112.7 0.7 collective-permute-start.3
  113.5 2.1 %collective-permute-start.2 = (f32[256,256]{1,0:T(8,128)S(1)}, f32[256,256]{1,0:T(8,128)S(1)}, u32[]{:S(2)}, u32[]{:S(2)}) collective-permute-start(f32[256,256]{1,0:T(8,128)S(1)} %get-tuple-element.8), channel_id=1, source_target_pairs={{0,6},{2,0},{4,2},{6,4},{1,7},{3,1},{5,3},{7,5},{8,14},{10,8},{12,... | collective-permute-start | bytes 786440 | tf_op jit(solution)/shard_map/ppermute | solution.py:20
  115.5 8.7 %collective-permute-done.1 = f32[256,256]{1,0:T(8,128)S(1)} collective-permute-done((f32[256,256]{1,0:T(8,128)S(1)}, f32[256,256]{1,0:T(8,128)S(1)}, u32[]{:S(2)}, u32[]{:S(2)}) %collective-permute-start.1) | collective-permute-done | bytes 262176 | tf_op jit(solution)/shard_map/ppermute | solution.py:20
  124.2 0.0 collective-permute-done.3
  124.2 2.6 %collective-permute-done.2 = f32[256,256]{1,0:T(8,128)S(1)} collective-permute-done((f32[256,256]{1,0:T(8,128)S(1)}, f32[256,256]{1,0:T(8,128)S(1)}, u32[]{:S(2)}, u32[]{:S(2)}) %collective-permute-start.2) | collective-permute-done | bytes 262176 | tf_op jit(solution)/shard_map/ppermute | solution.py:20
  126.9 0.0 copy-done.3
  126.9 0.1 fusion.2.refs_1_
  127.0 0.6 fusion.9
  127.6 12.2 %all_to_all.15 = f32[16,16,256]{2,1,0:T(8,128)S(1)} all-to-all(f32[16,16,256]{2,1,0:T(8,128)S(1)} %bitcast.12), channel_id=1, replica_groups=mesh['z'=8,'y'=4,'x'=4,'core'=2] {'y','x'}, dimensions={0} | all-to-all | bytes 524288 | tf_op jit(solution)/shard_map/all_to_all | solution.py:147
  139.9 16.9 %all_to_all.16 = f32[16,16,256]{2,1,0:T(8,128)S(1)} all-to-all(f32[16,16,256]{2,1,0:T(8,128)S(1)} %broadcast_in_dim.11), channel_id=1, replica_groups=mesh['z'=8,'y'=4,'x'=4,'core'=2] {'z','core'}, dimensions={0} | all-to-all | bytes 524288 | tf_op jit(solution)/shard_map/all_to_all | solution.py:141
  156.8 12.7 %all_to_all.17 = f32[16,16,256]{2,1,0:T(8,128)S(1)} all-to-all(f32[16,16,256]{2,1,0:T(8,128)S(1)} %broadcast_in_dim.12), channel_id=1, replica_groups=mesh['z'=8,'y'=4,'x'=4,'core'=2] {'y','x'}, dimensions={0} | all-to-all | bytes 524288 | tf_op jit(solution)/shard_map/all_to_all | solution.py:141
  169.5 23.0 %orthonormalize.1 = (f32[256,256]{1,0:T(8,128)}, f32[256,256]{1,0:T(8,128)}) custom-call(f32[256,256]{1,0:T(8,128)S(1)} %bitcast.10, f32[256,256]{1,0:T(8,128)S(1)} %fusion.2.refs_1_), custom_call_target="tpu_custom_call" | custom-call | tf_op jit(solution)/shard_map/orthonormalize/pallas_call | solution.py:128
  (4 shorter events, 0.1 us)
Async XLA Ops:
  7.2 88.2 %all-gather.2.cloned.1.call-start = ((), (), s32[]{:S(2)}) async-start(), calls=%async_computation.3 | async-start | bytes 4325376 | tf_op jit(solution)/shard_map/all_gather | solution.py:162
  95.4 3.1 %copy-start = (bf16[1,1,224,128,128]{4,3,2,1,0:T(8,128)(2,1)S(1)}, bf16[1,1,224,128,128]{4,3,2,1,0:T(8,128)(2,1)}, u32[]{:S(2)}) copy-start(bf16[1,1,224,128,128]{4,3,2,1,0:T(8,128)(2,1)} %param.6) | copy-start | bytes 22020100
  98.5 2.2 %copy-start.1 = (bf16[8192,256]{1,0:T(8,128)(2,1)S(1)}, bf16[8192,256]{1,0:T(8,128)(2,1)}, u32[]{:S(2)}) copy-start(bf16[8192,256]{1,0:T(8,128)(2,1)} %all-gather.2.cloned.1.call-done.omega_ref) | copy-start | bytes 12582916
  100.7 0.7 copy-start.2
  107.3 19.6 %copy-start.3 = (f32[256]{0:T(256)S(1)}, f32[256]{0:T(256)}, u32[]{:S(2)}) copy-start(f32[256]{0:T(256)} %param.11) | copy-start | bytes 3076
  107.4 2.7 %collective-permute-start = (f32[1024,256]{1,0:T(8,128)S(1)}, f32[1024,256]{1,0:T(8,128)S(1)}, u32[]{:S(2)}, u32[]{:S(2)}) collective-permute-start(f32[1024,256]{1,0:T(8,128)S(1)} %slice.29), channel_id=1, source_target_pairs={{0,1},{1,0},{2,3},{3,2},{4,5},{5,4},{6,7},{7,6},{8,9},{9,8},{10,11... | collective-permute-start | bytes 3145736 | tf_op jit(solution)/shard_map/ppermute | solution.py:20
  110.3 13.9 %collective-permute-start.1 = (f32[256,256]{1,0:T(8,128)S(1)}, f32[256,256]{1,0:T(8,128)S(1)}, u32[]{:S(2)}, u32[]{:S(2)}) collective-permute-start(f32[256,256]{1,0:T(8,128)S(1)} %get-tuple-element.6), channel_id=1, source_target_pairs={{0,2},{2,4},{4,6},{6,0},{1,3},{3,5},{5,7},{7,1},{8,10},{10,12},{12... | collective-permute-start | bytes 786440 | tf_op jit(solution)/shard_map/ppermute | solution.py:20
  112.7 11.5 %collective-permute-start.3 = (f32[256,256]{1,0:T(8,128)S(1)}, f32[256,256]{1,0:T(8,128)S(1)}, u32[]{:S(2)}, u32[]{:S(2)}) collective-permute-start(f32[256,256]{1,0:T(8,128)S(1)} %get-tuple-element.7), channel_id=1, source_target_pairs={{0,4},{2,6},{4,0},{6,2},{1,5},{3,7},{5,1},{7,3},{8,12},{10,14},{12... | collective-permute-start | bytes 786440 | tf_op jit(solution)/shard_map/ppermute | solution.py:20
  113.5 13.4 %collective-permute-start.2 = (f32[256,256]{1,0:T(8,128)S(1)}, f32[256,256]{1,0:T(8,128)S(1)}, u32[]{:S(2)}, u32[]{:S(2)}) collective-permute-start(f32[256,256]{1,0:T(8,128)S(1)} %get-tuple-element.8), channel_id=1, source_target_pairs={{0,6},{2,0},{4,2},{6,4},{1,7},{3,1},{5,3},{7,5},{8,14},{10,8},{12,... | collective-permute-start | bytes 786440 | tf_op jit(solution)/shard_map/ppermute | solution.py:20
Sparse Core Ops, SparseCore 0:
  10.6 84.7 all-gather.1

commit v2 on v1

v2 whole, which is shorter than its diff:
```python
import math

import jax
import jax.numpy as jnp
from jax import lax
from jax.experimental import pallas as pl
from jax.experimental.pallas import tpu as pltpu
from jax.sharding import Mesh
from jax.sharding import PartitionSpec as P

f32 = jnp.float32
HIGHEST = lax.Precision.HIGHEST
BS = 128
GROUP = 16
CHUNKS = 7
KIND = 1 << 20
FIRST_LIMIT = 48
SIZES = {"z": 8, "y": 4, "x": 4, "core": 2}


def shift(value, axis, step):
    size = SIZES[axis]
    return lax.ppermute(value, axis, [(i, (i + step) % size) for i in range(size)])


def add_groups(groups, end, list_ref, blocks_ref, omega_ref, out_ref):
    spare = (out_ref.shape[0] // BS - 1) * 256

    def group(step, carry):
        for index in range(GROUP):
            place = step * GROUP + index
            entry = jnp.where(place < end, list_ref[place], spare)
            row = pl.multiple_of((entry // 256) % 32 * BS, BS)
            out_ref[pl.ds(row, BS), :] += jnp.dot(
                blocks_ref[entry % 256], omega_ref[entry // 8192], preferred_element_type=f32
            )
        return carry

    lax.fori_loop(*groups, group, 0)


def copies_of(part_refs, places, omega_ref, sems):
    return [
        pltpu.make_async_copy(part_refs[index], omega_ref.at[pl.ds(*place)], sems.at[index])
        for index, place in enumerate(places)
    ]


def first_kernel(entries_ref, *refs, places):
    part_refs = refs[:len(places)]
    source_ref, out_ref, blocks_ref, late_ref, late_count_ref = refs[len(places):-4]
    early_ref, omega_ref, sems, block_sems = refs[-4:]
    slots = blocks_ref.shape[0]
    chunk = slots // CHUNKS
    loads = [
        pltpu.make_async_copy(
            source_ref.at[pl.ds(i * chunk, chunk)],
            blocks_ref.at[pl.ds(i * chunk, chunk)],
            block_sems.at[i],
        )
        for i in range(CHUNKS)
    ]
    copies = copies_of(part_refs, places, omega_ref, sems)
    for copy in loads[:1] + copies + loads[1:]:
        copy.start()
    out_ref[...] = jnp.zeros_like(out_ref)

    def sort(slot, counts):
        early, late = counts
        entry = entries_ref[slot]
        kind = entry // KIND
        early_ref[early] = entry
        late_ref[late] = entry - KIND
        return early + (kind == 0).astype(jnp.int32), late + (kind == 1).astype(jnp.int32)

    counts, ends = (jnp.int32(0), jnp.int32(0)), []
    for i in range(CHUNKS):
        counts = lax.fori_loop(i * chunk, (i + 1) * chunk, sort, counts, unroll=8)
        ends.append(counts[0])
    late_count_ref[0] = counts[1]
    for copy in copies:
        copy.wait()
    done = 0
    for i, copy in enumerate(loads):
        copy.wait()
        full = ends[i] // GROUP if i < CHUNKS - 1 else (ends[i] + GROUP - 1) // GROUP
        add_groups((done, full), ends[i], early_ref, blocks_ref, omega_ref, out_ref)
        done = full


def rest_kernel(late_ref, late_count_ref, *refs, places):
    part_refs = refs[:len(places)]
    out_ref, blocks_ref, theirs_ref, ours_ref, omega_ref, sems = refs[len(places):]
    copies = copies_of(part_refs, places, omega_ref, sems)
    for copy in copies:
        copy.start()
    for copy in copies:
        copy.wait()
    count = late_count_ref[0]
    groups = 0, (count + GROUP - 1) // GROUP
    add_groups(groups, count, late_ref, blocks_ref, omega_ref, out_ref)
    half = theirs_ref.shape[0]
    theirs_ref[...] = out_ref[pl.ds(0, half), :]
    ours_ref[...] = out_ref[pl.ds(half, half), :]


def block_products(entries, early, late, blocks, total):
    slots, width = blocks.shape[0], early[0][0].shape[-1]
    smem, vmem = (pl.BlockSpec(memory_space=space) for space in (pltpu.SMEM, pltpu.VMEM))
    anywhere = pl.BlockSpec(memory_space=pl.ANY)

    def places_of(parts):
        return [place for _, place in parts]

    def omega_scratch(parts):
        held = max(sum(place) for place in places_of(parts))
        return pltpu.VMEM((held, BS, width), jnp.bfloat16)

    def params(mebibytes):
        return pltpu.CompilerParams(vmem_limit_bytes=mebibytes * 1024 * 1024)

    def cost(flops):
        return pl.CostEstimate(flops=flops, bytes_accessed=0, transcendentals=0)

    before, held, late_list, late_count = pl.pallas_call(
        lambda *refs: first_kernel(*refs, places=places_of(early)),
        in_specs=[smem] + [anywhere] * (len(early) + 1),
        out_specs=(vmem, vmem, smem, smem),
        out_shape=(
            pltpu.VMEM((total + BS, width), f32),
            pltpu.VMEM(blocks.shape, blocks.dtype),
            jax.ShapeDtypeStruct((slots + 2 * GROUP,), jnp.int32),
            jax.ShapeDtypeStruct((1,), jnp.int32),
        ),
        scratch_shapes=[
            pltpu.SMEM((slots + 2 * GROUP,), jnp.int32),
            omega_scratch(early),
            pltpu.SemaphoreType.DMA((len(early),)),
            pltpu.SemaphoreType.DMA((CHUNKS,)),
        ],
        compiler_params=params(FIRST_LIMIT),
        cost_estimate=cost(6 * 10**9),
        name="multiply_first",
    )(entries, *(part for part, _ in early), blocks)
    return pl.pallas_call(
        lambda *refs: rest_kernel(*refs, places=places_of(late)),
        in_specs=[smem] * 2 + [anywhere] * len(late) + [vmem] * 2,
        out_specs=(vmem, vmem),
        out_shape=(jax.ShapeDtypeStruct((total // 2, width), f32),) * 2,
        scratch_shapes=[omega_scratch(late), pltpu.SemaphoreType.DMA((len(late),))],
        compiler_params=params(24),
        cost_estimate=cost(10**9),
        name="multiply_rest",
    )(late_list, late_count, *(part for part, _ in late), before, held)


def dot(a, b, contract):
    return lax.dot_general(
        a, b, ((contract[:1], contract[1:]), ((), ())),
        precision=HIGHEST, preferred_element_type=f32,
    )


def eliminate(sym):
    size = sym.shape[0]
    tiles = size // 8
    full = (8, size)
    lane = lax.broadcasted_iota(jnp.int32, full, 1)
    sub = lax.broadcasted_iota(jnp.int32, full, 0)
    upper = [sym[8 * t:8 * t + 8, :] for t in range(tiles)]
    inverse = [(lane == sub + 8 * t).astype(f32) for t in range(tiles)]
    for t in range(tiles):
        k = 8 * t
        rows = [jnp.broadcast_to(upper[t][i:i + 1, :], full) for i in range(8)]
        inv_rows = [jnp.broadcast_to(inverse[t][i:i + 1, :], full) for i in range(8)]
        own = [jnp.broadcast_to(upper[t][:, k + i:k + i + 1], full) for i in range(8)]
        entry = {
            (a, b): jnp.broadcast_to(own[b][a:a + 1, :], full) for a in range(8) for b in range(a, 8)
        }
        columns = {
            i: [jnp.broadcast_to(upper[i][:, k + a:k + a + 1], full) for a in range(8)]
            for i in range(t + 1, tiles)
        }
        recip, ratio = [], {}
        for a in range(8):
            recip.append(1.0 / entry[a, a])
            for b in range(a + 1, 8):
                ratio[a, b] = entry[a, b] * recip[a]
            for b in range(a + 1, 8):
                for c in range(b, 8):
                    entry[b, c] = entry[b, c] - ratio[a, b] * entry[a, c]
                rows[b] = rows[b] - ratio[a, b] * rows[a]
                inv_rows[b] = inv_rows[b] - ratio[a, b] * inv_rows[a]
            if t + 1 < tiles:
                next_columns = columns[t + 1]
                part = next_columns[a] * recip[a]
                for b in range(a + 1, 8):
                    next_columns[b] = next_columns[b] - next_columns[a] * ratio[a, b]
                upper[t + 1] = upper[t + 1] - part * rows[a]
                inverse[t + 1] = inverse[t + 1] - part * inv_rows[a]
        if t + 2 < tiles:
            back = [rows[a] * recip[a] for a in range(8)]
            inv_back = [inv_rows[a] * recip[a] for a in range(8)]
            for a in range(6, -1, -1):
                for b in range(a + 1, 8):
                    back[a] = back[a] - ratio[a, b] * back[b]
                    inv_back[a] = inv_back[a] - ratio[a, b] * inv_back[b]
            for i in range(t + 2, tiles):
                for a in range(7, -1, -1):
                    upper[i] = upper[i] - columns[i][a] * back[a]
                    inverse[i] = inverse[i] - columns[i][a] * inv_back[a]
        pivot = entry[0, 0]
        for a in range(1, 8):
            upper[t] = jnp.where(sub == a, rows[a], upper[t])
            inverse[t] = jnp.where(sub == a, inv_rows[a], inverse[t])
            pivot = jnp.where(sub == a, entry[a, a], pivot)
        scale = 1.0 / jnp.sqrt(pivot)
        upper[t] = jnp.where(lane >= sub + k, upper[t] * scale, 0.0)
        inverse[t] = inverse[t] * scale
    return jnp.concatenate(upper, 0), jnp.concatenate(inverse, 0)


def factor_kernel(gram_ref, sketch_ref, factor_ref, basis_ref, *, scale):
    half = gram_ref.shape[1]
    top, bottom = pl.ds(0, half), pl.ds(half, half)
    upper1, inverse1 = eliminate(gram_ref[top, :])
    cross = dot(inverse1, gram_ref[bottom, :], (1, 0))
    upper2, inverse2 = eliminate(gram_ref[pl.ds(2 * half, half), :] - dot(cross, cross, (0, 0)))
    factor_ref[top, top] = upper1 * (1.0 / scale)
    factor_ref[top, bottom] = cross * (1.0 / scale)
    factor_ref[bottom, top] = jnp.zeros((half, half), f32)
    factor_ref[bottom, bottom] = upper2 * (1.0 / scale)
    first = dot(sketch_ref[:, top], inverse1, (1, 1))
    rest = sketch_ref[:, bottom] - dot(first, cross, (1, 0))
    basis_ref[:, top] = first * scale
    basis_ref[:, bottom] = dot(rest, inverse2, (1, 1)) * scale


def orthonormalize(gram, sketch, vertex_total):
    return pl.pallas_call(
        lambda *refs: factor_kernel(*refs, scale=math.sqrt(vertex_total)),
        out_shape=(
            jax.ShapeDtypeStruct((sketch.shape[1],) * 2, f32),
            jax.ShapeDtypeStruct(sketch.shape, f32),
        ),
        compiler_params=pltpu.CompilerParams(vmem_limit_bytes=32 * 1024 * 1024),
        name="orthonormalize",
    )(gram, sketch)


def spread(value, axes, count):
    copies = jnp.broadcast_to(value[None], (count,) + value.shape)
    return lax.all_to_all(copies, axes, 0, 0, tiled=True)


def sum_over_all(gram):
    half = gram.shape[0] // 2
    packed = jnp.concatenate([gram[:half, :half], gram[:half, half:], gram[half:, half:]], 0)
    pieces = packed.reshape(16, -1, half)
    part = lax.all_to_all(pieces, ("y", "x"), 0, 0, tiled=True).sum(0)
    part = part + shift(part, "core", 1)
    part = spread(part, ("z",), 8).sum(0)
    return spread(part, ("y", "x"), 16).reshape(packed.shape)


def gather(omega):
    half = omega.shape[0] // 2

    def ring(block, axis):
        size = SIZES[axis]
        forth, back, found = block, block, {0: block}
        for step in range(1, size // 2):
            forth, back = shift(forth, axis, 1), shift(back, axis, -1)
            found[size - step], found[step] = forth, back
        return found, forth, back

    def last(forth, back, axis, dim):
        cut = forth.shape[dim] // 2
        return (
            shift(lax.slice_in_dim(forth, 0, cut, axis=dim), axis, 1),
            shift(lax.slice_in_dim(back, cut, 2 * cut, axis=dim), axis, -1),
        )

    first, second = omega[None, :half], omega[None, half:]
    found1, forth1, back1 = ring(first, "y")
    found2, forth2, back2 = ring(second, "z")
    found1[2] = jnp.concatenate(last(forth1, back1, "y", 1), 1)
    found2[4] = jnp.concatenate(last(forth2, back2, "z", 1), 1)
    block1 = jnp.concatenate([found1[i] for i in range(4)], 0)
    block2 = jnp.concatenate([found2[i] for i in range(8)], 0)
    full1, forth1, back1 = ring(block1, "z")
    full2, forth2, back2 = ring(block2, "y")
    end1, end2 = last(forth1, back1, "z", 0), last(forth2, back2, "y", 0)
    early = [(full1[dz], (4 * dz, 4)) for dz in (0, 7, 1, 6, 2, 5, 3)]
    early += [(full2[dy], (32 + 8 * dy, 8)) for dy in (0, 3, 1)]
    late = [(end1[0], (0, 2)), (end1[1], (2, 2)), (end2[0], (4, 4)), (end2[1], (8, 4))]
    return early, late


def shards(blocks, block_rows, block_cols, live_counts, omega, row_scale):
    own_rows, width = omega.shape
    row_blocks = own_rows * 8 // BS
    per = own_rows // BS
    x_here, core_here = lax.axis_index("x"), lax.axis_index("core")
    rows, cols, count = block_rows[0, 0], block_cols[0, 0], live_counts[0, 0]
    x_of, core_of, rest = rows // (2 * per), (rows // per) % 2, rows % per
    rows = (
        jnp.where(core_of == core_here, 4 * per, 0) + ((x_of - x_here + 4) % 4) * per + rest
    )
    z_here, y_here = lax.axis_index("z"), lax.axis_index("y")
    far_z, far_y = (cols // 8 - z_here + 8) % 8, (cols // 2 - y_here + 4) % 4
    is_second = cols % 2
    is_late = jnp.where(is_second == 1, far_y == 2, far_z == 4)
    cols = jnp.where(
        is_late,
        jnp.where(is_second == 1, 4 + far_z, far_y),
        jnp.where(is_second == 1, 32 + 8 * far_y + far_z, 4 * far_z + far_y),
    )
    slot = jnp.arange(rows.shape[0], dtype=jnp.int32)
    kind = jnp.where(slot < count, is_late.astype(jnp.int32), 2)
    entries = slot + 256 * rows + 8192 * cols + KIND * kind
    early, late = gather(omega)
    theirs, ours = block_products(entries, early, late, blocks[0, 0], row_blocks * BS)
    ours = ours + shift(theirs, "core", 1)
    pieces = ours.reshape(4, own_rows, width)
    arrived = [shift(pieces[k], "x", k) for k in (1, 3, 2)]
    sketch = pieces[0] + arrived[0] + arrived[1] + arrived[2]
    sketch = sketch * row_scale[:, None]
    gram = sum_over_all(dot(sketch, sketch, (0, 0)))
    factor, basis = orthonormalize(gram, sketch, own_rows * 256)
    return (basis, factor)


def solution(mesh):
    fine = Mesh(mesh.devices.reshape(8, 4, 4, 2), ("z", "y", "x", "core"))
    row, col = ("z", "y"), ("x", "core")
    placed = (
        P(row, col, None, None, None),
        P(row, col, None),
        P(row, col, None),
        P(row, col),
        P(col + row, None),
        P(row + col),
    )
    return jax.shard_map(
        shards,
        mesh=fine,
        in_specs=placed,
        out_specs=(P(row + col, None), P()),
        check_vma=False,
    )
```

time: 201 us -> 142 us (0.71)
  waiting for transfers between devices: 101 us -> 31.7 us
  starting transfers between devices: 5.36 us -> 44.5 us
  between operations: 14.8 us -> 1.71 us
  blocking collectives: 41.8 us -> 35.4 us
  Pallas kernels: 28.9 us -> 23.4 us
  local copies, waits for them, and re-layouts: 6.12 us -> 2.58 us
    all_gather x1 -> x0, waiting for transfers between devices: 86.2 us -> none  [shards(): gathered = lax.all_gather(omega, ('z', 'y'), axis=0, tiled=True)]
    ppermute x4 -> x29, starting transfers between devices: 5.32 us -> 44.5 us  [shift(): lax.ppermute(value, axis, [(i, (i + step) % size) for i in range(size)])]
    ppermute x4 -> x29, waiting for transfers between devices: 14 us -> 31.7 us  [shift(): lax.ppermute(value, axis, [(i, (i + step) % size) for i in range(size)])]
    pallas_call x1, Pallas kernels: 23 us -> 11 us  [orthonormalize(): pl.pallas_call(lambda *refs: factor_kernel(*refs, scale=math.sqrt(vertex_...]
    pallas_call x1 -> x2, Pallas kernels: 5.91 us -> 12.5 us  [the longest x1 9.35 us: block_products(): pl.pallas_call(lambda *refs: first_kernel(*refs, places=places_of(early))...]
    all_to_all x2, blocking collectives: 29.5 us -> 23.6 us  [spread(): return lax.all_to_all(copies, axes, 0, 0, tiled=True)]
    unnamed x8 -> x30, local copies, waits for them, and re-layouts: 5.95 us -> 1.52 us
  transfers between devices with their start and end apart: 5 -> 29, of which waited for: 4 -> 8; matrix products, arithmetic and copies ran while one was open for 0% -> 2% of each run, Pallas kernels for 0% -> 7%
where the time goes in v2:
time: 142 us; the launch traced here: 141 us
  starting transfers between devices  44.5 us (31%)
  blocking collectives  35.4 us (25%)
  waiting for transfers between devices  31.7 us (22%)
  Pallas kernels  23.4 us (16%)
  local copies, waits for them, and re-layouts  2.58 us (2%)
  between operations  1.71 us (1%)
  other arithmetic  1.58 us (1%)
    ppermute x29, starting transfers between devices, shift(): lax.ppermute(value, axis, [(i, (i + step) % size) for i in range(size)])  44.5 us
    ppermute x29, waiting for transfers between devices, shift(): lax.ppermute(value, axis, [(i, (i + step) % size) for i in range(size)])  31.7 us
    all_to_all x2, blocking collectives, spread(): return lax.all_to_all(copies, axes, 0, 0, tiled=True)  23.6 us
    all_to_all x1, blocking collectives, sum_over_all(): part = lax.all_to_all(pieces, ('y', 'x'), 0, 0, tiled=True).sum(0)  11.7 us
    pallas_call x1, Pallas kernels, orthonormalize(): pl.pallas_call(lambda *refs: factor_kernel(*refs, scale=math.sqrt(vertex_...  11 us
    pallas_call x1, Pallas kernels, block_products(): pl.pallas_call(lambda *refs: first_kernel(*refs, places=places_of(early))...  9.35 us
    pallas_call x1, Pallas kernels, block_products(): pl.pallas_call(lambda *refs: rest_kernel(*refs, places=places_of(late)),...  3.1 us
  transfers between devices with their start and end apart: 29, of which 8 were waited for; matrix products, arithmetic and copies ran while one was open for 2% of the time, Pallas kernels for 7%

profile of v2, /device:TPU:2, one launch (start us, length us, event | category | flops | bytes accessed | tf_op | source)
XLA Modules:
  0.0 141.4 jit_solution(11722357159409053209)
XLA Ops:
  0.6 0.9 slice_bitcast_fusion
  1.5 5.9 %collective-permute-start.10 = (bf16[1,128,256]{2,1,0:T(8,128)(2,1)S(1)}, bf16[1,128,256]{2,1,0:T(8,128)(2,1)S(1)}, u32[]{:S(2)}, u32[]{:S(2)}) collective-permute-start(bf16[1,128,256]{2,1,0:T(8,128)(2,1)S(1)} %get-tuple-element.21), channel_id=1, source_target_pairs={{0,224},{32,0},{64,32},{96,64},{128,96},{160,128},{192,160},{224,1... | collective-permute-start | bytes 196616 | tf_op jit(solution)/shard_map/ppermute | solution.py:23
  7.5 1.6 %collective-permute-start.1 = (bf16[1,128,256]{2,1,0:T(8,128)(2,1)S(1)}, bf16[1,128,256]{2,1,0:T(8,128)(2,1)S(1)}, u32[]{:S(2)}, u32[]{:S(2)}) collective-permute-start(bf16[1,128,256]{2,1,0:T(8,128)(2,1)S(1)} %get-tuple-element.22), channel_id=1, source_target_pairs={{0,8},{8,16},{16,24},{24,0},{1,9},{9,17},{17,25},{25,1},{2,10},{10... | collective-permute-start | bytes 196616 | tf_op jit(solution)/shard_map/ppermute | solution.py:23
  9.0 1.7 %collective-permute-start = (bf16[1,128,256]{2,1,0:T(8,128)(2,1)S(1)}, bf16[1,128,256]{2,1,0:T(8,128)(2,1)S(1)}, u32[]{:S(2)}, u32[]{:S(2)}) collective-permute-start(bf16[1,128,256]{2,1,0:T(8,128)(2,1)S(1)} %get-tuple-element.22), channel_id=1, source_target_pairs={{0,24},{8,0},{16,8},{24,16},{1,25},{9,1},{17,9},{25,17},{2,26},{10... | collective-permute-start | bytes 196616 | tf_op jit(solution)/shard_map/ppermute | solution.py:23
  10.7 0.8 constant_dynamic-update-slice_fusion.6
  11.5 1.4 collective-permute-done.1
  12.9 0.4 collective-permute-start.2
  13.3 2.9 %collective-permute-start.3 = (bf16[1,64,256]{2,1,0:T(8,128)(2,1)S(1)}, bf16[1,64,256]{2,1,0:T(8,128)(2,1)S(1)}, u32[]{:S(2)}, u32[]{:S(2)}) collective-permute-start(bf16[1,64,256]{2,1,0:T(8,128)(2,1)S(1)} %slice.71), channel_id=1, source_target_pairs={{0,24},{8,0},{16,8},{24,16},{1,25},{9,1},{17,9},{25,17},{2,26},{10... | collective-permute-start | bytes 98312 | tf_op jit(solution)/shard_map/ppermute | solution.py:23
  16.2 3.2 %collective-permute-start.11 = (bf16[1,128,256]{2,1,0:T(8,128)(2,1)S(1)}, bf16[1,128,256]{2,1,0:T(8,128)(2,1)S(1)}, u32[]{:S(2)}, u32[]{:S(2)}) collective-permute-start(bf16[1,128,256]{2,1,0:T(8,128)(2,1)S(1)} %collective-permute-done.10), channel_id=1, source_target_pairs={{0,224},{32,0},{64,32},{96,64},{128,96},{160,128},{192,160},{224,1... | collective-permute-start | bytes 196616 | tf_op jit(solution)/shard_map/ppermute | solution.py:23
  19.4 0.1 collective-permute-start.14
  19.5 0.0 collective-permute-done.2
  19.6 0.0 copy-start.1
  19.6 0.1 collective-permute-start.4
  19.7 3.3 %collective-permute-start.5 = (bf16[4,128,256]{2,1,0:T(8,128)(2,1)S(1)}, bf16[4,128,256]{2,1,0:T(8,128)(2,1)S(1)}, u32[]{:S(2)}, u32[]{:S(2)}) collective-permute-start(bf16[4,128,256]{2,1,0:T(8,128)(2,1)S(1)} %pad_maximum_fusion.refs_1_), channel_id=1, source_target_pairs={{0,224},{32,0},{64,32},{96,64},{128,96},{160,128},{192,160},{224,1... | collective-permute-start | bytes 786440 | tf_op jit(solution)/shard_map/ppermute | solution.py:23
  23.0 2.5 %collective-permute-start.12 = (bf16[1,128,256]{2,1,0:T(8,128)(2,1)S(1)}, bf16[1,128,256]{2,1,0:T(8,128)(2,1)S(1)}, u32[]{:S(2)}, u32[]{:S(2)}) collective-permute-start(bf16[1,128,256]{2,1,0:T(8,128)(2,1)S(1)} %collective-permute-done.11), channel_id=1, source_target_pairs={{0,224},{32,0},{64,32},{96,64},{128,96},{160,128},{192,160},{224,1... | collective-permute-start | bytes 196616 | tf_op jit(solution)/shard_map/ppermute | solution.py:23
  25.5 5.8 %collective-permute-done.15 = bf16[1,128,256]{2,1,0:T(8,128)(2,1)S(1)} collective-permute-done((bf16[1,128,256]{2,1,0:T(8,128)(2,1)S(1)}, bf16[1,128,256]{2,1,0:T(8,128)(2,1)S(1)}, u32[]{:S(2)}, u32[]{:S(2)}) %collective-permute-start.15) | collective-permute-done | bytes 65568 | tf_op jit(solution)/shard_map/ppermute | solution.py:23
  31.3 3.2 %collective-permute-start.17 = (bf16[1,64,256]{2,1,0:T(8,128)(2,1)S(1)}, bf16[1,64,256]{2,1,0:T(8,128)(2,1)S(1)}, u32[]{:S(2)}, u32[]{:S(2)}) collective-permute-start(bf16[1,64,256]{2,1,0:T(8,128)(2,1)S(1)} %slice.73), channel_id=1, source_target_pairs={{0,224},{32,0},{64,32},{96,64},{128,96},{160,128},{192,160},{224,1... | collective-permute-start | bytes 98312 | tf_op jit(solution)/shard_map/ppermute | solution.py:23
  34.6 1.9 %collective-permute-done.16 = bf16[1,64,256]{2,1,0:T(8,128)(2,1)S(1)} collective-permute-done((bf16[1,64,256]{2,1,0:T(8,128)(2,1)S(1)}, bf16[1,64,256]{2,1,0:T(8,128)(2,1)S(1)}, u32[]{:S(2)}, u32[]{:S(2)}) %collective-permute-start.16) | collective-permute-done | bytes 32800 | tf_op jit(solution)/shard_map/ppermute | solution.py:23
  36.5 0.1 collective-permute-start.18
  36.6 3.2 %collective-permute-start.19 = (bf16[8,128,256]{2,1,0:T(8,128)(2,1)S(1)}, bf16[8,128,256]{2,1,0:T(8,128)(2,1)S(1)}, u32[]{:S(2)}, u32[]{:S(2)}) collective-permute-start(bf16[8,128,256]{2,1,0:T(8,128)(2,1)S(1)} %constant_dynamic-update-slice_fusion.refs_8_), channel_id=1, source_target_pairs={{0,24},{8,0},{16,8},{24,16},{1,25},{9,1},{17,9},{25,17},{2,26},{10... | collective-permute-start | bytes 1572872 | tf_op jit(solution)/shard_map/ppermute | solution.py:23
  39.9 3.3 %collective-permute-start.7 = (bf16[4,128,256]{2,1,0:T(8,128)(2,1)S(1)}, bf16[4,128,256]{2,1,0:T(8,128)(2,1)S(1)}, u32[]{:S(2)}, u32[]{:S(2)}) collective-permute-start(bf16[4,128,256]{2,1,0:T(8,128)(2,1)S(1)} %collective-permute-done.5.refs_3_), channel_id=1, source_target_pairs={{0,224},{32,0},{64,32},{96,64},{128,96},{160,128},{192,160},{224,1... | collective-permute-start | bytes 786440 | tf_op jit(solution)/shard_map/ppermute | solution.py:23
  43.2 6.6 %collective-permute-done.6.refs_4_ = bf16[4,128,256]{2,1,0:T(8,128)(2,1)S(1)} collective-permute-done((bf16[4,128,256]{2,1,0:T(8,128)(2,1)S(1)}, bf16[4,128,256]{2,1,0:T(8,128)(2,1)S(1)}, u32[]{:S(2)}, u32[]{:S(2)}) %collective-permute-start.6) | collective-permute-done | bytes 262176 | tf_op jit(solution)/shard_map/ppermute | solution.py:23
  49.8 3.2 %collective-permute-start.9 = (bf16[4,128,256]{2,1,0:T(8,128)(2,1)S(1)}, bf16[4,128,256]{2,1,0:T(8,128)(2,1)S(1)}, u32[]{:S(2)}, u32[]{:S(2)}) collective-permute-start(bf16[4,128,256]{2,1,0:T(8,128)(2,1)S(1)} %collective-permute-done.7.refs_5_), channel_id=1, source_target_pairs={{0,224},{32,0},{64,32},{96,64},{128,96},{160,128},{192,160},{224,1... | collective-permute-start | bytes 786440 | tf_op jit(solution)/shard_map/ppermute | solution.py:23
  53.6 1.2 fusion.7.refs_0_
  54.9 0.1 collective-permute-start.22
  55.1 3.3 %collective-permute-start.23 = (bf16[4,128,256]{2,1,0:T(8,128)(2,1)S(1)}, bf16[4,128,256]{2,1,0:T(8,128)(2,1)S(1)}, u32[]{:S(2)}, u32[]{:S(2)}) collective-permute-start(bf16[4,128,256]{2,1,0:T(8,128)(2,1)S(1)} %slice.77), channel_id=1, source_target_pairs={{0,24},{8,0},{16,8},{24,16},{1,25},{9,1},{17,9},{25,17},{2,26},{10... | collective-permute-start | bytes 786440 | tf_op jit(solution)/shard_map/ppermute | solution.py:23
  58.4 0.1 collective-permute-start.20
  58.5 3.3 %collective-permute-start.21 = (bf16[2,128,256]{2,1,0:T(8,128)(2,1)S(1)}, bf16[2,128,256]{2,1,0:T(8,128)(2,1)S(1)}, u32[]{:S(2)}, u32[]{:S(2)}) collective-permute-start(bf16[2,128,256]{2,1,0:T(8,128)(2,1)S(1)} %slice.75), channel_id=1, source_target_pairs={{0,224},{32,0},{64,32},{96,64},{128,96},{160,128},{192,160},{224,1... | collective-permute-start | bytes 393224 | tf_op jit(solution)/shard_map/ppermute | solution.py:23
  61.8 9.3 %multiply_first.1 = (f32[2176,256]{1,0:T(8,128)S(1)}, bf16[224,128,128]{2,1,0:T(8,128)(2,1)S(1)}, s32[256]{0:T(256)}, s32[1]{0:T(128)}) custom-call(s32[224]{0:T(256)} %fusion.7.refs_0_, bf16[4,128,256]{2,1,0:T(8,128)(2,1)} %copy-done.1, bf16[4,128,256]{2,1,0:T(8,128)(2,1)} %copy-done.8, bf16[4,128,256]{2,1,0:T(8,128)(2,1)} %copy-done.9, ...), custom_call_target="tpu_custom_call" | custom-call | flops 6000000000 | tf_op jit(solution)/shard_map/multiply_first/pallas_call | solution.py:125
  71.3 0.6 copy-done
  71.9 3.1 %multiply_rest.1 = (f32[1024,256]{1,0:T(8,128)S(1)}, f32[1024,256]{1,0:T(8,128)S(1)}) custom-call(s32[256]{0:T(256)S(1)} %copy-done, s32[1]{0:T(128)} %get-tuple-element.11.refs_1_, bf16[2,128,256]{2,1,0:T(8,128)(2,1)S(1)} %collective-permute-done.20.refs_2_, bf16[2,128,256]{2,1,0:T(8,128)(2,1)S(1)} %collective-permute-done.21.refs_3_, ...), custom_call_target="tpu_custom_call" | custom-call | flops 1000000000 | tf_op jit(solution)/shard_map/multiply_rest/pallas_call | solution.py:145
  75.0 0.1 collective-permute-start.24
  75.1 2.6 %collective-permute-done.24 = f32[1024,256]{1,0:T(8,128)S(1)} collective-permute-done((f32[1024,256]{1,0:T(8,128)S(1)}, f32[1024,256]{1,0:T(8,128)S(1)}, u32[]{:S(2)}, u32[]{:S(2)}) %collective-permute-start.24) | collective-permute-done | bytes 1048608 | tf_op jit(solution)/shard_map/ppermute | solution.py:23
  77.7 0.1 add.103
  77.9 0.1 fusion.12
  77.9 1.3 collective-permute-start.25
  79.2 1.0 collective-permute-start.26
  80.2 0.5 collective-permute-start.27
  80.8 6.6 %collective-permute-done.25 = f32[256,256]{1,0:T(8,128)S(1)} collective-permute-done((f32[256,256]{1,0:T(8,128)S(1)}, f32[256,256]{1,0:T(8,128)S(1)}, u32[]{:S(2)}, u32[]{:S(2)}) %collective-permute-start.25) | collective-permute-done | bytes 262176 | tf_op jit(solution)/shard_map/ppermute | solution.py:23
  87.4 5.5 %collective-permute-done.26 = f32[256,256]{1,0:T(8,128)S(1)} collective-permute-done((f32[256,256]{1,0:T(8,128)S(1)}, f32[256,256]{1,0:T(8,128)S(1)}, u32[]{:S(2)}, u32[]{:S(2)}) %collective-permute-start.26) | collective-permute-done | bytes 262176 | tf_op jit(solution)/shard_map/ppermute | solution.py:23
  92.9 0.1 fusion.2.refs_1_
  93.0 0.6 fusion.13
  93.7 11.7 %all_to_all.15 = f32[16,24,128]{2,1,0:T(8,128)S(1)} all-to-all(f32[16,24,128]{2,1,0:T(8,128)S(1)} %bitcast.16), channel_id=1, replica_groups=mesh['z'=8,'y'=4,'x'=4,'core'=2] {'y','x'}, dimensions={0} | all-to-all | bytes 393216 | tf_op jit(solution)/shard_map/all_to_all | solution.py:260
  105.5 0.1 collective-permute-start.28
  105.6 1.2 collective-permute-done.28
  106.7 12.3 %all_to_all.16 = f32[8,24,128]{2,1,0:T(8,128)S(1)} all-to-all(f32[8,24,128]{2,1,0:T(8,128)S(1)} %broadcast_in_dim.30), channel_id=1, replica_groups=mesh['z'=8,'y'=4,'x'=4,'core'=2] {'z'}, dimensions={0} | all-to-all | bytes 196608 | tf_op jit(solution)/shard_map/all_to_all | solution.py:253
  119.1 11.3 %all_to_all.17 = f32[16,24,128]{2,1,0:T(8,128)S(1)} all-to-all(f32[16,24,128]{2,1,0:T(8,128)S(1)} %broadcast_in_dim.31), channel_id=1, replica_groups=mesh['z'=8,'y'=4,'x'=4,'core'=2] {'y','x'}, dimensions={0} | all-to-all | bytes 393216 | tf_op jit(solution)/shard_map/all_to_all | solution.py:253
  130.4 11.0 %orthonormalize.1 = (f32[256,256]{1,0:T(8,128)}, f32[256,256]{1,0:T(8,128)}) custom-call(f32[384,128]{1,0:T(8,128)S(1)} %bitcast.15, f32[256,256]{1,0:T(8,128)S(1)} %fusion.2.refs_1_), custom_call_target="tpu_custom_call" | custom-call | tf_op jit(solution)/shard_map/orthonormalize/pallas_call | solution.py:240
  (71 shorter events, 0.3 us)
Async XLA Ops:
  1.5 14.7 %collective-permute-start.10 = (bf16[1,128,256]{2,1,0:T(8,128)(2,1)S(1)}, bf16[1,128,256]{2,1,0:T(8,128)(2,1)S(1)}, u32[]{:S(2)}, u32[]{:S(2)}) collective-permute-start(bf16[1,128,256]{2,1,0:T(8,128)(2,1)S(1)} %get-tuple-element.21), channel_id=1, source_target_pairs={{0,224},{32,0},{64,32},{96,64},{128,96},{160,128},{192,160},{224,1... | collective-permute-start | bytes 196616 | tf_op jit(solution)/shard_map/ppermute | solution.py:23
  7.4 12.0 %collective-permute-start.13 = (bf16[1,128,256]{2,1,0:T(8,128)(2,1)S(1)}, bf16[1,128,256]{2,1,0:T(8,128)(2,1)S(1)}, u32[]{:S(2)}, u32[]{:S(2)}) collective-permute-start(bf16[1,128,256]{2,1,0:T(8,128)(2,1)S(1)} %get-tuple-element.21), channel_id=1, source_target_pairs={{0,32},{32,64},{64,96},{96,128},{128,160},{160,192},{192,224},{224... | collective-permute-start | bytes 196616 | tf_op jit(solution)/shard_map/ppermute | solution.py:23
  7.5 5.5 %collective-permute-start.1 = (bf16[1,128,256]{2,1,0:T(8,128)(2,1)S(1)}, bf16[1,128,256]{2,1,0:T(8,128)(2,1)S(1)}, u32[]{:S(2)}, u32[]{:S(2)}) collective-permute-start(bf16[1,128,256]{2,1,0:T(8,128)(2,1)S(1)} %get-tuple-element.22), channel_id=1, source_target_pairs={{0,8},{8,16},{16,24},{24,0},{1,9},{9,17},{17,25},{25,1},{2,10},{10... | collective-permute-start | bytes 196616 | tf_op jit(solution)/shard_map/ppermute | solution.py:23
  9.0 4.3 %collective-permute-start = (bf16[1,128,256]{2,1,0:T(8,128)(2,1)S(1)}, bf16[1,128,256]{2,1,0:T(8,128)(2,1)S(1)}, u32[]{:S(2)}, u32[]{:S(2)}) collective-permute-start(bf16[1,128,256]{2,1,0:T(8,128)(2,1)S(1)} %get-tuple-element.22), channel_id=1, source_target_pairs={{0,24},{8,0},{16,8},{24,16},{1,25},{9,1},{17,9},{25,17},{2,26},{10... | collective-permute-start | bytes 196616 | tf_op jit(solution)/shard_map/ppermute | solution.py:23
  12.9 6.6 %collective-permute-start.2 = (bf16[1,64,256]{2,1,0:T(8,128)(2,1)S(1)}, bf16[1,64,256]{2,1,0:T(8,128)(2,1)S(1)}, u32[]{:S(2)}, u32[]{:S(2)}) collective-permute-start(bf16[1,64,256]{2,1,0:T(8,128)(2,1)S(1)} %slice.70), channel_id=1, source_target_pairs={{0,8},{8,16},{16,24},{24,0},{1,9},{9,17},{17,25},{25,1},{2,10},{10... | collective-permute-start | bytes 98312 | tf_op jit(solution)/shard_map/ppermute | solution.py:23
  13.3 6.2 %collective-permute-start.3 = (bf16[1,64,256]{2,1,0:T(8,128)(2,1)S(1)}, bf16[1,64,256]{2,1,0:T(8,128)(2,1)S(1)}, u32[]{:S(2)}, u32[]{:S(2)}) collective-permute-start(bf16[1,64,256]{2,1,0:T(8,128)(2,1)S(1)} %slice.71), channel_id=1, source_target_pairs={{0,24},{8,0},{16,8},{24,16},{1,25},{9,1},{17,9},{25,17},{2,26},{10... | collective-permute-start | bytes 98312 | tf_op jit(solution)/shard_map/ppermute | solution.py:23
  16.2 6.8 %collective-permute-start.11 = (bf16[1,128,256]{2,1,0:T(8,128)(2,1)S(1)}, bf16[1,128,256]{2,1,0:T(8,128)(2,1)S(1)}, u32[]{:S(2)}, u32[]{:S(2)}) collective-permute-start(bf16[1,128,256]{2,1,0:T(8,128)(2,1)S(1)} %collective-permute-done.10), channel_id=1, source_target_pairs={{0,224},{32,0},{64,32},{96,64},{128,96},{160,128},{192,160},{224,1... | collective-permute-start | bytes 196616 | tf_op jit(solution)/shard_map/ppermute | solution.py:23
  19.4 6.1 %collective-permute-start.14 = (bf16[1,128,256]{2,1,0:T(8,128)(2,1)S(1)}, bf16[1,128,256]{2,1,0:T(8,128)(2,1)S(1)}, u32[]{:S(2)}, u32[]{:S(2)}) collective-permute-start(bf16[1,128,256]{2,1,0:T(8,128)(2,1)S(1)} %collective-permute-done.13), channel_id=1, source_target_pairs={{0,32},{32,64},{64,96},{96,128},{128,160},{160,192},{192,224},{224... | collective-permute-start | bytes 196616 | tf_op jit(solution)/shard_map/ppermute | solution.py:23
  19.6 42.2 %copy-start.1 = (bf16[4,128,256]{2,1,0:T(8,128)(2,1)}, bf16[4,128,256]{2,1,0:T(8,128)(2,1)S(1)}, u32[]{:S(2)}) copy-start(bf16[4,128,256]{2,1,0:T(8,128)(2,1)S(1)} %pad_maximum_fusion.refs_1_) | copy-start | bytes 786436
  19.6 20.3 %collective-permute-start.4 = (bf16[4,128,256]{2,1,0:T(8,128)(2,1)S(1)}, bf16[4,128,256]{2,1,0:T(8,128)(2,1)S(1)}, u32[]{:S(2)}, u32[]{:S(2)}) collective-permute-start(bf16[4,128,256]{2,1,0:T(8,128)(2,1)S(1)} %pad_maximum_fusion.refs_1_), channel_id=1, source_target_pairs={{0,32},{32,64},{64,96},{96,128},{128,160},{160,192},{192,224},{224... | collective-permute-start | bytes 786440 | tf_op jit(solution)/shard_map/ppermute | solution.py:23
  19.7 20.2 %collective-permute-start.5 = (bf16[4,128,256]{2,1,0:T(8,128)(2,1)S(1)}, bf16[4,128,256]{2,1,0:T(8,128)(2,1)S(1)}, u32[]{:S(2)}, u32[]{:S(2)}) collective-permute-start(bf16[4,128,256]{2,1,0:T(8,128)(2,1)S(1)} %pad_maximum_fusion.refs_1_), channel_id=1, source_target_pairs={{0,224},{32,0},{64,32},{96,64},{128,96},{160,128},{192,160},{224,1... | collective-permute-start | bytes 786440 | tf_op jit(solution)/shard_map/ppermute | solution.py:23
  23.0 8.4 %collective-permute-start.12 = (bf16[1,128,256]{2,1,0:T(8,128)(2,1)S(1)}, bf16[1,128,256]{2,1,0:T(8,128)(2,1)S(1)}, u32[]{:S(2)}, u32[]{:S(2)}) collective-permute-start(bf16[1,128,256]{2,1,0:T(8,128)(2,1)S(1)} %collective-permute-done.11), channel_id=1, source_target_pairs={{0,224},{32,0},{64,32},{96,64},{128,96},{160,128},{192,160},{224,1... | collective-permute-start | bytes 196616 | tf_op jit(solution)/shard_map/ppermute | solution.py:23
  25.5 5.8 %collective-permute-start.15 = (bf16[1,128,256]{2,1,0:T(8,128)(2,1)S(1)}, bf16[1,128,256]{2,1,0:T(8,128)(2,1)S(1)}, u32[]{:S(2)}, u32[]{:S(2)}) collective-permute-start(bf16[1,128,256]{2,1,0:T(8,128)(2,1)S(1)} %collective-permute-done.14), channel_id=1, source_target_pairs={{0,32},{32,64},{64,96},{96,128},{128,160},{160,192},{192,224},{224... | collective-permute-start | bytes 196616 | tf_op jit(solution)/shard_map/ppermute | solution.py:23
  31.3 5.1 %collective-permute-start.16 = (bf16[1,64,256]{2,1,0:T(8,128)(2,1)S(1)}, bf16[1,64,256]{2,1,0:T(8,128)(2,1)S(1)}, u32[]{:S(2)}, u32[]{:S(2)}) collective-permute-start(bf16[1,64,256]{2,1,0:T(8,128)(2,1)S(1)} %slice.72), channel_id=1, source_target_pairs={{0,32},{32,64},{64,96},{96,128},{128,160},{160,192},{192,224},{224... | collective-permute-start | bytes 98312 | tf_op jit(solution)/shard_map/ppermute | solution.py:23
  31.3 5.1 %collective-permute-start.17 = (bf16[1,64,256]{2,1,0:T(8,128)(2,1)S(1)}, bf16[1,64,256]{2,1,0:T(8,128)(2,1)S(1)}, u32[]{:S(2)}, u32[]{:S(2)}) collective-permute-start(bf16[1,64,256]{2,1,0:T(8,128)(2,1)S(1)} %slice.73), channel_id=1, source_target_pairs={{0,224},{32,0},{64,32},{96,64},{128,96},{160,128},{192,160},{224,1... | collective-permute-start | bytes 98312 | tf_op jit(solution)/shard_map/ppermute | solution.py:23
  36.5 25.3 %copy-start.6 = (bf16[8,128,256]{2,1,0:T(8,128)(2,1)}, bf16[8,128,256]{2,1,0:T(8,128)(2,1)S(1)}, u32[]{:S(2)}) copy-start(bf16[8,128,256]{2,1,0:T(8,128)(2,1)S(1)} %constant_dynamic-update-slice_fusion.refs_8_) | copy-start | bytes 1572868
  36.5 18.4 %collective-permute-start.18 = (bf16[8,128,256]{2,1,0:T(8,128)(2,1)S(1)}, bf16[8,128,256]{2,1,0:T(8,128)(2,1)S(1)}, u32[]{:S(2)}, u32[]{:S(2)}) collective-permute-start(bf16[8,128,256]{2,1,0:T(8,128)(2,1)S(1)} %constant_dynamic-update-slice_fusion.refs_8_), channel_id=1, source_target_pairs={{0,8},{8,16},{16,24},{24,0},{1,9},{9,17},{17,25},{25,1},{2,10},{10... | collective-permute-start | bytes 1572872 | tf_op jit(solution)/shard_map/ppermute | solution.py:23
  36.6 18.4 %collective-permute-start.19 = (bf16[8,128,256]{2,1,0:T(8,128)(2,1)S(1)}, bf16[8,128,256]{2,1,0:T(8,128)(2,1)S(1)}, u32[]{:S(2)}, u32[]{:S(2)}) collective-permute-start(bf16[8,128,256]{2,1,0:T(8,128)(2,1)S(1)} %constant_dynamic-update-slice_fusion.refs_8_), channel_id=1, source_target_pairs={{0,24},{8,0},{16,8},{24,16},{1,25},{9,1},{17,9},{25,17},{2,26},{10... | collective-permute-start | bytes 1572872 | tf_op jit(solution)/shard_map/ppermute | solution.py:23
  39.8 21.9 %copy-start.8 = (bf16[4,128,256]{2,1,0:T(8,128)(2,1)}, bf16[4,128,256]{2,1,0:T(8,128)(2,1)S(1)}, u32[]{:S(2)}) copy-start(bf16[4,128,256]{2,1,0:T(8,128)(2,1)S(1)} %collective-permute-done.4.refs_2_) | copy-start | bytes 786436
  39.8 9.9 %collective-permute-start.6 = (bf16[4,128,256]{2,1,0:T(8,128)(2,1)S(1)}, bf16[4,128,256]{2,1,0:T(8,128)(2,1)S(1)}, u32[]{:S(2)}, u32[]{:S(2)}) collective-permute-start(bf16[4,128,256]{2,1,0:T(8,128)(2,1)S(1)} %collective-permute-done.4.refs_2_), channel_id=1, source_target_pairs={{0,32},{32,64},{64,96},{96,128},{128,160},{160,192},{192,224},{224... | collective-permute-start | bytes 786440 | tf_op jit(solution)/shard_map/ppermute | solution.py:23
  39.9 21.9 %copy-start.9 = (bf16[4,128,256]{2,1,0:T(8,128)(2,1)}, bf16[4,128,256]{2,1,0:T(8,128)(2,1)S(1)}, u32[]{:S(2)}) copy-start(bf16[4,128,256]{2,1,0:T(8,128)(2,1)S(1)} %collective-permute-done.5.refs_3_) | copy-start | bytes 786436
  39.9 9.9 %collective-permute-start.7 = (bf16[4,128,256]{2,1,0:T(8,128)(2,1)S(1)}, bf16[4,128,256]{2,1,0:T(8,128)(2,1)S(1)}, u32[]{:S(2)}, u32[]{:S(2)}) collective-permute-start(bf16[4,128,256]{2,1,0:T(8,128)(2,1)S(1)} %collective-permute-done.5.refs_3_), channel_id=1, source_target_pairs={{0,224},{32,0},{64,32},{96,64},{128,96},{160,128},{192,160},{224,1... | collective-permute-start | bytes 786440 | tf_op jit(solution)/shard_map/ppermute | solution.py:23
  49.8 12.0 %copy-start.10 = (bf16[4,128,256]{2,1,0:T(8,128)(2,1)}, bf16[4,128,256]{2,1,0:T(8,128)(2,1)S(1)}, u32[]{:S(2)}) copy-start(bf16[4,128,256]{2,1,0:T(8,128)(2,1)S(1)} %collective-permute-done.6.refs_4_) | copy-start | bytes 786436
  49.8 8.6 %collective-permute-start.8 = (bf16[4,128,256]{2,1,0:T(8,128)(2,1)S(1)}, bf16[4,128,256]{2,1,0:T(8,128)(2,1)S(1)}, u32[]{:S(2)}, u32[]{:S(2)}) collective-permute-start(bf16[4,128,256]{2,1,0:T(8,128)(2,1)S(1)} %collective-permute-done.6.refs_4_), channel_id=1, source_target_pairs={{0,32},{32,64},{64,96},{96,128},{128,160},{160,192},{192,224},{224... | collective-permute-start | bytes 786440 | tf_op jit(solution)/shard_map/ppermute | solution.py:23
  49.8 12.0 %copy-start.11 = (bf16[4,128,256]{2,1,0:T(8,128)(2,1)}, bf16[4,128,256]{2,1,0:T(8,128)(2,1)S(1)}, u32[]{:S(2)}) copy-start(bf16[4,128,256]{2,1,0:T(8,128)(2,1)S(1)} %collective-permute-done.7.refs_5_) | copy-start | bytes 786436
  49.8 8.7 %collective-permute-start.9 = (bf16[4,128,256]{2,1,0:T(8,128)(2,1)S(1)}, bf16[4,128,256]{2,1,0:T(8,128)(2,1)S(1)}, u32[]{:S(2)}, u32[]{:S(2)}) collective-permute-start(bf16[4,128,256]{2,1,0:T(8,128)(2,1)S(1)} %collective-permute-done.7.refs_5_), channel_id=1, source_target_pairs={{0,224},{32,0},{64,32},{96,64},{128,96},{160,128},{192,160},{224,1... | collective-permute-start | bytes 786440 | tf_op jit(solution)/shard_map/ppermute | solution.py:23
  54.9 6.9 %copy-start.2 = (bf16[8,128,256]{2,1,0:T(8,128)(2,1)}, bf16[8,128,256]{2,1,0:T(8,128)(2,1)S(1)}, u32[]{:S(2)}) copy-start(bf16[8,128,256]{2,1,0:T(8,128)(2,1)S(1)} %collective-permute-done.18.refs_9_) | copy-start | bytes 1572868
  54.9 16.3 %collective-permute-start.22 = (bf16[4,128,256]{2,1,0:T(8,128)(2,1)S(1)}, bf16[4,128,256]{2,1,0:T(8,128)(2,1)S(1)}, u32[]{:S(2)}, u32[]{:S(2)}) collective-permute-start(bf16[4,128,256]{2,1,0:T(8,128)(2,1)S(1)} %slice.76), channel_id=1, source_target_pairs={{0,8},{8,16},{16,24},{24,0},{1,9},{9,17},{17,25},{25,1},{2,10},{10... | collective-permute-start | bytes 786440 | tf_op jit(solution)/shard_map/ppermute | solution.py:23
  55.0 6.8 %copy-start.3 = (bf16[8,128,256]{2,1,0:T(8,128)(2,1)}, bf16[8,128,256]{2,1,0:T(8,128)(2,1)S(1)}, u32[]{:S(2)}) copy-start(bf16[8,128,256]{2,1,0:T(8,128)(2,1)S(1)} %collective-permute-done.19.refs_10_) | copy-start | bytes 1572868
  55.1 16.2 %collective-permute-start.23 = (bf16[4,128,256]{2,1,0:T(8,128)(2,1)S(1)}, bf16[4,128,256]{2,1,0:T(8,128)(2,1)S(1)}, u32[]{:S(2)}, u32[]{:S(2)}) collective-permute-start(bf16[4,128,256]{2,1,0:T(8,128)(2,1)S(1)} %slice.77), channel_id=1, source_target_pairs={{0,24},{8,0},{16,8},{24,16},{1,25},{9,1},{17,9},{25,17},{2,26},{10... | collective-permute-start | bytes 786440 | tf_op jit(solution)/shard_map/ppermute | solution.py:23
  58.3 3.5 %copy-start.4 = (bf16[4,128,256]{2,1,0:T(8,128)(2,1)}, bf16[4,128,256]{2,1,0:T(8,128)(2,1)S(1)}, u32[]{:S(2)}) copy-start(bf16[4,128,256]{2,1,0:T(8,128)(2,1)S(1)} %collective-permute-done.8.refs_6_) | copy-start | bytes 786436
  58.4 12.9 %collective-permute-start.20 = (bf16[2,128,256]{2,1,0:T(8,128)(2,1)S(1)}, bf16[2,128,256]{2,1,0:T(8,128)(2,1)S(1)}, u32[]{:S(2)}, u32[]{:S(2)}) collective-permute-start(bf16[2,128,256]{2,1,0:T(8,128)(2,1)S(1)} %slice.74), channel_id=1, source_target_pairs={{0,32},{32,64},{64,96},{96,128},{128,160},{160,192},{192,224},{224... | collective-permute-start | bytes 393224 | tf_op jit(solution)/shard_map/ppermute | solution.py:23
  58.5 3.4 %copy-start.5 = (bf16[4,128,256]{2,1,0:T(8,128)(2,1)}, bf16[4,128,256]{2,1,0:T(8,128)(2,1)S(1)}, u32[]{:S(2)}) copy-start(bf16[4,128,256]{2,1,0:T(8,128)(2,1)S(1)} %collective-permute-done.9.refs_7_) | copy-start | bytes 786436
  58.5 12.7 %collective-permute-start.21 = (bf16[2,128,256]{2,1,0:T(8,128)(2,1)S(1)}, bf16[2,128,256]{2,1,0:T(8,128)(2,1)S(1)}, u32[]{:S(2)}, u32[]{:S(2)}) collective-permute-start(bf16[2,128,256]{2,1,0:T(8,128)(2,1)S(1)} %slice.75), channel_id=1, source_target_pairs={{0,224},{32,0},{64,32},{96,64},{128,96},{160,128},{192,160},{224,1... | collective-permute-start | bytes 393224 | tf_op jit(solution)/shard_map/ppermute | solution.py:23
  71.2 0.6 copy-start
  71.9 21.1 %copy-start.7 = (f32[256]{0:T(256)S(1)}, f32[256]{0:T(256)}, u32[]{:S(2)}) copy-start(f32[256]{0:T(256)} %param.11) | copy-start | bytes 3076
  75.0 2.7 %collective-permute-start.24 = (f32[1024,256]{1,0:T(8,128)S(1)}, f32[1024,256]{1,0:T(8,128)S(1)}, u32[]{:S(2)}, u32[]{:S(2)}) collective-permute-start(f32[1024,256]{1,0:T(8,128)S(1)} %get-tuple-element.15), channel_id=1, source_target_pairs={{0,1},{1,0},{2,3},{3,2},{4,5},{5,4},{6,7},{7,6},{8,9},{9,8},{10,11... | collective-permute-start | bytes 3145736 | tf_op jit(solution)/shard_map/ppermute | solution.py:23
  77.9 9.4 %collective-permute-start.25 = (f32[256,256]{1,0:T(8,128)S(1)}, f32[256,256]{1,0:T(8,128)S(1)}, u32[]{:S(2)}, u32[]{:S(2)}) collective-permute-start(f32[256,256]{1,0:T(8,128)S(1)} %get-tuple-element.18), channel_id=1, source_target_pairs={{0,2},{2,4},{4,6},{6,0},{1,3},{3,5},{5,7},{7,1},{8,10},{10,12},{12... | collective-permute-start | bytes 786440 | tf_op jit(solution)/shard_map/ppermute | solution.py:23
  79.2 13.7 %collective-permute-start.26 = (f32[256,256]{1,0:T(8,128)S(1)}, f32[256,256]{1,0:T(8,128)S(1)}, u32[]{:S(2)}, u32[]{:S(2)}) collective-permute-start(f32[256,256]{1,0:T(8,128)S(1)} %get-tuple-element.20), channel_id=1, source_target_pairs={{0,6},{2,0},{4,2},{6,4},{1,7},{3,1},{5,3},{7,5},{8,14},{10,8},{12,... | collective-permute-start | bytes 786440 | tf_op jit(solution)/shard_map/ppermute | solution.py:23
  80.2 12.7 %collective-permute-start.27 = (f32[256,256]{1,0:T(8,128)S(1)}, f32[256,256]{1,0:T(8,128)S(1)}, u32[]{:S(2)}, u32[]{:S(2)}) collective-permute-start(f32[256,256]{1,0:T(8,128)S(1)} %get-tuple-element.19), channel_id=1, source_target_pairs={{0,4},{2,6},{4,0},{6,2},{1,5},{3,7},{5,1},{7,3},{8,12},{10,14},{12... | collective-permute-start | bytes 786440 | tf_op jit(solution)/shard_map/ppermute | solution.py:23
  105.5 1.3 collective-permute-start.28

commit v3 on v2

--- a/solution.py
+++ b/solution.py
@@ -12,9 +12,8 @@
 HIGHEST = lax.Precision.HIGHEST
 BS = 128
 GROUP = 16
-CHUNKS = 7
 KIND = 1 << 20
-FIRST_LIMIT = 48
+PREPARE_LIMIT = 46
 SIZES = {"z": 8, "y": 4, "x": 4, "core": 2}
 
 
@@ -30,9 +29,9 @@
         for index in range(GROUP):
             place = step * GROUP + index
             entry = jnp.where(place < end, list_ref[place], spare)
-            row = pl.multiple_of((entry // 256) % 32 * BS, BS)
+            row = pl.multiple_of(((entry >> 8) & 31) * BS, BS)
             out_ref[pl.ds(row, BS), :] += jnp.dot(
-                blocks_ref[entry % 256], omega_ref[entry // 8192], preferred_element_type=f32
+                blocks_ref[entry & 255], omega_ref[entry >> 13], preferred_element_type=f32
             )
         return carry
 
@@ -46,112 +45,100 @@
     ]
 
 
-def first_kernel(entries_ref, *refs, places):
-    part_refs = refs[:len(places)]
-    source_ref, out_ref, blocks_ref, late_ref, late_count_ref = refs[len(places):-4]
-    early_ref, omega_ref, sems, block_sems = refs[-4:]
-    slots = blocks_ref.shape[0]
-    chunk = slots // CHUNKS
-    loads = [
-        pltpu.make_async_copy(
-            source_ref.at[pl.ds(i * chunk, chunk)],
-            blocks_ref.at[pl.ds(i * chunk, chunk)],
-            block_sems.at[i],
-        )
-        for i in range(CHUNKS)
-    ]
-    copies = copies_of(part_refs, places, omega_ref, sems)
-    for copy in loads[:1] + copies + loads[1:]:
-        copy.start()
-    out_ref[...] = jnp.zeros_like(out_ref)
+def prepare_kernel(entries_ref, source_ref, blocks_ref, early_ref, late_ref, counts_ref, token_ref, sem):
+    load = pltpu.make_async_copy(source_ref, blocks_ref, sem)
+    load.start()
+    token_ref[...] = jnp.zeros_like(token_ref)
 
     def sort(slot, counts):
         early, late = counts
         entry = entries_ref[slot]
-        kind = entry // KIND
+        kind = entry >> 20
         early_ref[early] = entry
-        late_ref[late] = entry - KIND
-        return early + (kind == 0).astype(jnp.int32), late + (kind == 1).astype(jnp.int32)
-
-    counts, ends = (jnp.int32(0), jnp.int32(0)), []
-    for i in range(CHUNKS):
-        counts = lax.fori_loop(i * chunk, (i + 1) * chunk, sort, counts, unroll=8)
-        ends.append(counts[0])
-    late_count_ref[0] = counts[1]
-    for copy in copies:
-        copy.wait()
-    done = 0
-    for i, copy in enumerate(loads):
-        copy.wait()
-        full = ends[i] // GROUP if i < CHUNKS - 1 else (ends[i] + GROUP - 1) // GROUP
-        add_groups((done, full), ends[i], early_ref, blocks_ref, omega_ref, out_ref)
-        done = full
-
-
-def rest_kernel(late_ref, late_count_ref, *refs, places):
+        late_ref[late] = entry & (KIND - 1)
+        return early + ((kind + 3) >> 2 ^ 1), late + (kind & 1)
+
+    start = jnp.int32(0), jnp.int32(0)
+    counts_ref[0], counts_ref[1] = lax.fori_loop(0, blocks_ref.shape[0], sort, start, unroll=8)
+    load.wait()
+
+
+def multiply_kernel(list_ref, counts_ref, *refs, places, first):
     part_refs = refs[:len(places)]
-    out_ref, blocks_ref, theirs_ref, ours_ref, omega_ref, sems = refs[len(places):]
+    blocks_ref, omega_ref, sems = refs[len(places)], *refs[-2:]
     copies = copies_of(part_refs, places, omega_ref, sems)
     for copy in copies:
         copy.start()
+    if first:
+        out_ref = refs[len(places) + 1]
+        out_ref[...] = jnp.zeros_like(out_ref)
+    else:
+        out_ref, theirs_ref, ours_ref, peak_ref = refs[len(places) + 1:-2]
     for copy in copies:
         copy.wait()
-    count = late_count_ref[0]
+    count = counts_ref[0 if first else 1]
     groups = 0, (count + GROUP - 1) // GROUP
-    add_groups(groups, count, late_ref, blocks_ref, omega_ref, out_ref)
-    half = theirs_ref.shape[0]
-    theirs_ref[...] = out_ref[pl.ds(0, half), :]
-    ours_ref[...] = out_ref[pl.ds(half, half), :]
-
-
-def block_products(entries, early, late, blocks, total):
-    slots, width = blocks.shape[0], early[0][0].shape[-1]
+    add_groups(groups, count, list_ref, blocks_ref, omega_ref, out_ref)
+    if not first:
+        half = ours_ref.shape[0]
+        theirs, ours = out_ref[pl.ds(0, half), :], out_ref[pl.ds(half, half), :]
+        theirs_ref[pl.ds(0, half), :] = theirs
+        ours_ref[...] = ours
+        for value, ref in ((theirs, theirs_ref.at[pl.ds(half, 8)]), (ours, peak_ref)):
+            peak = jnp.max(jnp.abs(value), axis=0, keepdims=True)
+            ref[...] = jnp.broadcast_to(peak, ref.shape)
+
+
+def prepare(entries, blocks):
     smem, vmem = (pl.BlockSpec(memory_space=space) for space in (pltpu.SMEM, pltpu.VMEM))
-    anywhere = pl.BlockSpec(memory_space=pl.ANY)
-
-    def places_of(parts):
-        return [place for _, place in parts]
-
-    def omega_scratch(parts):
-        held = max(sum(place) for place in places_of(parts))
-        return pltpu.VMEM((held, BS, width), jnp.bfloat16)
-
-    def params(mebibytes):
-        return pltpu.CompilerParams(vmem_limit_bytes=mebibytes * 1024 * 1024)
-
-    def cost(flops):
-        return pl.CostEstimate(flops=flops, bytes_accessed=0, transcendentals=0)
-
-    before, held, late_list, late_count = pl.pallas_call(
-        lambda *refs: first_kernel(*refs, places=places_of(early)),
-        in_specs=[smem] + [anywhere] * (len(early) + 1),
-        out_specs=(vmem, vmem, smem, smem),
+    listed = jax.ShapeDtypeStruct((blocks.shape[0] + 2 * GROUP,), jnp.int32)
+    return pl.pallas_call(
+        prepare_kernel,
+        in_specs=[smem, pl.BlockSpec(memory_space=pl.ANY)],
+        out_specs=(vmem, smem, smem, smem, vmem),
         out_shape=(
-            pltpu.VMEM((total + BS, width), f32),
             pltpu.VMEM(blocks.shape, blocks.dtype),
-            jax.ShapeDtypeStruct((slots + 2 * GROUP,), jnp.int32),
-            jax.ShapeDtypeStruct((1,), jnp.int32),
+            listed,
+            listed,
+            jax.ShapeDtypeStruct((2,), jnp.int32),
+            jax.ShapeDtypeStruct((16, BS), jnp.bfloat16),
         ),
+        scratch_shapes=[pltpu.SemaphoreType.DMA(())],
+        compiler_params=pltpu.CompilerParams(vmem_limit_bytes=PREPARE_LIMIT * 1024 * 1024),
+        cost_estimate=pl.CostEstimate(
+            flops=0, bytes_accessed=8 * blocks.size, transcendentals=0
+        ),
+        name="prepare",
+    )(entries, blocks)
+
+
+def multiply(slots, counts, parts, blocks, total, before=None):
+    first, width = before is None, parts[0][0].shape[-1]
+    places = [place for _, place in parts]
+    smem, vmem = (pl.BlockSpec(memory_space=space) for space in (pltpu.SMEM, pltpu.VMEM))
+    if first:
+        out_shape = pltpu.VMEM((total + BS, width), f32)
+    else:
+        out_shape = tuple(
+            jax.ShapeDtypeStruct((rows, width), f32) for rows in (total // 2 + 8, total // 2, 8)
+        )
+    return pl.pallas_call(
+        lambda *refs: multiply_kernel(*refs, places=places, first=first),
+        in_specs=[smem] * 2
+        + [pl.BlockSpec(memory_space=pl.ANY)] * len(parts)
+        + [vmem] * (1 if first else 2),
+        out_specs=vmem if first else (vmem,) * 3,
+        out_shape=out_shape,
         scratch_shapes=[
-            pltpu.SMEM((slots + 2 * GROUP,), jnp.int32),
-            omega_scratch(early),
-            pltpu.SemaphoreType.DMA((len(early),)),
-            pltpu.SemaphoreType.DMA((CHUNKS,)),
+            pltpu.VMEM((max(sum(place) for place in places), BS, width), jnp.bfloat16),
+            pltpu.SemaphoreType.DMA((len(parts),)),
         ],
-        compiler_params=params(FIRST_LIMIT),
-        cost_estimate=cost(6 * 10**9),
-        name="multiply_first",
-    )(entries, *(part for part, _ in early), blocks)
-    return pl.pallas_call(
-        lambda *refs: rest_kernel(*refs, places=places_of(late)),
-        in_specs=[smem] * 2 + [anywhere] * len(late) + [vmem] * 2,
-        out_specs=(vmem, vmem),
-        out_shape=(jax.ShapeDtypeStruct((total // 2, width), f32),) * 2,
-        scratch_shapes=[omega_scratch(late), pltpu.SemaphoreType.DMA((len(late),))],
-        compiler_params=params(24),
-        cost_estimate=cost(10**9),
-        name="multiply_rest",
-    )(late_list, late_count, *(part for part, _ in late), before, held)
+        compiler_params=pltpu.CompilerParams(vmem_limit_bytes=24 * 1024 * 1024),
+        cost_estimate=pl.CostEstimate(
+            flops=(6 if first else 1) * 10**9, bytes_accessed=0, transcendentals=0
+        ),
+        name="multiply_first" if first else "multiply_rest",
+    )(slots, counts, *(part for part, _ in parts), blocks, *(() if first else (before,)))
 
 
 def dot(a, b, contract):
@@ -263,38 +250,67 @@
     return spread(part, ("y", "x"), 16).reshape(packed.shape)
 
 
-def gather(omega):
+def split_shift(value, axis):
+    size = SIZES[axis]
+    pairs = []
+    for i in range(size):
+        pairs += [(2 * i, 2 * ((i + 1) % size)), (2 * i + 1, 2 * ((i - 1) % size) + 1)]
+    return lax.ppermute(value, (axis, "core"), pairs)
+
+
+def gather(omega, token):
     half = omega.shape[0] // 2
 
-    def ring(block, axis):
+    def short_way(both, axis):
+        count = SIZES[axis] // 2
+        steps = [both]
+        for _ in range(count - 1):
+            steps.append(split_shift(steps[-1], axis))
+        end = split_shift(steps[-1][:1], axis)
+        others = shift(jnp.concatenate([step[1:] for step in steps[1:]], 0), "core", 1)
+        near = [step[:1] for step in steps]
+        return jnp.concatenate([near[0], others, end] + near[:0:-1], 0)
+
+    def ring(block, axis, token=None):
         size = SIZES[axis]
         forth, back, found = block, block, {0: block}
         for step in range(1, size // 2):
             forth, back = shift(forth, axis, 1), shift(back, axis, -1)
+            if step == 1 and token is not None:
+                forth, token = lax.optimization_barrier((forth, token))
             found[size - step], found[step] = forth, back
         return found, forth, back
 
-    def last(forth, back, axis, dim):
-        cut = forth.shape[dim] // 2
-        return (
-            shift(lax.slice_in_dim(forth, 0, cut, axis=dim), axis, 1),
-            shift(lax.slice_in_dim(back, cut, 2 * cut, axis=dim), axis, -1),
-        )
-
-    first, second = omega[None, :half], omega[None, half:]
-    found1, forth1, back1 = ring(first, "y")
-    found2, forth2, back2 = ring(second, "z")
-    found1[2] = jnp.concatenate(last(forth1, back1, "y", 1), 1)
-    found2[4] = jnp.concatenate(last(forth2, back2, "z", 1), 1)
-    block1 = jnp.concatenate([found1[i] for i in range(4)], 0)
-    block2 = jnp.concatenate([found2[i] for i in range(8)], 0)
-    full1, forth1, back1 = ring(block1, "z")
+    def last(forth, back, axis):
+        cut = forth.shape[0] // 2
+        return shift(forth[:cut], axis, 1), shift(back[cut:], axis, -1)
+
+    both = jnp.stack([omega, shift(omega, "core", 1)])
+    block1, block2 = short_way(both[:, :half], "y"), short_way(both[:, half:], "z")
+    full1, forth1, back1 = ring(block1, "z", token)
     full2, forth2, back2 = ring(block2, "y")
-    end1, end2 = last(forth1, back1, "z", 0), last(forth2, back2, "y", 0)
+    end1, end2 = last(forth1, back1, "z"), last(forth2, back2, "y")
     early = [(full1[dz], (4 * dz, 4)) for dz in (0, 7, 1, 6, 2, 5, 3)]
     early += [(full2[dy], (32 + 8 * dy, 8)) for dy in (0, 3, 1)]
     late = [(end1[0], (0, 2)), (end1[1], (2, 2)), (end2[0], (4, 4)), (end2[1], (8, 4))]
     return early, late
+
+
+def sum_over_columns(theirs, ours, peak):
+    received = shift(theirs, "core", 1)
+    count = ours.shape[0]
+    ours = ours + received[:count]
+    rows = count // 4
+    bound = jnp.maximum(peak[:1] + received[count:count + 1], 1e-30)
+    exponent = jnp.ceil(jnp.log2(bound)) - 13.0
+    sent = ours[rows:] * jnp.exp2(-exponent)
+    exponents = jnp.broadcast_to(exponent, (16, exponent.shape[1]))
+    result = ours[:rows]
+    for k in (2, 1, 3):
+        term = jnp.concatenate([sent[(k - 1) * rows:k * rows], exponents], 0)
+        term = shift(term.astype(jnp.float16), "x", k).astype(f32)
+        result = result + term[:rows] * jnp.exp2(term[rows:rows + 1])
+    return result
 
 
 def shards(blocks, block_rows, block_cols, live_counts, omega, row_scale):
@@ -311,6 +327,9 @@
     far_z, far_y = (cols // 8 - z_here + 8) % 8, (cols // 2 - y_here + 4) % 4
     is_second = cols % 2
     is_late = jnp.where(is_second == 1, far_y == 2, far_z == 4)
+    back = core_here == 1
+    far_z = jnp.where(back & (is_second == 1), (8 - far_z) % 8, far_z)
+    far_y = jnp.where(back & (is_second == 0), (4 - far_y) % 4, far_y)
     cols = jnp.where(
         is_late,
         jnp.where(is_second == 1, 4 + far_z, far_y),
@@ -319,12 +338,12 @@
     slot = jnp.arange(rows.shape[0], dtype=jnp.int32)
     kind = jnp.where(slot < count, is_late.astype(jnp.int32), 2)
     entries = slot + 256 * rows + 8192 * cols + KIND * kind
-    early, late = gather(omega)
-    theirs, ours = block_products(entries, early, late, blocks[0, 0], row_blocks * BS)
-    ours = ours + shift(theirs, "core", 1)
-    pieces = ours.reshape(4, own_rows, width)
-    arrived = [shift(pieces[k], "x", k) for k in (1, 3, 2)]
-    sketch = pieces[0] + arrived[0] + arrived[1] + arrived[2]
+    held, early_list, late_list, counts, token = prepare(entries, blocks[0, 0])
+    early, late = gather(omega, token)
+    total = row_blocks * BS
+    before = multiply(early_list, counts, early, held, total)
+    theirs, ours, peak = multiply(late_list, counts, late, held, total, before)
+    sketch = sum_over_columns(theirs, ours, peak)
     sketch = sketch * row_scale[:, None]
     gram = sum_over_all(dot(sketch, sketch, (0, 0)))
     factor, basis = orthonormalize(gram, sketch, own_rows * 256)

time: 142 us -> 129 us (0.908)
  starting transfers between devices: 44.5 us -> 32 us
  blocking collectives: 35.4 us -> 40.5 us
  waiting for transfers between devices: 31.7 us -> 28.4 us
  local copies, waits for them, and re-layouts: 2.58 us -> 1.16 us
    ppermute x29 -> x20, starting transfers between devices: 44.5 us -> 26.7 us  [shift(): lax.ppermute(value, axis, [(i, (i + step) % size) for i in range(size)])]
    ppermute x29 -> x20, waiting for transfers between devices: 31.7 us -> 19.7 us  [shift(): lax.ppermute(value, axis, [(i, (i + step) % size) for i in range(size)])]
    ppermute x0 -> x6, waiting for transfers between devices: none -> 8.66 us  [split_shift(): return lax.ppermute(value, (axis, 'core'), pairs)]
    ppermute x0 -> x6, starting transfers between devices: none -> 5.31 us  [split_shift(): return lax.ppermute(value, (axis, 'core'), pairs)]
    all_to_all x2, blocking collectives: 23.6 us -> 27.2 us  [spread(): return lax.all_to_all(copies, axes, 0, 0, tiled=True)]
    all_to_all x1, blocking collectives: 11.7 us -> 13.3 us  [sum_over_all(): part = lax.all_to_all(pieces, ('y', 'x'), 0, 0, tiled=True).sum(0)]
    pallas_call x2 -> x3, Pallas kernels: 12.5 us -> 12.3 us  [the longest x2 7.98 us: multiply(): pl.pallas_call(lambda *refs: multiply_kernel(*refs, places=places, first=...]
  transfers between devices with their start and end apart: 29 -> 26, of which waited for: 8 -> 12; matrix products, arithmetic and copies ran while one was open for 2% -> 1% of each run, Pallas kernels for 7% -> 8%
where the time goes in v3:
time: 129 us
  blocking collectives  40.5 us (31%)
  starting transfers between devices  32 us (25%)
  waiting for transfers between devices  28.4 us (22%)
  Pallas kernels  23.2 us (18%)
  between operations  1.7 us (1%)
  other arithmetic  1.59 us (1%)
    all_to_all x2, blocking collectives, spread(): return lax.all_to_all(copies, axes, 0, 0, tiled=True)  27.2 us
    ppermute x20, starting transfers between devices, shift(): lax.ppermute(value, axis, [(i, (i + step) % size) for i in range(size)])  26.7 us
    ppermute x20, waiting for transfers between devices, shift(): lax.ppermute(value, axis, [(i, (i + step) % size) for i in range(size)])  19.7 us
    all_to_all x1, blocking collectives, sum_over_all(): part = lax.all_to_all(pieces, ('y', 'x'), 0, 0, tiled=True).sum(0)  13.3 us
    pallas_call x1, Pallas kernels, orthonormalize(): pl.pallas_call(lambda *refs: factor_kernel(*refs, scale=math.sqrt(vertex_...  11 us
    ppermute x6, waiting for transfers between devices, split_shift(): return lax.ppermute(value, (axis, 'core'), pairs)  8.66 us
    pallas_call x2, Pallas kernels, multiply(): pl.pallas_call(lambda *refs: multiply_kernel(*refs, places=places, first=...  7.98 us
    ppermute x6, starting transfers between devices, split_shift(): return lax.ppermute(value, (axis, 'core'), pairs)  5.31 us
  transfers between devices with their start and end apart: 26, of which 12 were waited for; matrix products, arithmetic and copies ran while one was open for 1% of the time, Pallas kernels for 8%

profile of v3, /device:TPU:2, one launch (start us, length us, event | category | flops | bytes accessed | tf_op | source)
XLA Modules:
  0.0 129.2 jit_solution(6625894337653449082)
XLA Ops:
  0.6 0.1 collective-permute-start
  0.7 1.5 %collective-permute-done = bf16[256,256]{1,0:T(8,128)(2,1)S(1)} collective-permute-done((bf16[256,256]{1,0:T(8,128)(2,1)}, bf16[256,256]{1,0:T(8,128)(2,1)S(1)}, u32[]{:S(2)}, u32[]{:S(2)}) %collective-permute-start) | collective-permute-done | bytes 131104 | tf_op jit(solution)/shard_map/ppermute | solution.py:22
  2.3 0.9 pad_maximum_fusion.6
  3.2 2.0 %collective-permute-start.12 = (bf16[2,128,256]{2,1,0:T(8,128)(2,1)S(1)}, bf16[2,128,256]{2,1,0:T(8,128)(2,1)S(1)}, u32[]{:S(2)}, u32[]{:S(2)}) collective-permute-start(bf16[2,128,256]{2,1,0:T(8,128)(2,1)S(1)} %get-tuple-element.25), channel_id=1, source_target_pairs={{0,32},{1,225},{32,64},{33,1},{64,96},{65,33},{96,128},{97,65},{12... | collective-permute-start | bytes 393224 | tf_op jit(solution)/shard_map/ppermute | solution.py:258
  5.2 1.6 %collective-permute-start.1 = (bf16[2,128,256]{2,1,0:T(8,128)(2,1)S(1)}, bf16[2,128,256]{2,1,0:T(8,128)(2,1)S(1)}, u32[]{:S(2)}, u32[]{:S(2)}) collective-permute-start(bf16[2,128,256]{2,1,0:T(8,128)(2,1)S(1)} %get-tuple-element.26), channel_id=1, source_target_pairs={{0,8},{1,25},{8,16},{9,1},{16,24},{17,9},{24,0},{25,17},{2,10},{3,... | collective-permute-start | bytes 393224 | tf_op jit(solution)/shard_map/ppermute | solution.py:258
  6.7 5.3 %collective-permute-done.12 = bf16[2,128,256]{2,1,0:T(8,128)(2,1)S(1)} collective-permute-done((bf16[2,128,256]{2,1,0:T(8,128)(2,1)S(1)}, bf16[2,128,256]{2,1,0:T(8,128)(2,1)S(1)}, u32[]{:S(2)}, u32[]{:S(2)}) %collective-permute-start.12) | collective-permute-done | bytes 131104 | tf_op jit(solution)/shard_map/ppermute | solution.py:258
  12.1 1.7 %collective-permute-start.3 = (bf16[1,128,256]{2,1,0:T(8,128)(2,1)S(1)}, bf16[1,128,256]{2,1,0:T(8,128)(2,1)S(1)}, u32[]{:S(2)}, u32[]{:S(2)}) collective-permute-start(bf16[1,128,256]{2,1,0:T(8,128)(2,1)S(1)} %get-tuple-element.32), channel_id=1, source_target_pairs={{0,8},{1,25},{8,16},{9,1},{16,24},{17,9},{24,0},{25,17},{2,10},{3,... | collective-permute-start | bytes 196616 | tf_op jit(solution)/shard_map/ppermute | solution.py:258
  13.7 3.1 %collective-permute-start.2 = (bf16[1,128,256]{2,1,0:T(8,128)(2,1)S(1)}, bf16[1,128,256]{2,1,0:T(8,128)(2,1)S(1)}, u32[]{:S(2)}, u32[]{:S(2)}) collective-permute-start(bf16[1,128,256]{2,1,0:T(8,128)(2,1)S(1)} %get-tuple-element.31), channel_id=1, source_target_pairs={{0,1},{1,0},{2,3},{3,2},{4,5},{5,4},{6,7},{7,6},{8,9},{9,8},{10,11... | collective-permute-start | bytes 196616 | tf_op jit(solution)/shard_map/ppermute | solution.py:22
  16.8 1.4 %collective-permute-done.13 = bf16[2,128,256]{2,1,0:T(8,128)(2,1)S(1)} collective-permute-done((bf16[2,128,256]{2,1,0:T(8,128)(2,1)S(1)}, bf16[2,128,256]{2,1,0:T(8,128)(2,1)S(1)}, u32[]{:S(2)}, u32[]{:S(2)}) %collective-permute-start.13) | collective-permute-done | bytes 131104 | tf_op jit(solution)/shard_map/ppermute | solution.py:258
  18.2 0.9 slice_dynamic-update-slice_fusion.2
  19.2 3.3 %collective-permute-start.8 = (bf16[4,128,256]{2,1,0:T(8,128)(2,1)S(1)}, bf16[4,128,256]{2,1,0:T(8,128)(2,1)S(1)}, u32[]{:S(2)}, u32[]{:S(2)}) collective-permute-start(bf16[4,128,256]{2,1,0:T(8,128)(2,1)S(1)} %pad_maximum_fusion.refs_2_), channel_id=1, source_target_pairs={{0,224},{32,0},{64,32},{96,64},{128,96},{160,128},{192,160},{224,1... | collective-permute-start | bytes 786440 | tf_op jit(solution)/shard_map/ppermute | solution.py:22
  22.5 1.9 %collective-permute-done.14 = bf16[2,128,256]{2,1,0:T(8,128)(2,1)S(1)} collective-permute-done((bf16[2,128,256]{2,1,0:T(8,128)(2,1)S(1)}, bf16[2,128,256]{2,1,0:T(8,128)(2,1)S(1)}, u32[]{:S(2)}, u32[]{:S(2)}) %collective-permute-start.14) | collective-permute-done | bytes 131104 | tf_op jit(solution)/shard_map/ppermute | solution.py:258
  24.5 0.1 collective-permute-start.15
  24.6 0.1 collective-permute-start.16
  24.7 5.4 %collective-permute-done.4.refs_3_ = bf16[4,128,256]{2,1,0:T(8,128)(2,1)S(1)} collective-permute-done((bf16[4,128,256]{2,1,0:T(8,128)(2,1)S(1)}, bf16[4,128,256]{2,1,0:T(8,128)(2,1)S(1)}, u32[]{:S(2)}, u32[]{:S(2)}) %collective-permute-start.4) | collective-permute-done | bytes 262176 | tf_op jit(solution)/shard_map/ppermute | solution.py:22
  30.1 0.2 collective-permute-start.5
  30.3 3.0 %collective-permute-start.9 = (bf16[4,128,256]{2,1,0:T(8,128)(2,1)S(1)}, bf16[4,128,256]{2,1,0:T(8,128)(2,1)S(1)}, u32[]{:S(2)}, u32[]{:S(2)}) collective-permute-start(bf16[4,128,256]{2,1,0:T(8,128)(2,1)S(1)} %collective-permute-done.8.refs_4_), channel_id=1, source_target_pairs={{0,224},{32,0},{64,32},{96,64},{128,96},{160,128},{192,160},{224,1... | collective-permute-start | bytes 786440 | tf_op jit(solution)/shard_map/ppermute | solution.py:22
  33.4 1.7 %collective-permute-start.17 = (bf16[8,128,256]{2,1,0:T(8,128)(2,1)S(1)}, bf16[8,128,256]{2,1,0:T(8,128)(2,1)S(1)}, u32[]{:S(2)}, u32[]{:S(2)}) collective-permute-start(bf16[8,128,256]{2,1,0:T(8,128)(2,1)S(1)} %slice_dynamic-update-slice_fusion.refs_9_), channel_id=1, source_target_pairs={{0,8},{8,16},{16,24},{24,0},{1,9},{9,17},{17,25},{25,1},{2,10},{10... | collective-permute-start | bytes 1572872 | tf_op jit(solution)/shard_map/ppermute | solution.py:22
  35.1 1.7 %collective-permute-start.19 = (bf16[8,128,256]{2,1,0:T(8,128)(2,1)S(1)}, bf16[8,128,256]{2,1,0:T(8,128)(2,1)S(1)}, u32[]{:S(2)}, u32[]{:S(2)}) collective-permute-start(bf16[8,128,256]{2,1,0:T(8,128)(2,1)S(1)} %slice_dynamic-update-slice_fusion.refs_9_), channel_id=1, source_target_pairs={{0,24},{8,0},{16,8},{24,16},{1,25},{9,1},{17,9},{25,17},{2,26},{10... | collective-permute-start | bytes 1572872 | tf_op jit(solution)/shard_map/ppermute | solution.py:22
  36.8 1.1 collective-permute-done.9.refs_6_
  37.9 3.7 %collective-permute-start.10 = (bf16[4,128,256]{2,1,0:T(8,128)(2,1)S(1)}, bf16[4,128,256]{2,1,0:T(8,128)(2,1)S(1)}, u32[]{:S(2)}, u32[]{:S(2)}) collective-permute-start(bf16[4,128,256]{2,1,0:T(8,128)(2,1)S(1)} %collective-permute-done.9.refs_6_), channel_id=1, source_target_pairs={{0,224},{32,0},{64,32},{96,64},{128,96},{160,128},{192,160},{224,1... | collective-permute-start | bytes 786440 | tf_op jit(solution)/shard_map/ppermute | solution.py:22
  42.3 4.3 %prepare.1 = (bf16[224,128,128]{2,1,0:T(8,128)(2,1)S(1)}, s32[256]{0:T(256)S(1)}, s32[256]{0:T(256)S(1)}, s32[2]{0:T(128)S(1)}, bf16[16,128]{1,0:T(8,128)(2,1)}) custom-call(s32[224]{0:T(256)S(1)} %fusion.10.entries_ref, bf16[224,128,128]{2,1,0:T(8,128)(2,1)} %bitcast.16), custom_call_target="tpu_custom_call" | custom-call | bytes 29360128 | tf_op jit(solution)/shard_map/prepare/pallas_call | solution.py:95
  46.6 3.7 %collective-permute-start.11 = (bf16[2,128,256]{2,1,0:T(8,128)(2,1)S(1)}, bf16[2,128,256]{2,1,0:T(8,128)(2,1)S(1)}, u32[]{:S(2)}, u32[]{:S(2)}) collective-permute-start(bf16[2,128,256]{2,1,0:T(8,128)(2,1)S(1)} %slice.145), channel_id=1, source_target_pairs={{0,224},{32,0},{64,32},{96,64},{128,96},{160,128},{192,160},{224,1... | collective-permute-start | bytes 393224 | tf_op jit(solution)/shard_map/ppermute | solution.py:22
  50.3 0.1 collective-permute-done.6.refs_7_
  50.4 0.1 collective-permute-start.7
  50.5 1.7 %collective-permute-start.18 = (bf16[4,128,256]{2,1,0:T(8,128)(2,1)S(1)}, bf16[4,128,256]{2,1,0:T(8,128)(2,1)S(1)}, u32[]{:S(2)}, u32[]{:S(2)}) collective-permute-start(bf16[4,128,256]{2,1,0:T(8,128)(2,1)S(1)} %slice.153), channel_id=1, source_target_pairs={{0,8},{8,16},{16,24},{24,0},{1,9},{9,17},{17,25},{25,1},{2,10},{10... | collective-permute-start | bytes 786440 | tf_op jit(solution)/shard_map/ppermute | solution.py:22
  52.2 1.7 %collective-permute-start.20 = (bf16[4,128,256]{2,1,0:T(8,128)(2,1)S(1)}, bf16[4,128,256]{2,1,0:T(8,128)(2,1)S(1)}, u32[]{:S(2)}, u32[]{:S(2)}) collective-permute-start(bf16[4,128,256]{2,1,0:T(8,128)(2,1)S(1)} %slice.154), channel_id=1, source_target_pairs={{0,24},{8,0},{16,8},{24,16},{1,25},{9,1},{17,9},{25,17},{2,26},{10... | collective-permute-start | bytes 786440 | tf_op jit(solution)/shard_map/ppermute | solution.py:22
  54.0 5.5 %multiply_first.1.refs_7_ = f32[2176,256]{1,0:T(8,128)S(1)} custom-call(s32[256]{0:T(256)S(1)} %get-tuple-element.14.refs_0_, s32[2]{0:T(128)S(1)} %get-tuple-element.12.refs_1_, bf16[4,128,256]{2,1,0:T(8,128)(2,1)S(1)} %pad_maximum_fusion.refs_2_, bf16[4,128,256]{2,1,0:T(8,128)(2,1)S(1)} %collective-permute-done.4.refs_3_, ...), custom_call_target="tpu_custom_call" | custom-call | flops 6000000000 | tf_op jit(solution)/shard_map/multiply_first/pallas_call | solution.py:125
  59.5 2.5 %multiply_rest.1 = (f32[1032,256]{1,0:T(8,128)S(1)}, f32[1024,256]{1,0:T(8,128)S(1)}, f32[8,256]{1,0:T(8,128)S(1)}) custom-call(s32[256]{0:T(256)S(1)} %get-tuple-element.11.refs_0_, s32[2]{0:T(128)S(1)} %get-tuple-element.12.refs_1_, bf16[2,128,256]{2,1,0:T(8,128)(2,1)S(1)} %collective-permute-done.7.refs_2_, ...), custom_call_target="tpu_custom_call" | custom-call | flops 1000000000 | tf_op jit(solution)/shard_map/multiply_rest/pallas_call | solution.py:125
  62.0 0.1 collective-permute-start.21
  62.1 2.7 %collective-permute-done.21 = f32[1032,256]{1,0:T(8,128)S(1)} collective-permute-done((f32[1032,256]{1,0:T(8,128)S(1)}, f32[1032,256]{1,0:T(8,128)S(1)}, u32[]{:S(2)}, u32[]{:S(2)}) %collective-permute-start.21) | collective-permute-done | bytes 1056800 | tf_op jit(solution)/shard_map/ppermute | solution.py:22
  64.8 0.1 slice_add_fusion
  64.9 0.1 fusion
  65.1 0.1 pad_maximum_fusion.3
  65.3 0.5 collective-permute-start.22
  65.7 1.6 %collective-permute-start.23 = (f16[272,256]{1,0:T(8,128)(2,1)S(1)}, f16[272,256]{1,0:T(8,128)(2,1)S(1)}, u32[]{:S(2)}, u32[]{:S(2)}) collective-permute-start(f16[272,256]{1,0:T(8,128)(2,1)S(1)} %get-tuple-element.34), channel_id=1, source_target_pairs={{0,2},{2,4},{4,6},{6,0},{1,3},{3,5},{5,7},{7,1},{8,10},{10,12},{12... | collective-permute-start | bytes 417800 | tf_op jit(solution)/shard_map/ppermute | solution.py:22
  67.3 0.4 collective-permute-start.24
  67.7 5.7 %collective-permute-done.22 = f16[272,256]{1,0:T(8,128)(2,1)S(1)} collective-permute-done((f16[272,256]{1,0:T(8,128)(2,1)S(1)}, f16[272,256]{1,0:T(8,128)(2,1)S(1)}, u32[]{:S(2)}, u32[]{:S(2)}) %collective-permute-start.22) | collective-permute-done | bytes 139296 | tf_op jit(solution)/shard_map/ppermute | solution.py:22
  73.4 0.4 collective-permute-done.23
  73.9 1.7 %collective-permute-done.24 = f16[272,256]{1,0:T(8,128)(2,1)S(1)} collective-permute-done((f16[272,256]{1,0:T(8,128)(2,1)S(1)}, f16[272,256]{1,0:T(8,128)(2,1)S(1)}, u32[]{:S(2)}, u32[]{:S(2)}) %collective-permute-start.24) | collective-permute-done | bytes 139296 | tf_op jit(solution)/shard_map/ppermute | solution.py:22
  75.6 0.1 fusion.2.refs_1_
  75.7 0.6 fusion.24
  76.4 13.3 %all_to_all.15 = f32[16,24,128]{2,1,0:T(8,128)S(1)} all-to-all(f32[16,24,128]{2,1,0:T(8,128)S(1)} %bitcast.17), channel_id=1, replica_groups=mesh['z'=8,'y'=4,'x'=4,'core'=2] {'y','x'}, dimensions={0} | all-to-all | bytes 393216 | tf_op jit(solution)/shard_map/all_to_all | solution.py:247
  89.7 0.1 collective-permute-start.25
  89.8 1.2 collective-permute-done.25
  91.0 15.9 %all_to_all.16 = f32[8,24,128]{2,1,0:T(8,128)S(1)} all-to-all(f32[8,24,128]{2,1,0:T(8,128)S(1)} %broadcast_in_dim.31), channel_id=1, replica_groups=mesh['z'=8,'y'=4,'x'=4,'core'=2] {'z'}, dimensions={0} | all-to-all | bytes 196608 | tf_op jit(solution)/shard_map/all_to_all | solution.py:240
  106.9 11.3 %all_to_all.17 = f32[16,24,128]{2,1,0:T(8,128)S(1)} all-to-all(f32[16,24,128]{2,1,0:T(8,128)S(1)} %broadcast_in_dim.32), channel_id=1, replica_groups=mesh['z'=8,'y'=4,'x'=4,'core'=2] {'y','x'}, dimensions={0} | all-to-all | bytes 393216 | tf_op jit(solution)/shard_map/all_to_all | solution.py:240
  118.2 11.0 %orthonormalize.1 = (f32[256,256]{1,0:T(8,128)}, f32[256,256]{1,0:T(8,128)}) custom-call(f32[384,128]{1,0:T(8,128)S(1)} %bitcast.15, f32[256,256]{1,0:T(8,128)S(1)} %fusion.2.refs_1_), custom_call_target="tpu_custom_call" | custom-call | tf_op jit(solution)/shard_map/orthonormalize/pallas_call | solution.py:227
  (58 shorter events, 0.6 us)
Async XLA Ops:
  0.6 1.6 %collective-permute-start = (bf16[256,256]{1,0:T(8,128)(2,1)}, bf16[256,256]{1,0:T(8,128)(2,1)S(1)}, u32[]{:S(2)}, u32[]{:S(2)}) collective-permute-start(bf16[256,256]{1,0:T(8,128)(2,1)} %param.10), channel_id=1, source_target_pairs={{0,1},{1,0},{2,3},{3,2},{4,5},{5,4},{6,7},{7,6},{8,9},{9,8},{10,11... | collective-permute-start | bytes 393224 | tf_op jit(solution)/shard_map/ppermute | solution.py:22
  3.2 8.9 %collective-permute-start.12 = (bf16[2,128,256]{2,1,0:T(8,128)(2,1)S(1)}, bf16[2,128,256]{2,1,0:T(8,128)(2,1)S(1)}, u32[]{:S(2)}, u32[]{:S(2)}) collective-permute-start(bf16[2,128,256]{2,1,0:T(8,128)(2,1)S(1)} %get-tuple-element.25), channel_id=1, source_target_pairs={{0,32},{1,225},{32,64},{33,1},{64,96},{65,33},{96,128},{97,65},{12... | collective-permute-start | bytes 393224 | tf_op jit(solution)/shard_map/ppermute | solution.py:258
  5.2 6.9 %collective-permute-start.1 = (bf16[2,128,256]{2,1,0:T(8,128)(2,1)S(1)}, bf16[2,128,256]{2,1,0:T(8,128)(2,1)S(1)}, u32[]{:S(2)}, u32[]{:S(2)}) collective-permute-start(bf16[2,128,256]{2,1,0:T(8,128)(2,1)S(1)} %get-tuple-element.26), channel_id=1, source_target_pairs={{0,8},{1,25},{8,16},{9,1},{16,24},{17,9},{24,0},{25,17},{2,10},{3,... | collective-permute-start | bytes 393224 | tf_op jit(solution)/shard_map/ppermute | solution.py:258
  12.0 6.2 %collective-permute-start.13 = (bf16[2,128,256]{2,1,0:T(8,128)(2,1)S(1)}, bf16[2,128,256]{2,1,0:T(8,128)(2,1)S(1)}, u32[]{:S(2)}, u32[]{:S(2)}) collective-permute-start(bf16[2,128,256]{2,1,0:T(8,128)(2,1)S(1)} %collective-permute-done.12), channel_id=1, source_target_pairs={{0,32},{1,225},{32,64},{33,1},{64,96},{65,33},{96,128},{97,65},{12... | collective-permute-start | bytes 393224 | tf_op jit(solution)/shard_map/ppermute | solution.py:258
  12.1 7.1 %collective-permute-start.3 = (bf16[1,128,256]{2,1,0:T(8,128)(2,1)S(1)}, bf16[1,128,256]{2,1,0:T(8,128)(2,1)S(1)}, u32[]{:S(2)}, u32[]{:S(2)}) collective-permute-start(bf16[1,128,256]{2,1,0:T(8,128)(2,1)S(1)} %get-tuple-element.32), channel_id=1, source_target_pairs={{0,8},{1,25},{8,16},{9,1},{16,24},{17,9},{24,0},{25,17},{2,10},{3,... | collective-permute-start | bytes 196616 | tf_op jit(solution)/shard_map/ppermute | solution.py:258
  13.7 5.4 %collective-permute-start.2 = (bf16[1,128,256]{2,1,0:T(8,128)(2,1)S(1)}, bf16[1,128,256]{2,1,0:T(8,128)(2,1)S(1)}, u32[]{:S(2)}, u32[]{:S(2)}) collective-permute-start(bf16[1,128,256]{2,1,0:T(8,128)(2,1)S(1)} %get-tuple-element.31), channel_id=1, source_target_pairs={{0,1},{1,0},{2,3},{3,2},{4,5},{5,4},{6,7},{7,6},{8,9},{9,8},{10,11... | collective-permute-start | bytes 196616 | tf_op jit(solution)/shard_map/ppermute | solution.py:22
  18.2 6.3 %collective-permute-start.14 = (bf16[2,128,256]{2,1,0:T(8,128)(2,1)S(1)}, bf16[2,128,256]{2,1,0:T(8,128)(2,1)S(1)}, u32[]{:S(2)}, u32[]{:S(2)}) collective-permute-start(bf16[2,128,256]{2,1,0:T(8,128)(2,1)S(1)} %collective-permute-done.13), channel_id=1, source_target_pairs={{0,32},{1,225},{32,64},{33,1},{64,96},{65,33},{96,128},{97,65},{12... | collective-permute-start | bytes 393224 | tf_op jit(solution)/shard_map/ppermute | solution.py:258
  19.1 23.1 %copy-start.1 = (s32[1,1,224]{2,1,0:T(1,128)S(1)}, s32[1,1,224]{2,1,0:T(1,128)}, u32[]{:S(2)}) copy-start(s32[1,1,224]{2,1,0:T(1,128)} %param.8) | copy-start | bytes 2692
  19.2 23.1 %copy-start.2 = (s32[1,1,224]{2,1,0:T(1,128)S(1)}, s32[1,1,224]{2,1,0:T(1,128)}, u32[]{:S(2)}) copy-start(s32[1,1,224]{2,1,0:T(1,128)} %param.7) | copy-start | bytes 2692
  19.2 11.1 %collective-permute-start.8 = (bf16[4,128,256]{2,1,0:T(8,128)(2,1)S(1)}, bf16[4,128,256]{2,1,0:T(8,128)(2,1)S(1)}, u32[]{:S(2)}, u32[]{:S(2)}) collective-permute-start(bf16[4,128,256]{2,1,0:T(8,128)(2,1)S(1)} %pad_maximum_fusion.refs_2_), channel_id=1, source_target_pairs={{0,224},{32,0},{64,32},{96,64},{128,96},{160,128},{192,160},{224,1... | collective-permute-start | bytes 786440 | tf_op jit(solution)/shard_map/ppermute | solution.py:22
  22.5 7.6 %collective-permute-start.4 = (bf16[4,128,256]{2,1,0:T(8,128)(2,1)S(1)}, bf16[4,128,256]{2,1,0:T(8,128)(2,1)S(1)}, u32[]{:S(2)}, u32[]{:S(2)}) collective-permute-start(bf16[4,128,256]{2,1,0:T(8,128)(2,1)S(1)} %pad_maximum_fusion.refs_2_), channel_id=1, source_target_pairs={{0,32},{32,64},{64,96},{96,128},{128,160},{160,192},{192,224},{224... | collective-permute-start | bytes 786440 | tf_op jit(solution)/shard_map/ppermute | solution.py:22
  24.5 8.8 %collective-permute-start.15 = (bf16[3,128,256]{2,1,0:T(8,128)(2,1)S(1)}, bf16[3,128,256]{2,1,0:T(8,128)(2,1)S(1)}, u32[]{:S(2)}, u32[]{:S(2)}) collective-permute-start(bf16[3,128,256]{2,1,0:T(8,128)(2,1)S(1)} %pad_maximum_fusion.4), channel_id=1, source_target_pairs={{0,1},{1,0},{2,3},{3,2},{4,5},{5,4},{6,7},{7,6},{8,9},{9,8},{10,11... | collective-permute-start | bytes 589832 | tf_op jit(solution)/shard_map/ppermute | solution.py:22
  24.6 8.7 %collective-permute-start.16 = (bf16[1,128,256]{2,1,0:T(8,128)(2,1)S(1)}, bf16[1,128,256]{2,1,0:T(8,128)(2,1)S(1)}, u32[]{:S(2)}, u32[]{:S(2)}) collective-permute-start(bf16[1,128,256]{2,1,0:T(8,128)(2,1)S(1)} %get-tuple-element.27), channel_id=1, source_target_pairs={{0,32},{1,225},{32,64},{33,1},{64,96},{65,33},{96,128},{97,65},{12... | collective-permute-start | bytes 196616 | tf_op jit(solution)/shard_map/ppermute | solution.py:258
  30.1 11.5 %collective-permute-start.5 = (bf16[4,128,256]{2,1,0:T(8,128)(2,1)S(1)}, bf16[4,128,256]{2,1,0:T(8,128)(2,1)S(1)}, u32[]{:S(2)}, u32[]{:S(2)}) collective-permute-start(bf16[4,128,256]{2,1,0:T(8,128)(2,1)S(1)} %collective-permute-done.4.refs_3_), channel_id=1, source_target_pairs={{0,32},{32,64},{64,96},{96,128},{128,160},{160,192},{192,224},{224... | collective-permute-start | bytes 786440 | tf_op jit(solution)/shard_map/ppermute | solution.py:22
  30.3 7.5 %collective-permute-start.9 = (bf16[4,128,256]{2,1,0:T(8,128)(2,1)S(1)}, bf16[4,128,256]{2,1,0:T(8,128)(2,1)S(1)}, u32[]{:S(2)}, u32[]{:S(2)}) collective-permute-start(bf16[4,128,256]{2,1,0:T(8,128)(2,1)S(1)} %collective-permute-done.8.refs_4_), channel_id=1, source_target_pairs={{0,224},{32,0},{64,32},{96,64},{128,96},{160,128},{192,160},{224,1... | collective-permute-start | bytes 786440 | tf_op jit(solution)/shard_map/ppermute | solution.py:22
  33.4 17.1 %collective-permute-start.17 = (bf16[8,128,256]{2,1,0:T(8,128)(2,1)S(1)}, bf16[8,128,256]{2,1,0:T(8,128)(2,1)S(1)}, u32[]{:S(2)}, u32[]{:S(2)}) collective-permute-start(bf16[8,128,256]{2,1,0:T(8,128)(2,1)S(1)} %slice_dynamic-update-slice_fusion.refs_9_), channel_id=1, source_target_pairs={{0,8},{8,16},{16,24},{24,0},{1,9},{9,17},{17,25},{25,1},{2,10},{10... | collective-permute-start | bytes 1572872 | tf_op jit(solution)/shard_map/ppermute | solution.py:22
  35.1 17.1 %collective-permute-start.19 = (bf16[8,128,256]{2,1,0:T(8,128)(2,1)S(1)}, bf16[8,128,256]{2,1,0:T(8,128)(2,1)S(1)}, u32[]{:S(2)}, u32[]{:S(2)}) collective-permute-start(bf16[8,128,256]{2,1,0:T(8,128)(2,1)S(1)} %slice_dynamic-update-slice_fusion.refs_9_), channel_id=1, source_target_pairs={{0,24},{8,0},{16,8},{24,16},{1,25},{9,1},{17,9},{25,17},{2,26},{10... | collective-permute-start | bytes 1572872 | tf_op jit(solution)/shard_map/ppermute | solution.py:22
  37.9 8.7 %collective-permute-start.10 = (bf16[4,128,256]{2,1,0:T(8,128)(2,1)S(1)}, bf16[4,128,256]{2,1,0:T(8,128)(2,1)S(1)}, u32[]{:S(2)}, u32[]{:S(2)}) collective-permute-start(bf16[4,128,256]{2,1,0:T(8,128)(2,1)S(1)} %collective-permute-done.9.refs_6_), channel_id=1, source_target_pairs={{0,224},{32,0},{64,32},{96,64},{128,96},{160,128},{192,160},{224,1... | collective-permute-start | bytes 786440 | tf_op jit(solution)/shard_map/ppermute | solution.py:22
  41.6 8.8 %collective-permute-start.6 = (bf16[4,128,256]{2,1,0:T(8,128)(2,1)S(1)}, bf16[4,128,256]{2,1,0:T(8,128)(2,1)S(1)}, u32[]{:S(2)}, u32[]{:S(2)}) collective-permute-start(bf16[4,128,256]{2,1,0:T(8,128)(2,1)S(1)} %collective-permute-done.5.refs_5_), channel_id=1, source_target_pairs={{0,32},{32,64},{64,96},{96,128},{128,160},{160,192},{192,224},{224... | collective-permute-start | bytes 786440 | tf_op jit(solution)/shard_map/ppermute | solution.py:22
  46.6 12.9 %collective-permute-start.11 = (bf16[2,128,256]{2,1,0:T(8,128)(2,1)S(1)}, bf16[2,128,256]{2,1,0:T(8,128)(2,1)S(1)}, u32[]{:S(2)}, u32[]{:S(2)}) collective-permute-start(bf16[2,128,256]{2,1,0:T(8,128)(2,1)S(1)} %slice.145), channel_id=1, source_target_pairs={{0,224},{32,0},{64,32},{96,64},{128,96},{160,128},{192,160},{224,1... | collective-permute-start | bytes 393224 | tf_op jit(solution)/shard_map/ppermute | solution.py:22
  50.4 9.1 %collective-permute-start.7 = (bf16[2,128,256]{2,1,0:T(8,128)(2,1)S(1)}, bf16[2,128,256]{2,1,0:T(8,128)(2,1)S(1)}, u32[]{:S(2)}, u32[]{:S(2)}) collective-permute-start(bf16[2,128,256]{2,1,0:T(8,128)(2,1)S(1)} %slice.144), channel_id=1, source_target_pairs={{0,32},{32,64},{64,96},{96,128},{128,160},{160,192},{192,224},{224... | collective-permute-start | bytes 393224 | tf_op jit(solution)/shard_map/ppermute | solution.py:22
  50.5 9.0 %collective-permute-start.18 = (bf16[4,128,256]{2,1,0:T(8,128)(2,1)S(1)}, bf16[4,128,256]{2,1,0:T(8,128)(2,1)S(1)}, u32[]{:S(2)}, u32[]{:S(2)}) collective-permute-start(bf16[4,128,256]{2,1,0:T(8,128)(2,1)S(1)} %slice.153), channel_id=1, source_target_pairs={{0,8},{8,16},{16,24},{24,0},{1,9},{9,17},{17,25},{25,1},{2,10},{10... | collective-permute-start | bytes 786440 | tf_op jit(solution)/shard_map/ppermute | solution.py:22
  52.2 7.3 %collective-permute-start.20 = (bf16[4,128,256]{2,1,0:T(8,128)(2,1)S(1)}, bf16[4,128,256]{2,1,0:T(8,128)(2,1)S(1)}, u32[]{:S(2)}, u32[]{:S(2)}) collective-permute-start(bf16[4,128,256]{2,1,0:T(8,128)(2,1)S(1)} %slice.154), channel_id=1, source_target_pairs={{0,24},{8,0},{16,8},{24,16},{1,25},{9,1},{17,9},{25,17},{2,26},{10... | collective-permute-start | bytes 786440 | tf_op jit(solution)/shard_map/ppermute | solution.py:22
  62.0 2.8 %collective-permute-start.21 = (f32[1032,256]{1,0:T(8,128)S(1)}, f32[1032,256]{1,0:T(8,128)S(1)}, u32[]{:S(2)}, u32[]{:S(2)}) collective-permute-start(f32[1032,256]{1,0:T(8,128)S(1)} %get-tuple-element.16), channel_id=1, source_target_pairs={{0,1},{1,0},{2,3},{3,2},{4,5},{5,4},{6,7},{7,6},{8,9},{9,8},{10,11... | collective-permute-start | bytes 3170312 | tf_op jit(solution)/shard_map/ppermute | solution.py:22
  65.1 10.5 %copy-start = (f32[256]{0:T(256)S(1)}, f32[256]{0:T(256)}, u32[]{:S(2)}) copy-start(f32[256]{0:T(256)} %param.11) | copy-start | bytes 3076
  65.3 8.2 %collective-permute-start.22 = (f16[272,256]{1,0:T(8,128)(2,1)S(1)}, f16[272,256]{1,0:T(8,128)(2,1)S(1)}, u32[]{:S(2)}, u32[]{:S(2)}) collective-permute-start(f16[272,256]{1,0:T(8,128)(2,1)S(1)} %get-tuple-element.33), channel_id=1, source_target_pairs={{0,4},{2,6},{4,0},{6,2},{1,5},{3,7},{5,1},{7,3},{8,12},{10,14},{12... | collective-permute-start | bytes 417800 | tf_op jit(solution)/shard_map/ppermute | solution.py:22
  65.7 8.1 %collective-permute-start.23 = (f16[272,256]{1,0:T(8,128)(2,1)S(1)}, f16[272,256]{1,0:T(8,128)(2,1)S(1)}, u32[]{:S(2)}, u32[]{:S(2)}) collective-permute-start(f16[272,256]{1,0:T(8,128)(2,1)S(1)} %get-tuple-element.34), channel_id=1, source_target_pairs={{0,2},{2,4},{4,6},{6,0},{1,3},{3,5},{5,7},{7,1},{8,10},{10,12},{12... | collective-permute-start | bytes 417800 | tf_op jit(solution)/shard_map/ppermute | solution.py:22
  67.3 8.2 %collective-permute-start.24 = (f16[272,256]{1,0:T(8,128)(2,1)S(1)}, f16[272,256]{1,0:T(8,128)(2,1)S(1)}, u32[]{:S(2)}, u32[]{:S(2)}) collective-permute-start(f16[272,256]{1,0:T(8,128)(2,1)S(1)} %get-tuple-element.35), channel_id=1, source_target_pairs={{0,6},{2,0},{4,2},{6,4},{1,7},{3,1},{5,3},{7,5},{8,14},{10,8},{12,... | collective-permute-start | bytes 417800 | tf_op jit(solution)/shard_map/ppermute | solution.py:22
  89.7 1.3 collective-permute-start.25

commit v4 on v3

--- a/solution.py
+++ b/solution.py
@@ -287,7 +287,8 @@
 
     both = jnp.stack([omega, shift(omega, "core", 1)])
     block1, block2 = short_way(both[:, :half], "y"), short_way(both[:, half:], "z")
-    full1, forth1, back1 = ring(block1, "z", token)
+    full1, forth1, back1 = ring(block1, "z")
+    block2, token = lax.optimization_barrier((block2, token))
     full2, forth2, back2 = ring(block2, "y")
     end1, end2 = last(forth1, back1, "z"), last(forth2, back2, "y")
     early = [(full1[dz], (4 * dz, 4)) for dz in (0, 7, 1, 6, 2, 5, 3)]

time: 129 us -> 124 us (0.961)
  Pallas kernels: 23.2 us -> 21.4 us
  blocking collectives: 40.5 us -> 39.1 us
  starting transfers between devices: 32 us -> 30.6 us
    pallas_call x2, Pallas kernels: 7.98 us -> 6.19 us  [multiply(): pl.pallas_call(lambda *refs: multiply_kernel(*refs, places=places, first=...]
    ppermute x20, starting transfers between devices: 26.7 us -> 25.3 us  [shift(): lax.ppermute(value, axis, [(i, (i + step) % size) for i in range(size)])]
  transfers between devices with their start and end apart: 26 -> 26, of which waited for: 12 -> 13; matrix products, arithmetic and copies ran while one was open for 1% -> 1% of each run, Pallas kernels for 8% -> 7%
where the time goes in v4:
time: 124 us
  blocking collectives  39.1 us (32%)
  starting transfers between devices  30.6 us (25%)
  waiting for transfers between devices  28 us (23%)
  Pallas kernels  21.4 us (17%)
  between operations  1.68 us (1%)
  other arithmetic  1.59 us (1%)
    all_to_all x2, blocking collectives, spread(): return lax.all_to_all(copies, axes, 0, 0, tiled=True)  26.3 us
    ppermute x20, starting transfers between devices, shift(): lax.ppermute(value, axis, [(i, (i + step) % size) for i in range(size)])  25.3 us
    ppermute x20, waiting for transfers between devices, shift(): lax.ppermute(value, axis, [(i, (i + step) % size) for i in range(size)])  19.1 us
    all_to_all x1, blocking collectives, sum_over_all(): part = lax.all_to_all(pieces, ('y', 'x'), 0, 0, tiled=True).sum(0)  12.7 us
    pallas_call x1, Pallas kernels, orthonormalize(): pl.pallas_call(lambda *refs: factor_kernel(*refs, scale=math.sqrt(vertex_...  11 us
    ppermute x6, waiting for transfers between devices, split_shift(): return lax.ppermute(value, (axis, 'core'), pairs)  8.88 us
    pallas_call x2, Pallas kernels, multiply(): pl.pallas_call(lambda *refs: multiply_kernel(*refs, places=places, first=...  6.19 us
    ppermute x6, starting transfers between devices, split_shift(): return lax.ppermute(value, (axis, 'core'), pairs)  5.31 us
  transfers between devices with their start and end apart: 26, of which 13 were waited for; matrix products, arithmetic and copies ran while one was open for 1% of the time, Pallas kernels for 7%

profile of v4, /device:TPU:2, one launch (start us, length us, event | category | flops | bytes accessed | tf_op | source)
XLA Modules:
  0.0 124.1 jit_solution(3486838173157653036)
XLA Ops:
  0.6 0.1 collective-permute-start
  0.7 1.5 %collective-permute-done = bf16[256,256]{1,0:T(8,128)(2,1)S(1)} collective-permute-done((bf16[256,256]{1,0:T(8,128)(2,1)}, bf16[256,256]{1,0:T(8,128)(2,1)S(1)}, u32[]{:S(2)}, u32[]{:S(2)}) %collective-permute-start) | collective-permute-done | bytes 131104 | tf_op jit(solution)/shard_map/ppermute | solution.py:22
  2.3 0.9 pad_maximum_fusion.6
  3.2 2.0 %collective-permute-start.12 = (bf16[2,128,256]{2,1,0:T(8,128)(2,1)S(1)}, bf16[2,128,256]{2,1,0:T(8,128)(2,1)S(1)}, u32[]{:S(2)}, u32[]{:S(2)}) collective-permute-start(bf16[2,128,256]{2,1,0:T(8,128)(2,1)S(1)} %get-tuple-element.25), channel_id=1, source_target_pairs={{0,32},{1,225},{32,64},{33,1},{64,96},{65,33},{96,128},{97,65},{12... | collective-permute-start | bytes 393224 | tf_op jit(solution)/shard_map/ppermute | solution.py:258
  5.2 1.6 %collective-permute-start.1 = (bf16[2,128,256]{2,1,0:T(8,128)(2,1)S(1)}, bf16[2,128,256]{2,1,0:T(8,128)(2,1)S(1)}, u32[]{:S(2)}, u32[]{:S(2)}) collective-permute-start(bf16[2,128,256]{2,1,0:T(8,128)(2,1)S(1)} %get-tuple-element.26), channel_id=1, source_target_pairs={{0,8},{1,25},{8,16},{9,1},{16,24},{17,9},{24,0},{25,17},{2,10},{3,... | collective-permute-start | bytes 393224 | tf_op jit(solution)/shard_map/ppermute | solution.py:258
  6.7 5.3 %collective-permute-done.12 = bf16[2,128,256]{2,1,0:T(8,128)(2,1)S(1)} collective-permute-done((bf16[2,128,256]{2,1,0:T(8,128)(2,1)S(1)}, bf16[2,128,256]{2,1,0:T(8,128)(2,1)S(1)}, u32[]{:S(2)}, u32[]{:S(2)}) %collective-permute-start.12) | collective-permute-done | bytes 131104 | tf_op jit(solution)/shard_map/ppermute | solution.py:258
  12.1 1.7 %collective-permute-start.3 = (bf16[1,128,256]{2,1,0:T(8,128)(2,1)S(1)}, bf16[1,128,256]{2,1,0:T(8,128)(2,1)S(1)}, u32[]{:S(2)}, u32[]{:S(2)}) collective-permute-start(bf16[1,128,256]{2,1,0:T(8,128)(2,1)S(1)} %get-tuple-element.32), channel_id=1, source_target_pairs={{0,8},{1,25},{8,16},{9,1},{16,24},{17,9},{24,0},{25,17},{2,10},{3,... | collective-permute-start | bytes 196616 | tf_op jit(solution)/shard_map/ppermute | solution.py:258
  13.7 3.1 %collective-permute-start.2 = (bf16[1,128,256]{2,1,0:T(8,128)(2,1)S(1)}, bf16[1,128,256]{2,1,0:T(8,128)(2,1)S(1)}, u32[]{:S(2)}, u32[]{:S(2)}) collective-permute-start(bf16[1,128,256]{2,1,0:T(8,128)(2,1)S(1)} %get-tuple-element.31), channel_id=1, source_target_pairs={{0,1},{1,0},{2,3},{3,2},{4,5},{5,4},{6,7},{7,6},{8,9},{9,8},{10,11... | collective-permute-start | bytes 196616 | tf_op jit(solution)/shard_map/ppermute | solution.py:22
  16.8 1.4 %collective-permute-done.13 = bf16[2,128,256]{2,1,0:T(8,128)(2,1)S(1)} collective-permute-done((bf16[2,128,256]{2,1,0:T(8,128)(2,1)S(1)}, bf16[2,128,256]{2,1,0:T(8,128)(2,1)S(1)}, u32[]{:S(2)}, u32[]{:S(2)}) %collective-permute-start.13) | collective-permute-done | bytes 131104 | tf_op jit(solution)/shard_map/ppermute | solution.py:258
  18.2 0.9 slice_dynamic-update-slice_fusion.2
  19.2 3.3 %collective-permute-start.8 = (bf16[4,128,256]{2,1,0:T(8,128)(2,1)S(1)}, bf16[4,128,256]{2,1,0:T(8,128)(2,1)S(1)}, u32[]{:S(2)}, u32[]{:S(2)}) collective-permute-start(bf16[4,128,256]{2,1,0:T(8,128)(2,1)S(1)} %pad_maximum_fusion.refs_2_), channel_id=1, source_target_pairs={{0,224},{32,0},{64,32},{96,64},{128,96},{160,128},{192,160},{224,1... | collective-permute-start | bytes 786440 | tf_op jit(solution)/shard_map/ppermute | solution.py:22
  22.5 1.9 %collective-permute-done.14 = bf16[2,128,256]{2,1,0:T(8,128)(2,1)S(1)} collective-permute-done((bf16[2,128,256]{2,1,0:T(8,128)(2,1)S(1)}, bf16[2,128,256]{2,1,0:T(8,128)(2,1)S(1)}, u32[]{:S(2)}, u32[]{:S(2)}) %collective-permute-start.14) | collective-permute-done | bytes 131104 | tf_op jit(solution)/shard_map/ppermute | solution.py:258
  24.5 0.1 collective-permute-start.15
  24.6 0.1 collective-permute-start.16
  24.7 3.6 %collective-permute-done.8.refs_4_ = bf16[4,128,256]{2,1,0:T(8,128)(2,1)S(1)} collective-permute-done((bf16[4,128,256]{2,1,0:T(8,128)(2,1)S(1)}, bf16[4,128,256]{2,1,0:T(8,128)(2,1)S(1)}, u32[]{:S(2)}, u32[]{:S(2)}) %collective-permute-start.8) | collective-permute-done | bytes 262176 | tf_op jit(solution)/shard_map/ppermute | solution.py:22
  28.4 2.2 %collective-permute-start.9 = (bf16[4,128,256]{2,1,0:T(8,128)(2,1)S(1)}, bf16[4,128,256]{2,1,0:T(8,128)(2,1)S(1)}, u32[]{:S(2)}, u32[]{:S(2)}) collective-permute-start(bf16[4,128,256]{2,1,0:T(8,128)(2,1)S(1)} %collective-permute-done.8.refs_4_), channel_id=1, source_target_pairs={{0,224},{32,0},{64,32},{96,64},{128,96},{160,128},{192,160},{224,1... | collective-permute-start | bytes 786440 | tf_op jit(solution)/shard_map/ppermute | solution.py:22
  30.6 0.2 collective-permute-done.16
  30.9 1.7 %collective-permute-start.17 = (bf16[8,128,256]{2,1,0:T(8,128)(2,1)S(1)}, bf16[8,128,256]{2,1,0:T(8,128)(2,1)S(1)}, u32[]{:S(2)}, u32[]{:S(2)}) collective-permute-start(bf16[8,128,256]{2,1,0:T(8,128)(2,1)S(1)} %slice_dynamic-update-slice_fusion.refs_9_), channel_id=1, source_target_pairs={{0,8},{8,16},{16,24},{24,0},{1,9},{9,17},{17,25},{25,1},{2,10},{10... | collective-permute-start | bytes 1572872 | tf_op jit(solution)/shard_map/ppermute | solution.py:22
  32.5 1.7 %collective-permute-start.19 = (bf16[8,128,256]{2,1,0:T(8,128)(2,1)S(1)}, bf16[8,128,256]{2,1,0:T(8,128)(2,1)S(1)}, u32[]{:S(2)}, u32[]{:S(2)}) collective-permute-start(bf16[8,128,256]{2,1,0:T(8,128)(2,1)S(1)} %slice_dynamic-update-slice_fusion.refs_9_), channel_id=1, source_target_pairs={{0,24},{8,0},{16,8},{24,16},{1,25},{9,1},{17,9},{25,17},{2,26},{10... | collective-permute-start | bytes 1572872 | tf_op jit(solution)/shard_map/ppermute | solution.py:22
  34.2 2.6 %collective-permute-done.9.refs_6_ = bf16[4,128,256]{2,1,0:T(8,128)(2,1)S(1)} collective-permute-done((bf16[4,128,256]{2,1,0:T(8,128)(2,1)S(1)}, bf16[4,128,256]{2,1,0:T(8,128)(2,1)S(1)}, u32[]{:S(2)}, u32[]{:S(2)}) %collective-permute-start.9) | collective-permute-done | bytes 262176 | tf_op jit(solution)/shard_map/ppermute | solution.py:22
  36.8 1.5 %collective-permute-start.10 = (bf16[4,128,256]{2,1,0:T(8,128)(2,1)S(1)}, bf16[4,128,256]{2,1,0:T(8,128)(2,1)S(1)}, u32[]{:S(2)}, u32[]{:S(2)}) collective-permute-start(bf16[4,128,256]{2,1,0:T(8,128)(2,1)S(1)} %collective-permute-done.9.refs_6_), channel_id=1, source_target_pairs={{0,224},{32,0},{64,32},{96,64},{128,96},{160,128},{192,160},{224,1... | collective-permute-start | bytes 786440 | tf_op jit(solution)/shard_map/ppermute | solution.py:22
  38.3 0.5 collective-permute-start.6
  39.6 4.3 %prepare.1 = (bf16[224,128,128]{2,1,0:T(8,128)(2,1)S(1)}, s32[256]{0:T(256)S(1)}, s32[256]{0:T(256)S(1)}, s32[2]{0:T(128)S(1)}, bf16[16,128]{1,0:T(8,128)(2,1)}) custom-call(s32[224]{0:T(256)S(1)} %fusion.10.entries_ref, bf16[224,128,128]{2,1,0:T(8,128)(2,1)} %bitcast.16), custom_call_target="tpu_custom_call" | custom-call | bytes 29360128 | tf_op jit(solution)/shard_map/prepare/pallas_call | solution.py:95
  43.8 0.6 collective-permute-done.10.refs_8_
  44.4 2.2 %collective-permute-start.11 = (bf16[2,128,256]{2,1,0:T(8,128)(2,1)S(1)}, bf16[2,128,256]{2,1,0:T(8,128)(2,1)S(1)}, u32[]{:S(2)}, u32[]{:S(2)}) collective-permute-start(bf16[2,128,256]{2,1,0:T(8,128)(2,1)S(1)} %slice.145), channel_id=1, source_target_pairs={{0,224},{32,0},{64,32},{96,64},{128,96},{160,128},{192,160},{224,1... | collective-permute-start | bytes 393224 | tf_op jit(solution)/shard_map/ppermute | solution.py:22
  46.8 1.3 %collective-permute-start.18 = (bf16[4,128,256]{2,1,0:T(8,128)(2,1)S(1)}, bf16[4,128,256]{2,1,0:T(8,128)(2,1)S(1)}, u32[]{:S(2)}, u32[]{:S(2)}) collective-permute-start(bf16[4,128,256]{2,1,0:T(8,128)(2,1)S(1)} %slice.153), channel_id=1, source_target_pairs={{0,8},{8,16},{16,24},{24,0},{1,9},{9,17},{17,25},{25,1},{2,10},{10... | collective-permute-start | bytes 786440 | tf_op jit(solution)/shard_map/ppermute | solution.py:22
  48.1 2.1 %collective-permute-start.20 = (bf16[4,128,256]{2,1,0:T(8,128)(2,1)S(1)}, bf16[4,128,256]{2,1,0:T(8,128)(2,1)S(1)}, u32[]{:S(2)}, u32[]{:S(2)}) collective-permute-start(bf16[4,128,256]{2,1,0:T(8,128)(2,1)S(1)} %slice.154), channel_id=1, source_target_pairs={{0,24},{8,0},{16,8},{24,16},{1,25},{9,1},{17,9},{25,17},{2,26},{10... | collective-permute-start | bytes 786440 | tf_op jit(solution)/shard_map/ppermute | solution.py:22
  50.2 4.2 %multiply_first.1.refs_7_ = f32[2176,256]{1,0:T(8,128)S(1)} custom-call(s32[256]{0:T(256)S(1)} %get-tuple-element.14.refs_0_, s32[2]{0:T(128)S(1)} %get-tuple-element.12.refs_1_, bf16[4,128,256]{2,1,0:T(8,128)(2,1)S(1)} %pad_maximum_fusion.refs_2_, bf16[4,128,256]{2,1,0:T(8,128)(2,1)S(1)} %collective-permute-done.4.refs_3_, ...), custom_call_target="tpu_custom_call" | custom-call | flops 6000000000 | tf_op jit(solution)/shard_map/multiply_first/pallas_call | solution.py:125
  54.4 0.1 collective-permute-done.20.refs_5_
  54.6 2.0 %multiply_rest.1 = (f32[1032,256]{1,0:T(8,128)S(1)}, f32[1024,256]{1,0:T(8,128)S(1)}, f32[8,256]{1,0:T(8,128)S(1)}) custom-call(s32[256]{0:T(256)S(1)} %get-tuple-element.11.refs_0_, s32[2]{0:T(128)S(1)} %get-tuple-element.12.refs_1_, bf16[2,128,256]{2,1,0:T(8,128)(2,1)S(1)} %collective-permute-done.7.refs_2_, ...), custom_call_target="tpu_custom_call" | custom-call | flops 1000000000 | tf_op jit(solution)/shard_map/multiply_rest/pallas_call | solution.py:125
  56.6 0.1 collective-permute-start.21
  56.7 2.7 %collective-permute-done.21 = f32[1032,256]{1,0:T(8,128)S(1)} collective-permute-done((f32[1032,256]{1,0:T(8,128)S(1)}, f32[1032,256]{1,0:T(8,128)S(1)}, u32[]{:S(2)}, u32[]{:S(2)}) %collective-permute-start.21) | collective-permute-done | bytes 1056800 | tf_op jit(solution)/shard_map/ppermute | solution.py:22
  59.4 0.1 slice_add_fusion
  59.5 0.1 fusion
  59.7 0.1 pad_maximum_fusion.3
  59.8 2.2 %collective-permute-start.22 = (f16[272,256]{1,0:T(8,128)(2,1)S(1)}, f16[272,256]{1,0:T(8,128)(2,1)S(1)}, u32[]{:S(2)}, u32[]{:S(2)}) collective-permute-start(f16[272,256]{1,0:T(8,128)(2,1)S(1)} %get-tuple-element.33), channel_id=1, source_target_pairs={{0,4},{2,6},{4,0},{6,2},{1,5},{3,7},{5,1},{7,3},{8,12},{10,14},{12... | collective-permute-start | bytes 417800 | tf_op jit(solution)/shard_map/ppermute | solution.py:22
  62.1 1.5 %collective-permute-start.23 = (f16[272,256]{1,0:T(8,128)(2,1)S(1)}, f16[272,256]{1,0:T(8,128)(2,1)S(1)}, u32[]{:S(2)}, u32[]{:S(2)}) collective-permute-start(f16[272,256]{1,0:T(8,128)(2,1)S(1)} %get-tuple-element.34), channel_id=1, source_target_pairs={{0,2},{2,4},{4,6},{6,0},{1,3},{3,5},{5,7},{7,1},{8,10},{10,12},{12... | collective-permute-start | bytes 417800 | tf_op jit(solution)/shard_map/ppermute | solution.py:22
  63.6 1.6 %collective-permute-start.24 = (f16[272,256]{1,0:T(8,128)(2,1)S(1)}, f16[272,256]{1,0:T(8,128)(2,1)S(1)}, u32[]{:S(2)}, u32[]{:S(2)}) collective-permute-start(f16[272,256]{1,0:T(8,128)(2,1)S(1)} %get-tuple-element.35), channel_id=1, source_target_pairs={{0,6},{2,0},{4,2},{6,4},{1,7},{3,1},{5,3},{7,5},{8,14},{10,8},{12,... | collective-permute-start | bytes 417800 | tf_op jit(solution)/shard_map/ppermute | solution.py:22
  65.1 2.1 %collective-permute-done.22 = f16[272,256]{1,0:T(8,128)(2,1)S(1)} collective-permute-done((f16[272,256]{1,0:T(8,128)(2,1)S(1)}, f16[272,256]{1,0:T(8,128)(2,1)S(1)}, u32[]{:S(2)}, u32[]{:S(2)}) %collective-permute-start.22) | collective-permute-done | bytes 139296 | tf_op jit(solution)/shard_map/ppermute | solution.py:22
  67.3 4.6 %collective-permute-done.23 = f16[272,256]{1,0:T(8,128)(2,1)S(1)} collective-permute-done((f16[272,256]{1,0:T(8,128)(2,1)S(1)}, f16[272,256]{1,0:T(8,128)(2,1)S(1)}, u32[]{:S(2)}, u32[]{:S(2)}) %collective-permute-start.23) | collective-permute-done | bytes 139296 | tf_op jit(solution)/shard_map/ppermute | solution.py:22
  72.0 0.1 fusion.2.refs_1_
  72.1 0.6 fusion.24
  72.7 12.7 %all_to_all.15 = f32[16,24,128]{2,1,0:T(8,128)S(1)} all-to-all(f32[16,24,128]{2,1,0:T(8,128)S(1)} %bitcast.17), channel_id=1, replica_groups=mesh['z'=8,'y'=4,'x'=4,'core'=2] {'y','x'}, dimensions={0} | all-to-all | bytes 393216 | tf_op jit(solution)/shard_map/all_to_all | solution.py:247
  85.5 0.1 collective-permute-start.25
  85.6 1.2 collective-permute-done.25
  86.8 15.0 %all_to_all.16 = f32[8,24,128]{2,1,0:T(8,128)S(1)} all-to-all(f32[8,24,128]{2,1,0:T(8,128)S(1)} %broadcast_in_dim.31), channel_id=1, replica_groups=mesh['z'=8,'y'=4,'x'=4,'core'=2] {'z'}, dimensions={0} | all-to-all | bytes 196608 | tf_op jit(solution)/shard_map/all_to_all | solution.py:240
  101.8 11.3 %all_to_all.17 = f32[16,24,128]{2,1,0:T(8,128)S(1)} all-to-all(f32[16,24,128]{2,1,0:T(8,128)S(1)} %broadcast_in_dim.32), channel_id=1, replica_groups=mesh['z'=8,'y'=4,'x'=4,'core'=2] {'y','x'}, dimensions={0} | all-to-all | bytes 393216 | tf_op jit(solution)/shard_map/all_to_all | solution.py:240
  113.2 11.0 %orthonormalize.1 = (f32[256,256]{1,0:T(8,128)}, f32[256,256]{1,0:T(8,128)}) custom-call(f32[384,128]{1,0:T(8,128)S(1)} %bitcast.15, f32[256,256]{1,0:T(8,128)S(1)} %fusion.2.refs_1_), custom_call_target="tpu_custom_call" | custom-call | tf_op jit(solution)/shard_map/orthonormalize/pallas_call | solution.py:227
  (58 shorter events, 0.7 us)
Async XLA Ops:
  0.6 1.6 %collective-permute-start = (bf16[256,256]{1,0:T(8,128)(2,1)}, bf16[256,256]{1,0:T(8,128)(2,1)S(1)}, u32[]{:S(2)}, u32[]{:S(2)}) collective-permute-start(bf16[256,256]{1,0:T(8,128)(2,1)} %param.10), channel_id=1, source_target_pairs={{0,1},{1,0},{2,3},{3,2},{4,5},{5,4},{6,7},{7,6},{8,9},{9,8},{10,11... | collective-permute-start | bytes 393224 | tf_op jit(solution)/shard_map/ppermute | solution.py:22
  3.2 8.9 %collective-permute-start.12 = (bf16[2,128,256]{2,1,0:T(8,128)(2,1)S(1)}, bf16[2,128,256]{2,1,0:T(8,128)(2,1)S(1)}, u32[]{:S(2)}, u32[]{:S(2)}) collective-permute-start(bf16[2,128,256]{2,1,0:T(8,128)(2,1)S(1)} %get-tuple-element.25), channel_id=1, source_target_pairs={{0,32},{1,225},{32,64},{33,1},{64,96},{65,33},{96,128},{97,65},{12... | collective-permute-start | bytes 393224 | tf_op jit(solution)/shard_map/ppermute | solution.py:258
  5.2 6.9 %collective-permute-start.1 = (bf16[2,128,256]{2,1,0:T(8,128)(2,1)S(1)}, bf16[2,128,256]{2,1,0:T(8,128)(2,1)S(1)}, u32[]{:S(2)}, u32[]{:S(2)}) collective-permute-start(bf16[2,128,256]{2,1,0:T(8,128)(2,1)S(1)} %get-tuple-element.26), channel_id=1, source_target_pairs={{0,8},{1,25},{8,16},{9,1},{16,24},{17,9},{24,0},{25,17},{2,10},{3,... | collective-permute-start | bytes 393224 | tf_op jit(solution)/shard_map/ppermute | solution.py:258
  12.0 6.2 %collective-permute-start.13 = (bf16[2,128,256]{2,1,0:T(8,128)(2,1)S(1)}, bf16[2,128,256]{2,1,0:T(8,128)(2,1)S(1)}, u32[]{:S(2)}, u32[]{:S(2)}) collective-permute-start(bf16[2,128,256]{2,1,0:T(8,128)(2,1)S(1)} %collective-permute-done.12), channel_id=1, source_target_pairs={{0,32},{1,225},{32,64},{33,1},{64,96},{65,33},{96,128},{97,65},{12... | collective-permute-start | bytes 393224 | tf_op jit(solution)/shard_map/ppermute | solution.py:258
  12.1 7.1 %collective-permute-start.3 = (bf16[1,128,256]{2,1,0:T(8,128)(2,1)S(1)}, bf16[1,128,256]{2,1,0:T(8,128)(2,1)S(1)}, u32[]{:S(2)}, u32[]{:S(2)}) collective-permute-start(bf16[1,128,256]{2,1,0:T(8,128)(2,1)S(1)} %get-tuple-element.32), channel_id=1, source_target_pairs={{0,8},{1,25},{8,16},{9,1},{16,24},{17,9},{24,0},{25,17},{2,10},{3,... | collective-permute-start | bytes 196616 | tf_op jit(solution)/shard_map/ppermute | solution.py:258
  13.7 5.4 %collective-permute-start.2 = (bf16[1,128,256]{2,1,0:T(8,128)(2,1)S(1)}, bf16[1,128,256]{2,1,0:T(8,128)(2,1)S(1)}, u32[]{:S(2)}, u32[]{:S(2)}) collective-permute-start(bf16[1,128,256]{2,1,0:T(8,128)(2,1)S(1)} %get-tuple-element.31), channel_id=1, source_target_pairs={{0,1},{1,0},{2,3},{3,2},{4,5},{5,4},{6,7},{7,6},{8,9},{9,8},{10,11... | collective-permute-start | bytes 196616 | tf_op jit(solution)/shard_map/ppermute | solution.py:22
  18.2 6.3 %collective-permute-start.14 = (bf16[2,128,256]{2,1,0:T(8,128)(2,1)S(1)}, bf16[2,128,256]{2,1,0:T(8,128)(2,1)S(1)}, u32[]{:S(2)}, u32[]{:S(2)}) collective-permute-start(bf16[2,128,256]{2,1,0:T(8,128)(2,1)S(1)} %collective-permute-done.13), channel_id=1, source_target_pairs={{0,32},{1,225},{32,64},{33,1},{64,96},{65,33},{96,128},{97,65},{12... | collective-permute-start | bytes 393224 | tf_op jit(solution)/shard_map/ppermute | solution.py:258
  19.1 20.3 %copy-start.1 = (s32[1,1,224]{2,1,0:T(1,128)S(1)}, s32[1,1,224]{2,1,0:T(1,128)}, u32[]{:S(2)}) copy-start(s32[1,1,224]{2,1,0:T(1,128)} %param.8) | copy-start | bytes 2692
  19.2 20.3 %copy-start.2 = (s32[1,1,224]{2,1,0:T(1,128)S(1)}, s32[1,1,224]{2,1,0:T(1,128)}, u32[]{:S(2)}) copy-start(s32[1,1,224]{2,1,0:T(1,128)} %param.7) | copy-start | bytes 2692
  19.2 9.1 %collective-permute-start.8 = (bf16[4,128,256]{2,1,0:T(8,128)(2,1)S(1)}, bf16[4,128,256]{2,1,0:T(8,128)(2,1)S(1)}, u32[]{:S(2)}, u32[]{:S(2)}) collective-permute-start(bf16[4,128,256]{2,1,0:T(8,128)(2,1)S(1)} %pad_maximum_fusion.refs_2_), channel_id=1, source_target_pairs={{0,224},{32,0},{64,32},{96,64},{128,96},{160,128},{192,160},{224,1... | collective-permute-start | bytes 786440 | tf_op jit(solution)/shard_map/ppermute | solution.py:22
  22.5 8.0 %collective-permute-start.4 = (bf16[4,128,256]{2,1,0:T(8,128)(2,1)S(1)}, bf16[4,128,256]{2,1,0:T(8,128)(2,1)S(1)}, u32[]{:S(2)}, u32[]{:S(2)}) collective-permute-start(bf16[4,128,256]{2,1,0:T(8,128)(2,1)S(1)} %pad_maximum_fusion.refs_2_), channel_id=1, source_target_pairs={{0,32},{32,64},{64,96},{96,128},{128,160},{160,192},{192,224},{224... | collective-permute-start | bytes 786440 | tf_op jit(solution)/shard_map/ppermute | solution.py:22
  24.5 6.0 %collective-permute-start.15 = (bf16[3,128,256]{2,1,0:T(8,128)(2,1)S(1)}, bf16[3,128,256]{2,1,0:T(8,128)(2,1)S(1)}, u32[]{:S(2)}, u32[]{:S(2)}) collective-permute-start(bf16[3,128,256]{2,1,0:T(8,128)(2,1)S(1)} %pad_maximum_fusion.4), channel_id=1, source_target_pairs={{0,1},{1,0},{2,3},{3,2},{4,5},{5,4},{6,7},{7,6},{8,9},{9,8},{10,11... | collective-permute-start | bytes 589832 | tf_op jit(solution)/shard_map/ppermute | solution.py:22
  24.6 6.2 %collective-permute-start.16 = (bf16[1,128,256]{2,1,0:T(8,128)(2,1)S(1)}, bf16[1,128,256]{2,1,0:T(8,128)(2,1)S(1)}, u32[]{:S(2)}, u32[]{:S(2)}) collective-permute-start(bf16[1,128,256]{2,1,0:T(8,128)(2,1)S(1)} %get-tuple-element.27), channel_id=1, source_target_pairs={{0,32},{1,225},{32,64},{33,1},{64,96},{65,33},{96,128},{97,65},{12... | collective-permute-start | bytes 196616 | tf_op jit(solution)/shard_map/ppermute | solution.py:258
  28.4 8.4 %collective-permute-start.9 = (bf16[4,128,256]{2,1,0:T(8,128)(2,1)S(1)}, bf16[4,128,256]{2,1,0:T(8,128)(2,1)S(1)}, u32[]{:S(2)}, u32[]{:S(2)}) collective-permute-start(bf16[4,128,256]{2,1,0:T(8,128)(2,1)S(1)} %collective-permute-done.8.refs_4_), channel_id=1, source_target_pairs={{0,224},{32,0},{64,32},{96,64},{128,96},{160,128},{192,160},{224,1... | collective-permute-start | bytes 786440 | tf_op jit(solution)/shard_map/ppermute | solution.py:22
  30.6 7.7 %collective-permute-start.5 = (bf16[4,128,256]{2,1,0:T(8,128)(2,1)S(1)}, bf16[4,128,256]{2,1,0:T(8,128)(2,1)S(1)}, u32[]{:S(2)}, u32[]{:S(2)}) collective-permute-start(bf16[4,128,256]{2,1,0:T(8,128)(2,1)S(1)} %collective-permute-done.4.refs_3_), channel_id=1, source_target_pairs={{0,32},{32,64},{64,96},{96,128},{128,160},{160,192},{192,224},{224... | collective-permute-start | bytes 786440 | tf_op jit(solution)/shard_map/ppermute | solution.py:22
  30.9 15.9 %collective-permute-start.17 = (bf16[8,128,256]{2,1,0:T(8,128)(2,1)S(1)}, bf16[8,128,256]{2,1,0:T(8,128)(2,1)S(1)}, u32[]{:S(2)}, u32[]{:S(2)}) collective-permute-start(bf16[8,128,256]{2,1,0:T(8,128)(2,1)S(1)} %slice_dynamic-update-slice_fusion.refs_9_), channel_id=1, source_target_pairs={{0,8},{8,16},{16,24},{24,0},{1,9},{9,17},{17,25},{25,1},{2,10},{10... | collective-permute-start | bytes 1572872 | tf_op jit(solution)/shard_map/ppermute | solution.py:22
  32.5 15.6 %collective-permute-start.19 = (bf16[8,128,256]{2,1,0:T(8,128)(2,1)S(1)}, bf16[8,128,256]{2,1,0:T(8,128)(2,1)S(1)}, u32[]{:S(2)}, u32[]{:S(2)}) collective-permute-start(bf16[8,128,256]{2,1,0:T(8,128)(2,1)S(1)} %slice_dynamic-update-slice_fusion.refs_9_), channel_id=1, source_target_pairs={{0,24},{8,0},{16,8},{24,16},{1,25},{9,1},{17,9},{25,17},{2,26},{10... | collective-permute-start | bytes 1572872 | tf_op jit(solution)/shard_map/ppermute | solution.py:22
  36.8 7.6 %collective-permute-start.10 = (bf16[4,128,256]{2,1,0:T(8,128)(2,1)S(1)}, bf16[4,128,256]{2,1,0:T(8,128)(2,1)S(1)}, u32[]{:S(2)}, u32[]{:S(2)}) collective-permute-start(bf16[4,128,256]{2,1,0:T(8,128)(2,1)S(1)} %collective-permute-done.9.refs_6_), channel_id=1, source_target_pairs={{0,224},{32,0},{64,32},{96,64},{128,96},{160,128},{192,160},{224,1... | collective-permute-start | bytes 786440 | tf_op jit(solution)/shard_map/ppermute | solution.py:22
  38.3 8.3 %collective-permute-start.6 = (bf16[4,128,256]{2,1,0:T(8,128)(2,1)S(1)}, bf16[4,128,256]{2,1,0:T(8,128)(2,1)S(1)}, u32[]{:S(2)}, u32[]{:S(2)}) collective-permute-start(bf16[4,128,256]{2,1,0:T(8,128)(2,1)S(1)} %collective-permute-done.5.refs_5_), channel_id=1, source_target_pairs={{0,32},{32,64},{64,96},{96,128},{128,160},{160,192},{192,224},{224... | collective-permute-start | bytes 786440 | tf_op jit(solution)/shard_map/ppermute | solution.py:22
  44.4 9.9 %collective-permute-start.11 = (bf16[2,128,256]{2,1,0:T(8,128)(2,1)S(1)}, bf16[2,128,256]{2,1,0:T(8,128)(2,1)S(1)}, u32[]{:S(2)}, u32[]{:S(2)}) collective-permute-start(bf16[2,128,256]{2,1,0:T(8,128)(2,1)S(1)} %slice.145), channel_id=1, source_target_pairs={{0,224},{32,0},{64,32},{96,64},{128,96},{160,128},{192,160},{224,1... | collective-permute-start | bytes 393224 | tf_op jit(solution)/shard_map/ppermute | solution.py:22
  46.7 7.7 %collective-permute-start.7 = (bf16[2,128,256]{2,1,0:T(8,128)(2,1)S(1)}, bf16[2,128,256]{2,1,0:T(8,128)(2,1)S(1)}, u32[]{:S(2)}, u32[]{:S(2)}) collective-permute-start(bf16[2,128,256]{2,1,0:T(8,128)(2,1)S(1)} %slice.144), channel_id=1, source_target_pairs={{0,32},{32,64},{64,96},{96,128},{128,160},{160,192},{192,224},{224... | collective-permute-start | bytes 393224 | tf_op jit(solution)/shard_map/ppermute | solution.py:22
  46.8 7.7 %collective-permute-start.18 = (bf16[4,128,256]{2,1,0:T(8,128)(2,1)S(1)}, bf16[4,128,256]{2,1,0:T(8,128)(2,1)S(1)}, u32[]{:S(2)}, u32[]{:S(2)}) collective-permute-start(bf16[4,128,256]{2,1,0:T(8,128)(2,1)S(1)} %slice.153), channel_id=1, source_target_pairs={{0,8},{8,16},{16,24},{24,0},{1,9},{9,17},{17,25},{25,1},{2,10},{10... | collective-permute-start | bytes 786440 | tf_op jit(solution)/shard_map/ppermute | solution.py:22
  48.1 6.4 %collective-permute-start.20 = (bf16[4,128,256]{2,1,0:T(8,128)(2,1)S(1)}, bf16[4,128,256]{2,1,0:T(8,128)(2,1)S(1)}, u32[]{:S(2)}, u32[]{:S(2)}) collective-permute-start(bf16[4,128,256]{2,1,0:T(8,128)(2,1)S(1)} %slice.154), channel_id=1, source_target_pairs={{0,24},{8,0},{16,8},{24,16},{1,25},{9,1},{17,9},{25,17},{2,26},{10... | collective-permute-start | bytes 786440 | tf_op jit(solution)/shard_map/ppermute | solution.py:22
  56.6 2.8 %collective-permute-start.21 = (f32[1032,256]{1,0:T(8,128)S(1)}, f32[1032,256]{1,0:T(8,128)S(1)}, u32[]{:S(2)}, u32[]{:S(2)}) collective-permute-start(f32[1032,256]{1,0:T(8,128)S(1)} %get-tuple-element.16), channel_id=1, source_target_pairs={{0,1},{1,0},{2,3},{3,2},{4,5},{5,4},{6,7},{7,6},{8,9},{9,8},{10,11... | collective-permute-start | bytes 3170312 | tf_op jit(solution)/shard_map/ppermute | solution.py:22
  59.7 12.3 %copy-start = (f32[256]{0:T(256)S(1)}, f32[256]{0:T(256)}, u32[]{:S(2)}) copy-start(f32[256]{0:T(256)} %param.11) | copy-start | bytes 3076
  59.8 7.4 %collective-permute-start.22 = (f16[272,256]{1,0:T(8,128)(2,1)S(1)}, f16[272,256]{1,0:T(8,128)(2,1)S(1)}, u32[]{:S(2)}, u32[]{:S(2)}) collective-permute-start(f16[272,256]{1,0:T(8,128)(2,1)S(1)} %get-tuple-element.33), channel_id=1, source_target_pairs={{0,4},{2,6},{4,0},{6,2},{1,5},{3,7},{5,1},{7,3},{8,12},{10,14},{12... | collective-permute-start | bytes 417800 | tf_op jit(solution)/shard_map/ppermute | solution.py:22
  62.1 9.8 %collective-permute-start.23 = (f16[272,256]{1,0:T(8,128)(2,1)S(1)}, f16[272,256]{1,0:T(8,128)(2,1)S(1)}, u32[]{:S(2)}, u32[]{:S(2)}) collective-permute-start(f16[272,256]{1,0:T(8,128)(2,1)S(1)} %get-tuple-element.34), channel_id=1, source_target_pairs={{0,2},{2,4},{4,6},{6,0},{1,3},{3,5},{5,7},{7,1},{8,10},{10,12},{12... | collective-permute-start | bytes 417800 | tf_op jit(solution)/shard_map/ppermute | solution.py:22
  63.6 8.3 %collective-permute-start.24 = (f16[272,256]{1,0:T(8,128)(2,1)S(1)}, f16[272,256]{1,0:T(8,128)(2,1)S(1)}, u32[]{:S(2)}, u32[]{:S(2)}) collective-permute-start(f16[272,256]{1,0:T(8,128)(2,1)S(1)} %get-tuple-element.35), channel_id=1, source_target_pairs={{0,6},{2,0},{4,2},{6,4},{1,7},{3,1},{5,3},{7,5},{8,14},{10,8},{12,... | collective-permute-start | bytes 417800 | tf_op jit(solution)/shard_map/ppermute | solution.py:22
  85.5 1.3 %collective-permute-start.25 = (f32[24,128]{1,0:T(8,128)S(1)}, f32[24,128]{1,0:T(8,128)S(1)}, u32[]{:S(2)}, u32[]{:S(2)}) collective-permute-start(f32[24,128]{1,0:T(8,128)S(1)} %reduce_sum.18), channel_id=1, source_target_pairs={{0,1},{1,0},{2,3},{3,2},{4,5},{5,4},{6,7},{7,6},{8,9},{9,8},{10,11... | collective-permute-start | bytes 36872 | tf_op jit(solution)/shard_map/ppermute | solution.py:22

commit v5 on v4

--- a/solution.py
+++ b/solution.py
@@ -154,56 +154,84 @@
     full = (8, size)
     lane = lax.broadcasted_iota(jnp.int32, full, 1)
     sub = lax.broadcasted_iota(jnp.int32, full, 0)
-    upper = [sym[8 * t:8 * t + 8, :] for t in range(tiles)]
-    inverse = [(lane == sub + 8 * t).astype(f32) for t in range(tiles)]
+    on_diagonal = [jnp.where(lane == sub + 8 * t, sym[8 * t:8 * t + 8, :], 0.0) for t in range(tiles)]
+    across = sum(on_diagonal[1:], on_diagonal[0]).sum(axis=0, keepdims=True)
+    across = lax.rsqrt(jnp.broadcast_to(across, full))
+    state = [
+        sym[8 * t:8 * t + 8, :]
+        * across
+        * lax.rsqrt(jnp.broadcast_to(on_diagonal[t].sum(axis=1, keepdims=True), full))
+        for t in range(tiles)
+    ]
+    undo = 1.0 / across
+    upper, inverse = [], []
     for t in range(tiles):
         k = 8 * t
-        rows = [jnp.broadcast_to(upper[t][i:i + 1, :], full) for i in range(8)]
-        inv_rows = [jnp.broadcast_to(inverse[t][i:i + 1, :], full) for i in range(8)]
-        own = [jnp.broadcast_to(upper[t][:, k + i:k + i + 1], full) for i in range(8)]
+        panel = (lane >= k) & (lane < k + 8)
+        rows = [jnp.broadcast_to(state[t][i:i + 1, :], full) for i in range(8)]
+        own = [jnp.broadcast_to(state[t][:, k + i:k + i + 1], full) for i in range(8)]
         entry = {
             (a, b): jnp.broadcast_to(own[b][a:a + 1, :], full) for a in range(8) for b in range(a, 8)
         }
         columns = {
-            i: [jnp.broadcast_to(upper[i][:, k + a:k + a + 1], full) for a in range(8)]
+            i: [jnp.broadcast_to(state[i][:, k + a:k + a + 1], full) for a in range(8)]
             for i in range(t + 1, tiles)
         }
-        recip, ratio = [], {}
-        for a in range(8):
-            recip.append(1.0 / entry[a, a])
-            for b in range(a + 1, 8):
-                ratio[a, b] = entry[a, b] * recip[a]
-            for b in range(a + 1, 8):
-                for c in range(b, 8):
-                    entry[b, c] = entry[b, c] - ratio[a, b] * entry[a, c]
-                rows[b] = rows[b] - ratio[a, b] * rows[a]
-                inv_rows[b] = inv_rows[b] - ratio[a, b] * inv_rows[a]
+        mixed = [jnp.where(panel, (lane == k + i).astype(f32), rows[i]) for i in range(8)]
+        for i in range(t + 1, tiles):
+            state[i] = jnp.where(panel, 0.0, state[i])
+
+        def solve(a, x, y, inverse_of):
+            p, q, r = entry[a, a], entry[a, a + 1], entry[a + 1, a + 1]
+            return (r * x - q * y) * inverse_of, (p * y - q * x) * inverse_of
+
+        recip, ratio = {}, {}
+        for a in range(0, 8, 2):
+            c = a + 1
+            recip[a] = 1.0 / (entry[a, a] * entry[c, c] - entry[a, c] * entry[a, c])
+            for b in range(a + 2, 8):
+                ratio[a, b], ratio[c, b] = solve(a, entry[a, b], entry[c, b], recip[a])
+            for b in range(a + 2, 8):
+                for d in range(b, 8):
+                    entry[b, d] = entry[b, d] - (
+                        ratio[a, b] * entry[a, d] + ratio[c, b] * entry[c, d]
+                    )
+                mixed[b] = mixed[b] - (ratio[a, b] * mixed[a] + ratio[c, b] * mixed[c])
             if t + 1 < tiles:
-                next_columns = columns[t + 1]
-                part = next_columns[a] * recip[a]
-                for b in range(a + 1, 8):
-                    next_columns[b] = next_columns[b] - next_columns[a] * ratio[a, b]
-                upper[t + 1] = upper[t + 1] - part * rows[a]
-                inverse[t + 1] = inverse[t + 1] - part * inv_rows[a]
+                ahead = columns[t + 1]
+                x, y = solve(a, ahead[a], ahead[c], recip[a])
+                for b in range(a + 2, 8):
+                    ahead[b] = ahead[b] - (x * entry[a, b] + y * entry[c, b])
+                state[t + 1] = state[t + 1] - (x * mixed[a] + y * mixed[c])
         if t + 2 < tiles:
-            back = [rows[a] * recip[a] for a in range(8)]
-            inv_back = [inv_rows[a] * recip[a] for a in range(8)]
-            for a in range(6, -1, -1):
-                for b in range(a + 1, 8):
+            back = [None] * 8
+            for a in range(6, -1, -2):
+                back[a], back[a + 1] = solve(a, mixed[a], mixed[a + 1], recip[a])
+                for b in range(a + 2, 8):
                     back[a] = back[a] - ratio[a, b] * back[b]
-                    inv_back[a] = inv_back[a] - ratio[a, b] * inv_back[b]
+                    back[a + 1] = back[a + 1] - ratio[a + 1, b] * back[b]
             for i in range(t + 2, tiles):
                 for a in range(7, -1, -1):
-                    upper[i] = upper[i] - columns[i][a] * back[a]
-                    inverse[i] = inverse[i] - columns[i][a] * inv_back[a]
-        pivot = entry[0, 0]
+                    state[i] = state[i] - columns[i][a] * back[a]
+        for a in range(0, 8, 2):
+            step = entry[a, a + 1] / entry[a, a]
+            mixed[a + 1] = mixed[a + 1] - step * mixed[a]
+            for b in range(7, a, -1):
+                entry[a + 1, b] = entry[a + 1, b] - step * entry[a, b]
+        pivot, result = entry[0, 0], mixed[0]
         for a in range(1, 8):
-            upper[t] = jnp.where(sub == a, rows[a], upper[t])
-            inverse[t] = jnp.where(sub == a, inv_rows[a], inverse[t])
             pivot = jnp.where(sub == a, entry[a, a], pivot)
+            result = jnp.where(sub == a, mixed[a], result)
         scale = 1.0 / jnp.sqrt(pivot)
-        upper[t] = jnp.where(lane >= sub + k, upper[t] * scale, 0.0)
-        inverse[t] = inverse[t] * scale
+        result = result * scale
+        corner = jnp.zeros(full, f32)
+        for b in range(8):
+            column = entry[0, b]
+            for a in range(1, b + 1):
+                column = jnp.where(sub == a, entry[a, b], column)
+            corner = jnp.where((lane == k + b) & (sub <= b), column * scale, corner)
+        upper.append(jnp.where(lane >= k + 8, result, corner) * undo)
+        inverse.append(jnp.where(lane < k + 8, result, 0.0) * across)
     return jnp.concatenate(upper, 0), jnp.concatenate(inverse, 0)
 
 

time: 124 us -> 122 us (0.984)
  Pallas kernels: 21.4 us -> 18.4 us
    pallas_call x1, Pallas kernels: 11 us -> 8.78 us  [orthonormalize(): pl.pallas_call(lambda *refs: factor_kernel(*refs, scale=math.sqrt(vertex_...]
  transfers between devices with their start and end apart: 26 -> 26, of which waited for: 13 -> 14; matrix products, arithmetic and copies ran while one was open for 1% -> 1% of each run, Pallas kernels for 7% -> 6%
where the time goes in v5:
time: 122 us
  blocking collectives  39.7 us (33%)
  starting transfers between devices  30.2 us (25%)
  waiting for transfers between devices  28.9 us (24%)
  Pallas kernels  18.4 us (15%)
  between operations  1.68 us (1%)
  other arithmetic  1.59 us (1%)
    all_to_all x2, blocking collectives, spread(): return lax.all_to_all(copies, axes, 0, 0, tiled=True)  26.6 us
    ppermute x20, starting transfers between devices, shift(): lax.ppermute(value, axis, [(i, (i + step) % size) for i in range(size)])  24.9 us
    ppermute x20, waiting for transfers between devices, shift(): lax.ppermute(value, axis, [(i, (i + step) % size) for i in range(size)])  20 us
    all_to_all x1, blocking collectives, sum_over_all(): part = lax.all_to_all(pieces, ('y', 'x'), 0, 0, tiled=True).sum(0)  13.1 us
    ppermute x6, waiting for transfers between devices, split_shift(): return lax.ppermute(value, (axis, 'core'), pairs)  8.88 us
    pallas_call x1, Pallas kernels, orthonormalize(): pl.pallas_call(lambda *refs: factor_kernel(*refs, scale=math.sqrt(vertex_...  8.78 us
    ppermute x6, starting transfers between devices, split_shift(): return lax.ppermute(value, (axis, 'core'), pairs)  5.31 us
    pallas_call x2, Pallas kernels, multiply(): pl.pallas_call(lambda *refs: multiply_kernel(*refs, places=places, first=...  5.3 us
  transfers between devices with their start and end apart: 26, of which 14 were waited for; matrix products, arithmetic and copies ran while one was open for 1% of the time, Pallas kernels for 6%

profile of v5, /device:TPU:2, one launch (start us, length us, event | category | flops | bytes accessed | tf_op | source)
XLA Modules:
  0.0 122.1 jit_solution(17363829755475386607)
XLA Ops:
  0.6 0.1 collective-permute-start
  0.7 1.5 %collective-permute-done = bf16[256,256]{1,0:T(8,128)(2,1)S(1)} collective-permute-done((bf16[256,256]{1,0:T(8,128)(2,1)}, bf16[256,256]{1,0:T(8,128)(2,1)S(1)}, u32[]{:S(2)}, u32[]{:S(2)}) %collective-permute-start) | collective-permute-done | bytes 131104 | tf_op jit(solution)/shard_map/ppermute | solution.py:22
  2.3 0.9 pad_maximum_fusion.6
  3.2 2.0 %collective-permute-start.12 = (bf16[2,128,256]{2,1,0:T(8,128)(2,1)S(1)}, bf16[2,128,256]{2,1,0:T(8,128)(2,1)S(1)}, u32[]{:S(2)}, u32[]{:S(2)}) collective-permute-start(bf16[2,128,256]{2,1,0:T(8,128)(2,1)S(1)} %get-tuple-element.25), channel_id=1, source_target_pairs={{0,32},{1,225},{32,64},{33,1},{64,96},{65,33},{96,128},{97,65},{12... | collective-permute-start | bytes 393224 | tf_op jit(solution)/shard_map/ppermute | solution.py:286
  5.2 1.6 %collective-permute-start.1 = (bf16[2,128,256]{2,1,0:T(8,128)(2,1)S(1)}, bf16[2,128,256]{2,1,0:T(8,128)(2,1)S(1)}, u32[]{:S(2)}, u32[]{:S(2)}) collective-permute-start(bf16[2,128,256]{2,1,0:T(8,128)(2,1)S(1)} %get-tuple-element.26), channel_id=1, source_target_pairs={{0,8},{1,25},{8,16},{9,1},{16,24},{17,9},{24,0},{25,17},{2,10},{3,... | collective-permute-start | bytes 393224 | tf_op jit(solution)/shard_map/ppermute | solution.py:286
  6.7 5.3 %collective-permute-done.12 = bf16[2,128,256]{2,1,0:T(8,128)(2,1)S(1)} collective-permute-done((bf16[2,128,256]{2,1,0:T(8,128)(2,1)S(1)}, bf16[2,128,256]{2,1,0:T(8,128)(2,1)S(1)}, u32[]{:S(2)}, u32[]{:S(2)}) %collective-permute-start.12) | collective-permute-done | bytes 131104 | tf_op jit(solution)/shard_map/ppermute | solution.py:286
  12.1 1.7 %collective-permute-start.3 = (bf16[1,128,256]{2,1,0:T(8,128)(2,1)S(1)}, bf16[1,128,256]{2,1,0:T(8,128)(2,1)S(1)}, u32[]{:S(2)}, u32[]{:S(2)}) collective-permute-start(bf16[1,128,256]{2,1,0:T(8,128)(2,1)S(1)} %get-tuple-element.32), channel_id=1, source_target_pairs={{0,8},{1,25},{8,16},{9,1},{16,24},{17,9},{24,0},{25,17},{2,10},{3,... | collective-permute-start | bytes 196616 | tf_op jit(solution)/shard_map/ppermute | solution.py:286
  13.7 3.1 %collective-permute-start.2 = (bf16[1,128,256]{2,1,0:T(8,128)(2,1)S(1)}, bf16[1,128,256]{2,1,0:T(8,128)(2,1)S(1)}, u32[]{:S(2)}, u32[]{:S(2)}) collective-permute-start(bf16[1,128,256]{2,1,0:T(8,128)(2,1)S(1)} %get-tuple-element.31), channel_id=1, source_target_pairs={{0,1},{1,0},{2,3},{3,2},{4,5},{5,4},{6,7},{7,6},{8,9},{9,8},{10,11... | collective-permute-start | bytes 196616 | tf_op jit(solution)/shard_map/ppermute | solution.py:22
  16.8 1.4 %collective-permute-done.13 = bf16[2,128,256]{2,1,0:T(8,128)(2,1)S(1)} collective-permute-done((bf16[2,128,256]{2,1,0:T(8,128)(2,1)S(1)}, bf16[2,128,256]{2,1,0:T(8,128)(2,1)S(1)}, u32[]{:S(2)}, u32[]{:S(2)}) %collective-permute-start.13) | collective-permute-done | bytes 131104 | tf_op jit(solution)/shard_map/ppermute | solution.py:286
  18.2 0.9 slice_dynamic-update-slice_fusion.2
  19.2 3.3 %collective-permute-start.8 = (bf16[4,128,256]{2,1,0:T(8,128)(2,1)S(1)}, bf16[4,128,256]{2,1,0:T(8,128)(2,1)S(1)}, u32[]{:S(2)}, u32[]{:S(2)}) collective-permute-start(bf16[4,128,256]{2,1,0:T(8,128)(2,1)S(1)} %pad_maximum_fusion.refs_2_), channel_id=1, source_target_pairs={{0,224},{32,0},{64,32},{96,64},{128,96},{160,128},{192,160},{224,1... | collective-permute-start | bytes 786440 | tf_op jit(solution)/shard_map/ppermute | solution.py:22
  22.5 1.9 %collective-permute-done.14 = bf16[2,128,256]{2,1,0:T(8,128)(2,1)S(1)} collective-permute-done((bf16[2,128,256]{2,1,0:T(8,128)(2,1)S(1)}, bf16[2,128,256]{2,1,0:T(8,128)(2,1)S(1)}, u32[]{:S(2)}, u32[]{:S(2)}) %collective-permute-start.14) | collective-permute-done | bytes 131104 | tf_op jit(solution)/shard_map/ppermute | solution.py:286
  24.5 0.1 collective-permute-start.15
  24.7 3.6 %collective-permute-done.8.refs_4_ = bf16[4,128,256]{2,1,0:T(8,128)(2,1)S(1)} collective-permute-done((bf16[4,128,256]{2,1,0:T(8,128)(2,1)S(1)}, bf16[4,128,256]{2,1,0:T(8,128)(2,1)S(1)}, u32[]{:S(2)}, u32[]{:S(2)}) %collective-permute-start.8) | collective-permute-done | bytes 262176 | tf_op jit(solution)/shard_map/ppermute | solution.py:22
  28.4 2.2 %collective-permute-start.9 = (bf16[4,128,256]{2,1,0:T(8,128)(2,1)S(1)}, bf16[4,128,256]{2,1,0:T(8,128)(2,1)S(1)}, u32[]{:S(2)}, u32[]{:S(2)}) collective-permute-start(bf16[4,128,256]{2,1,0:T(8,128)(2,1)S(1)} %collective-permute-done.8.refs_4_), channel_id=1, source_target_pairs={{0,224},{32,0},{64,32},{96,64},{128,96},{160,128},{192,160},{224,1... | collective-permute-start | bytes 786440 | tf_op jit(solution)/shard_map/ppermute | solution.py:22
  30.6 0.2 collective-permute-done.16
  30.9 1.7 %collective-permute-start.17 = (bf16[8,128,256]{2,1,0:T(8,128)(2,1)S(1)}, bf16[8,128,256]{2,1,0:T(8,128)(2,1)S(1)}, u32[]{:S(2)}, u32[]{:S(2)}) collective-permute-start(bf16[8,128,256]{2,1,0:T(8,128)(2,1)S(1)} %slice_dynamic-update-slice_fusion.refs_9_), channel_id=1, source_target_pairs={{0,8},{8,16},{16,24},{24,0},{1,9},{9,17},{17,25},{25,1},{2,10},{10... | collective-permute-start | bytes 1572872 | tf_op jit(solution)/shard_map/ppermute | solution.py:22
  32.5 1.7 %collective-permute-start.19 = (bf16[8,128,256]{2,1,0:T(8,128)(2,1)S(1)}, bf16[8,128,256]{2,1,0:T(8,128)(2,1)S(1)}, u32[]{:S(2)}, u32[]{:S(2)}) collective-permute-start(bf16[8,128,256]{2,1,0:T(8,128)(2,1)S(1)} %slice_dynamic-update-slice_fusion.refs_9_), channel_id=1, source_target_pairs={{0,24},{8,0},{16,8},{24,16},{1,25},{9,1},{17,9},{25,17},{2,26},{10... | collective-permute-start | bytes 1572872 | tf_op jit(solution)/shard_map/ppermute | solution.py:22
  34.2 2.6 %collective-permute-done.9.refs_6_ = bf16[4,128,256]{2,1,0:T(8,128)(2,1)S(1)} collective-permute-done((bf16[4,128,256]{2,1,0:T(8,128)(2,1)S(1)}, bf16[4,128,256]{2,1,0:T(8,128)(2,1)S(1)}, u32[]{:S(2)}, u32[]{:S(2)}) %collective-permute-start.9) | collective-permute-done | bytes 262176 | tf_op jit(solution)/shard_map/ppermute | solution.py:22
  36.8 1.5 %collective-permute-start.10 = (bf16[4,128,256]{2,1,0:T(8,128)(2,1)S(1)}, bf16[4,128,256]{2,1,0:T(8,128)(2,1)S(1)}, u32[]{:S(2)}, u32[]{:S(2)}) collective-permute-start(bf16[4,128,256]{2,1,0:T(8,128)(2,1)S(1)} %collective-permute-done.9.refs_6_), channel_id=1, source_target_pairs={{0,224},{32,0},{64,32},{96,64},{128,96},{160,128},{192,160},{224,1... | collective-permute-start | bytes 786440 | tf_op jit(solution)/shard_map/ppermute | solution.py:22
  38.3 0.5 collective-permute-start.6
  39.6 4.3 %prepare.1 = (bf16[224,128,128]{2,1,0:T(8,128)(2,1)S(1)}, s32[256]{0:T(256)S(1)}, s32[256]{0:T(256)S(1)}, s32[2]{0:T(128)S(1)}, bf16[16,128]{1,0:T(8,128)(2,1)}) custom-call(s32[224]{0:T(256)S(1)} %fusion.10.entries_ref, bf16[224,128,128]{2,1,0:T(8,128)(2,1)} %bitcast.16), custom_call_target="tpu_custom_call" | custom-call | bytes 29360128 | tf_op jit(solution)/shard_map/prepare/pallas_call | solution.py:95
  43.8 0.6 collective-permute-done.10.refs_8_
  44.4 2.2 %collective-permute-start.11 = (bf16[2,128,256]{2,1,0:T(8,128)(2,1)S(1)}, bf16[2,128,256]{2,1,0:T(8,128)(2,1)S(1)}, u32[]{:S(2)}, u32[]{:S(2)}) collective-permute-start(bf16[2,128,256]{2,1,0:T(8,128)(2,1)S(1)} %slice.145), channel_id=1, source_target_pairs={{0,224},{32,0},{64,32},{96,64},{128,96},{160,128},{192,160},{224,1... | collective-permute-start | bytes 393224 | tf_op jit(solution)/shard_map/ppermute | solution.py:22
  46.8 1.3 %collective-permute-start.18 = (bf16[4,128,256]{2,1,0:T(8,128)(2,1)S(1)}, bf16[4,128,256]{2,1,0:T(8,128)(2,1)S(1)}, u32[]{:S(2)}, u32[]{:S(2)}) collective-permute-start(bf16[4,128,256]{2,1,0:T(8,128)(2,1)S(1)} %slice.153), channel_id=1, source_target_pairs={{0,8},{8,16},{16,24},{24,0},{1,9},{9,17},{17,25},{25,1},{2,10},{10... | collective-permute-start | bytes 786440 | tf_op jit(solution)/shard_map/ppermute | solution.py:22
  48.1 2.1 %collective-permute-start.20 = (bf16[4,128,256]{2,1,0:T(8,128)(2,1)S(1)}, bf16[4,128,256]{2,1,0:T(8,128)(2,1)S(1)}, u32[]{:S(2)}, u32[]{:S(2)}) collective-permute-start(bf16[4,128,256]{2,1,0:T(8,128)(2,1)S(1)} %slice.154), channel_id=1, source_target_pairs={{0,24},{8,0},{16,8},{24,16},{1,25},{9,1},{17,9},{25,17},{2,26},{10... | collective-permute-start | bytes 786440 | tf_op jit(solution)/shard_map/ppermute | solution.py:22
  50.2 3.3 %multiply_first.1.refs_7_ = f32[2176,256]{1,0:T(8,128)S(1)} custom-call(s32[256]{0:T(256)S(1)} %get-tuple-element.14.refs_0_, s32[2]{0:T(128)S(1)} %get-tuple-element.12.refs_1_, bf16[4,128,256]{2,1,0:T(8,128)(2,1)S(1)} %pad_maximum_fusion.refs_2_, bf16[4,128,256]{2,1,0:T(8,128)(2,1)S(1)} %collective-permute-done.4.refs_3_, ...), custom_call_target="tpu_custom_call" | custom-call | flops 6000000000 | tf_op jit(solution)/shard_map/multiply_first/pallas_call | solution.py:125
  53.5 0.9 collective-permute-done.18.refs_4_
  54.4 0.1 collective-permute-done.20.refs_5_
  54.6 2.0 %multiply_rest.1 = (f32[1032,256]{1,0:T(8,128)S(1)}, f32[1024,256]{1,0:T(8,128)S(1)}, f32[8,256]{1,0:T(8,128)S(1)}) custom-call(s32[256]{0:T(256)S(1)} %get-tuple-element.11.refs_0_, s32[2]{0:T(128)S(1)} %get-tuple-element.12.refs_1_, bf16[2,128,256]{2,1,0:T(8,128)(2,1)S(1)} %collective-permute-done.7.refs_2_, ...), custom_call_target="tpu_custom_call" | custom-call | flops 1000000000 | tf_op jit(solution)/shard_map/multiply_rest/pallas_call | solution.py:125
  56.6 0.1 collective-permute-start.21
  56.7 2.7 %collective-permute-done.21 = f32[1032,256]{1,0:T(8,128)S(1)} collective-permute-done((f32[1032,256]{1,0:T(8,128)S(1)}, f32[1032,256]{1,0:T(8,128)S(1)}, u32[]{:S(2)}, u32[]{:S(2)}) %collective-permute-start.21) | collective-permute-done | bytes 1056800 | tf_op jit(solution)/shard_map/ppermute | solution.py:22
  59.4 0.1 slice_add_fusion
  59.5 0.1 fusion
  59.7 0.1 pad_maximum_fusion.3
  59.8 2.2 %collective-permute-start.22 = (f16[272,256]{1,0:T(8,128)(2,1)S(1)}, f16[272,256]{1,0:T(8,128)(2,1)S(1)}, u32[]{:S(2)}, u32[]{:S(2)}) collective-permute-start(f16[272,256]{1,0:T(8,128)(2,1)S(1)} %get-tuple-element.33), channel_id=1, source_target_pairs={{0,4},{2,6},{4,0},{6,2},{1,5},{3,7},{5,1},{7,3},{8,12},{10,14},{12... | collective-permute-start | bytes 417800 | tf_op jit(solution)/shard_map/ppermute | solution.py:22
  62.1 1.1 collective-permute-start.23
  63.1 1.6 %collective-permute-start.24 = (f16[272,256]{1,0:T(8,128)(2,1)S(1)}, f16[272,256]{1,0:T(8,128)(2,1)S(1)}, u32[]{:S(2)}, u32[]{:S(2)}) collective-permute-start(f16[272,256]{1,0:T(8,128)(2,1)S(1)} %get-tuple-element.35), channel_id=1, source_target_pairs={{0,6},{2,0},{4,2},{6,4},{1,7},{3,1},{5,3},{7,5},{8,14},{10,8},{12,... | collective-permute-start | bytes 417800 | tf_op jit(solution)/shard_map/ppermute | solution.py:22
  64.7 2.5 %collective-permute-done.22 = f16[272,256]{1,0:T(8,128)(2,1)S(1)} collective-permute-done((f16[272,256]{1,0:T(8,128)(2,1)S(1)}, f16[272,256]{1,0:T(8,128)(2,1)S(1)}, u32[]{:S(2)}, u32[]{:S(2)}) %collective-permute-start.22) | collective-permute-done | bytes 139296 | tf_op jit(solution)/shard_map/ppermute | solution.py:22
  67.3 4.1 %collective-permute-done.23 = f16[272,256]{1,0:T(8,128)(2,1)S(1)} collective-permute-done((f16[272,256]{1,0:T(8,128)(2,1)S(1)}, f16[272,256]{1,0:T(8,128)(2,1)S(1)}, u32[]{:S(2)}, u32[]{:S(2)}) %collective-permute-start.23) | collective-permute-done | bytes 139296 | tf_op jit(solution)/shard_map/ppermute | solution.py:22
  71.5 0.1 fusion.2.refs_1_
  71.6 0.6 fusion.24
  72.3 13.1 %all_to_all.15 = f32[16,24,128]{2,1,0:T(8,128)S(1)} all-to-all(f32[16,24,128]{2,1,0:T(8,128)S(1)} %bitcast.17), channel_id=1, replica_groups=mesh['z'=8,'y'=4,'x'=4,'core'=2] {'y','x'}, dimensions={0} | all-to-all | bytes 393216 | tf_op jit(solution)/shard_map/all_to_all | solution.py:275
  85.4 0.1 collective-permute-start.25
  85.5 1.2 collective-permute-done.25
  86.7 15.2 %all_to_all.16 = f32[8,24,128]{2,1,0:T(8,128)S(1)} all-to-all(f32[8,24,128]{2,1,0:T(8,128)S(1)} %broadcast_in_dim.31), channel_id=1, replica_groups=mesh['z'=8,'y'=4,'x'=4,'core'=2] {'z'}, dimensions={0} | all-to-all | bytes 196608 | tf_op jit(solution)/shard_map/all_to_all | solution.py:268
  102.0 11.3 %all_to_all.17 = f32[16,24,128]{2,1,0:T(8,128)S(1)} all-to-all(f32[16,24,128]{2,1,0:T(8,128)S(1)} %broadcast_in_dim.32), channel_id=1, replica_groups=mesh['z'=8,'y'=4,'x'=4,'core'=2] {'y','x'}, dimensions={0} | all-to-all | bytes 393216 | tf_op jit(solution)/shard_map/all_to_all | solution.py:268
  113.3 8.8 %orthonormalize.1 = (f32[256,256]{1,0:T(8,128)}, f32[256,256]{1,0:T(8,128)}) custom-call(f32[384,128]{1,0:T(8,128)S(1)} %bitcast.15, f32[256,256]{1,0:T(8,128)S(1)} %fusion.2.refs_1_), custom_call_target="tpu_custom_call" | custom-call | tf_op jit(solution)/shard_map/orthonormalize/pallas_call | solution.py:255
  (58 shorter events, 0.8 us)
Async XLA Ops:
  0.6 1.6 %collective-permute-start = (bf16[256,256]{1,0:T(8,128)(2,1)}, bf16[256,256]{1,0:T(8,128)(2,1)S(1)}, u32[]{:S(2)}, u32[]{:S(2)}) collective-permute-start(bf16[256,256]{1,0:T(8,128)(2,1)} %param.10), channel_id=1, source_target_pairs={{0,1},{1,0},{2,3},{3,2},{4,5},{5,4},{6,7},{7,6},{8,9},{9,8},{10,11... | collective-permute-start | bytes 393224 | tf_op jit(solution)/shard_map/ppermute | solution.py:22
  3.2 8.9 %collective-permute-start.12 = (bf16[2,128,256]{2,1,0:T(8,128)(2,1)S(1)}, bf16[2,128,256]{2,1,0:T(8,128)(2,1)S(1)}, u32[]{:S(2)}, u32[]{:S(2)}) collective-permute-start(bf16[2,128,256]{2,1,0:T(8,128)(2,1)S(1)} %get-tuple-element.25), channel_id=1, source_target_pairs={{0,32},{1,225},{32,64},{33,1},{64,96},{65,33},{96,128},{97,65},{12... | collective-permute-start | bytes 393224 | tf_op jit(solution)/shard_map/ppermute | solution.py:286
  5.2 6.9 %collective-permute-start.1 = (bf16[2,128,256]{2,1,0:T(8,128)(2,1)S(1)}, bf16[2,128,256]{2,1,0:T(8,128)(2,1)S(1)}, u32[]{:S(2)}, u32[]{:S(2)}) collective-permute-start(bf16[2,128,256]{2,1,0:T(8,128)(2,1)S(1)} %get-tuple-element.26), channel_id=1, source_target_pairs={{0,8},{1,25},{8,16},{9,1},{16,24},{17,9},{24,0},{25,17},{2,10},{3,... | collective-permute-start | bytes 393224 | tf_op jit(solution)/shard_map/ppermute | solution.py:286
  12.0 6.2 %collective-permute-start.13 = (bf16[2,128,256]{2,1,0:T(8,128)(2,1)S(1)}, bf16[2,128,256]{2,1,0:T(8,128)(2,1)S(1)}, u32[]{:S(2)}, u32[]{:S(2)}) collective-permute-start(bf16[2,128,256]{2,1,0:T(8,128)(2,1)S(1)} %collective-permute-done.12), channel_id=1, source_target_pairs={{0,32},{1,225},{32,64},{33,1},{64,96},{65,33},{96,128},{97,65},{12... | collective-permute-start | bytes 393224 | tf_op jit(solution)/shard_map/ppermute | solution.py:286
  12.1 7.1 %collective-permute-start.3 = (bf16[1,128,256]{2,1,0:T(8,128)(2,1)S(1)}, bf16[1,128,256]{2,1,0:T(8,128)(2,1)S(1)}, u32[]{:S(2)}, u32[]{:S(2)}) collective-permute-start(bf16[1,128,256]{2,1,0:T(8,128)(2,1)S(1)} %get-tuple-element.32), channel_id=1, source_target_pairs={{0,8},{1,25},{8,16},{9,1},{16,24},{17,9},{24,0},{25,17},{2,10},{3,... | collective-permute-start | bytes 196616 | tf_op jit(solution)/shard_map/ppermute | solution.py:286
  13.7 5.4 %collective-permute-start.2 = (bf16[1,128,256]{2,1,0:T(8,128)(2,1)S(1)}, bf16[1,128,256]{2,1,0:T(8,128)(2,1)S(1)}, u32[]{:S(2)}, u32[]{:S(2)}) collective-permute-start(bf16[1,128,256]{2,1,0:T(8,128)(2,1)S(1)} %get-tuple-element.31), channel_id=1, source_target_pairs={{0,1},{1,0},{2,3},{3,2},{4,5},{5,4},{6,7},{7,6},{8,9},{9,8},{10,11... | collective-permute-start | bytes 196616 | tf_op jit(solution)/shard_map/ppermute | solution.py:22
  18.2 6.3 %collective-permute-start.14 = (bf16[2,128,256]{2,1,0:T(8,128)(2,1)S(1)}, bf16[2,128,256]{2,1,0:T(8,128)(2,1)S(1)}, u32[]{:S(2)}, u32[]{:S(2)}) collective-permute-start(bf16[2,128,256]{2,1,0:T(8,128)(2,1)S(1)} %collective-permute-done.13), channel_id=1, source_target_pairs={{0,32},{1,225},{32,64},{33,1},{64,96},{65,33},{96,128},{97,65},{12... | collective-permute-start | bytes 393224 | tf_op jit(solution)/shard_map/ppermute | solution.py:286
  19.1 20.3 %copy-start.1 = (s32[1,1,224]{2,1,0:T(1,128)S(1)}, s32[1,1,224]{2,1,0:T(1,128)}, u32[]{:S(2)}) copy-start(s32[1,1,224]{2,1,0:T(1,128)} %param.8) | copy-start | bytes 2692
  19.2 20.3 %copy-start.2 = (s32[1,1,224]{2,1,0:T(1,128)S(1)}, s32[1,1,224]{2,1,0:T(1,128)}, u32[]{:S(2)}) copy-start(s32[1,1,224]{2,1,0:T(1,128)} %param.7) | copy-start | bytes 2692
  19.2 9.1 %collective-permute-start.8 = (bf16[4,128,256]{2,1,0:T(8,128)(2,1)S(1)}, bf16[4,128,256]{2,1,0:T(8,128)(2,1)S(1)}, u32[]{:S(2)}, u32[]{:S(2)}) collective-permute-start(bf16[4,128,256]{2,1,0:T(8,128)(2,1)S(1)} %pad_maximum_fusion.refs_2_), channel_id=1, source_target_pairs={{0,224},{32,0},{64,32},{96,64},{128,96},{160,128},{192,160},{224,1... | collective-permute-start | bytes 786440 | tf_op jit(solution)/shard_map/ppermute | solution.py:22
  22.5 8.0 %collective-permute-start.4 = (bf16[4,128,256]{2,1,0:T(8,128)(2,1)S(1)}, bf16[4,128,256]{2,1,0:T(8,128)(2,1)S(1)}, u32[]{:S(2)}, u32[]{:S(2)}) collective-permute-start(bf16[4,128,256]{2,1,0:T(8,128)(2,1)S(1)} %pad_maximum_fusion.refs_2_), channel_id=1, source_target_pairs={{0,32},{32,64},{64,96},{96,128},{128,160},{160,192},{192,224},{224... | collective-permute-start | bytes 786440 | tf_op jit(solution)/shard_map/ppermute | solution.py:22
  24.5 6.0 %collective-permute-start.15 = (bf16[3,128,256]{2,1,0:T(8,128)(2,1)S(1)}, bf16[3,128,256]{2,1,0:T(8,128)(2,1)S(1)}, u32[]{:S(2)}, u32[]{:S(2)}) collective-permute-start(bf16[3,128,256]{2,1,0:T(8,128)(2,1)S(1)} %pad_maximum_fusion.4), channel_id=1, source_target_pairs={{0,1},{1,0},{2,3},{3,2},{4,5},{5,4},{6,7},{7,6},{8,9},{9,8},{10,11... | collective-permute-start | bytes 589832 | tf_op jit(solution)/shard_map/ppermute | solution.py:22
  24.6 6.2 %collective-permute-start.16 = (bf16[1,128,256]{2,1,0:T(8,128)(2,1)S(1)}, bf16[1,128,256]{2,1,0:T(8,128)(2,1)S(1)}, u32[]{:S(2)}, u32[]{:S(2)}) collective-permute-start(bf16[1,128,256]{2,1,0:T(8,128)(2,1)S(1)} %get-tuple-element.27), channel_id=1, source_target_pairs={{0,32},{1,225},{32,64},{33,1},{64,96},{65,33},{96,128},{97,65},{12... | collective-permute-start | bytes 196616 | tf_op jit(solution)/shard_map/ppermute | solution.py:286
  28.4 8.4 %collective-permute-start.9 = (bf16[4,128,256]{2,1,0:T(8,128)(2,1)S(1)}, bf16[4,128,256]{2,1,0:T(8,128)(2,1)S(1)}, u32[]{:S(2)}, u32[]{:S(2)}) collective-permute-start(bf16[4,128,256]{2,1,0:T(8,128)(2,1)S(1)} %collective-permute-done.8.refs_4_), channel_id=1, source_target_pairs={{0,224},{32,0},{64,32},{96,64},{128,96},{160,128},{192,160},{224,1... | collective-permute-start | bytes 786440 | tf_op jit(solution)/shard_map/ppermute | solution.py:22
  30.6 7.7 %collective-permute-start.5 = (bf16[4,128,256]{2,1,0:T(8,128)(2,1)S(1)}, bf16[4,128,256]{2,1,0:T(8,128)(2,1)S(1)}, u32[]{:S(2)}, u32[]{:S(2)}) collective-permute-start(bf16[4,128,256]{2,1,0:T(8,128)(2,1)S(1)} %collective-permute-done.4.refs_3_), channel_id=1, source_target_pairs={{0,32},{32,64},{64,96},{96,128},{128,160},{160,192},{192,224},{224... | collective-permute-start | bytes 786440 | tf_op jit(solution)/shard_map/ppermute | solution.py:22
  30.9 15.9 %collective-permute-start.17 = (bf16[8,128,256]{2,1,0:T(8,128)(2,1)S(1)}, bf16[8,128,256]{2,1,0:T(8,128)(2,1)S(1)}, u32[]{:S(2)}, u32[]{:S(2)}) collective-permute-start(bf16[8,128,256]{2,1,0:T(8,128)(2,1)S(1)} %slice_dynamic-update-slice_fusion.refs_9_), channel_id=1, source_target_pairs={{0,8},{8,16},{16,24},{24,0},{1,9},{9,17},{17,25},{25,1},{2,10},{10... | collective-permute-start | bytes 1572872 | tf_op jit(solution)/shard_map/ppermute | solution.py:22
  32.5 15.6 %collective-permute-start.19 = (bf16[8,128,256]{2,1,0:T(8,128)(2,1)S(1)}, bf16[8,128,256]{2,1,0:T(8,128)(2,1)S(1)}, u32[]{:S(2)}, u32[]{:S(2)}) collective-permute-start(bf16[8,128,256]{2,1,0:T(8,128)(2,1)S(1)} %slice_dynamic-update-slice_fusion.refs_9_), channel_id=1, source_target_pairs={{0,24},{8,0},{16,8},{24,16},{1,25},{9,1},{17,9},{25,17},{2,26},{10... | collective-permute-start | bytes 1572872 | tf_op jit(solution)/shard_map/ppermute | solution.py:22
  36.8 7.6 %collective-permute-start.10 = (bf16[4,128,256]{2,1,0:T(8,128)(2,1)S(1)}, bf16[4,128,256]{2,1,0:T(8,128)(2,1)S(1)}, u32[]{:S(2)}, u32[]{:S(2)}) collective-permute-start(bf16[4,128,256]{2,1,0:T(8,128)(2,1)S(1)} %collective-permute-done.9.refs_6_), channel_id=1, source_target_pairs={{0,224},{32,0},{64,32},{96,64},{128,96},{160,128},{192,160},{224,1... | collective-permute-start | bytes 786440 | tf_op jit(solution)/shard_map/ppermute | solution.py:22
  38.3 8.3 %collective-permute-start.6 = (bf16[4,128,256]{2,1,0:T(8,128)(2,1)S(1)}, bf16[4,128,256]{2,1,0:T(8,128)(2,1)S(1)}, u32[]{:S(2)}, u32[]{:S(2)}) collective-permute-start(bf16[4,128,256]{2,1,0:T(8,128)(2,1)S(1)} %collective-permute-done.5.refs_5_), channel_id=1, source_target_pairs={{0,32},{32,64},{64,96},{96,128},{128,160},{160,192},{192,224},{224... | collective-permute-start | bytes 786440 | tf_op jit(solution)/shard_map/ppermute | solution.py:22
  44.4 9.1 %collective-permute-start.11 = (bf16[2,128,256]{2,1,0:T(8,128)(2,1)S(1)}, bf16[2,128,256]{2,1,0:T(8,128)(2,1)S(1)}, u32[]{:S(2)}, u32[]{:S(2)}) collective-permute-start(bf16[2,128,256]{2,1,0:T(8,128)(2,1)S(1)} %slice.145), channel_id=1, source_target_pairs={{0,224},{32,0},{64,32},{96,64},{128,96},{160,128},{192,160},{224,1... | collective-permute-start | bytes 393224 | tf_op jit(solution)/shard_map/ppermute | solution.py:22
  46.7 6.8 %collective-permute-start.7 = (bf16[2,128,256]{2,1,0:T(8,128)(2,1)S(1)}, bf16[2,128,256]{2,1,0:T(8,128)(2,1)S(1)}, u32[]{:S(2)}, u32[]{:S(2)}) collective-permute-start(bf16[2,128,256]{2,1,0:T(8,128)(2,1)S(1)} %slice.144), channel_id=1, source_target_pairs={{0,32},{32,64},{64,96},{96,128},{128,160},{160,192},{192,224},{224... | collective-permute-start | bytes 393224 | tf_op jit(solution)/shard_map/ppermute | solution.py:22
  46.8 7.7 %collective-permute-start.18 = (bf16[4,128,256]{2,1,0:T(8,128)(2,1)S(1)}, bf16[4,128,256]{2,1,0:T(8,128)(2,1)S(1)}, u32[]{:S(2)}, u32[]{:S(2)}) collective-permute-start(bf16[4,128,256]{2,1,0:T(8,128)(2,1)S(1)} %slice.153), channel_id=1, source_target_pairs={{0,8},{8,16},{16,24},{24,0},{1,9},{9,17},{17,25},{25,1},{2,10},{10... | collective-permute-start | bytes 786440 | tf_op jit(solution)/shard_map/ppermute | solution.py:22
  48.1 6.4 %collective-permute-start.20 = (bf16[4,128,256]{2,1,0:T(8,128)(2,1)S(1)}, bf16[4,128,256]{2,1,0:T(8,128)(2,1)S(1)}, u32[]{:S(2)}, u32[]{:S(2)}) collective-permute-start(bf16[4,128,256]{2,1,0:T(8,128)(2,1)S(1)} %slice.154), channel_id=1, source_target_pairs={{0,24},{8,0},{16,8},{24,16},{1,25},{9,1},{17,9},{25,17},{2,26},{10... | collective-permute-start | bytes 786440 | tf_op jit(solution)/shard_map/ppermute | solution.py:22
  56.6 2.8 %collective-permute-start.21 = (f32[1032,256]{1,0:T(8,128)S(1)}, f32[1032,256]{1,0:T(8,128)S(1)}, u32[]{:S(2)}, u32[]{:S(2)}) collective-permute-start(f32[1032,256]{1,0:T(8,128)S(1)} %get-tuple-element.16), channel_id=1, source_target_pairs={{0,1},{1,0},{2,3},{3,2},{4,5},{5,4},{6,7},{7,6},{8,9},{9,8},{10,11... | collective-permute-start | bytes 3170312 | tf_op jit(solution)/shard_map/ppermute | solution.py:22
  59.7 11.8 %copy-start = (f32[256]{0:T(256)S(1)}, f32[256]{0:T(256)}, u32[]{:S(2)}) copy-start(f32[256]{0:T(256)} %param.11) | copy-start | bytes 3076
  59.8 7.4 %collective-permute-start.22 = (f16[272,256]{1,0:T(8,128)(2,1)S(1)}, f16[272,256]{1,0:T(8,128)(2,1)S(1)}, u32[]{:S(2)}, u32[]{:S(2)}) collective-permute-start(f16[272,256]{1,0:T(8,128)(2,1)S(1)} %get-tuple-element.33), channel_id=1, source_target_pairs={{0,4},{2,6},{4,0},{6,2},{1,5},{3,7},{5,1},{7,3},{8,12},{10,14},{12... | collective-permute-start | bytes 417800 | tf_op jit(solution)/shard_map/ppermute | solution.py:22
  62.1 9.4 %collective-permute-start.23 = (f16[272,256]{1,0:T(8,128)(2,1)S(1)}, f16[272,256]{1,0:T(8,128)(2,1)S(1)}, u32[]{:S(2)}, u32[]{:S(2)}) collective-permute-start(f16[272,256]{1,0:T(8,128)(2,1)S(1)} %get-tuple-element.34), channel_id=1, source_target_pairs={{0,2},{2,4},{4,6},{6,0},{1,3},{3,5},{5,7},{7,1},{8,10},{10,12},{12... | collective-permute-start | bytes 417800 | tf_op jit(solution)/shard_map/ppermute | solution.py:22
  63.1 8.3 %collective-permute-start.24 = (f16[272,256]{1,0:T(8,128)(2,1)S(1)}, f16[272,256]{1,0:T(8,128)(2,1)S(1)}, u32[]{:S(2)}, u32[]{:S(2)}) collective-permute-start(f16[272,256]{1,0:T(8,128)(2,1)S(1)} %get-tuple-element.35), channel_id=1, source_target_pairs={{0,6},{2,0},{4,2},{6,4},{1,7},{3,1},{5,3},{7,5},{8,14},{10,8},{12,... | collective-permute-start | bytes 417800 | tf_op jit(solution)/shard_map/ppermute | solution.py:22
  85.4 1.3 %collective-permute-start.25 = (f32[24,128]{1,0:T(8,128)S(1)}, f32[24,128]{1,0:T(8,128)S(1)}, u32[]{:S(2)}, u32[]{:S(2)}) collective-permute-start(f32[24,128]{1,0:T(8,128)S(1)} %reduce_sum.18), channel_id=1, source_target_pairs={{0,1},{1,0},{2,3},{3,2},{4,5},{5,4},{6,7},{7,6},{8,9},{9,8},{10,11... | collective-permute-start | bytes 36872 | tf_op jit(solution)/shard_map/ppermute | solution.py:22

commit v6 on v5

--- a/solution.py
+++ b/solution.py
@@ -313,8 +313,9 @@
         cut = forth.shape[0] // 2
         return shift(forth[:cut], axis, 1), shift(back[cut:], axis, -1)
 
-    both = jnp.stack([omega, shift(omega, "core", 1)])
-    block1, block2 = short_way(both[:, :half], "y"), short_way(both[:, half:], "z")
+    other = shift(omega, "core", 1)
+    block2 = short_way(jnp.stack([omega[half:], other[half:]]), "z")
+    block1 = short_way(jnp.stack([omega[:half], other[:half]]), "y")
     full1, forth1, back1 = ring(block1, "z")
     block2, token = lax.optimization_barrier((block2, token))
     full2, forth2, back2 = ring(block2, "y")

time: 122 us -> 120 us (0.984)
  waiting for transfers between devices: 28.9 us -> 25.3 us
  starting transfers between devices: 30.2 us -> 33.5 us
  blocking collectives: 39.7 us -> 37.9 us
    ppermute x20, waiting for transfers between devices: 20 us -> 14.1 us  [shift(): lax.ppermute(value, axis, [(i, (i + step) % size) for i in range(size)])]
    ppermute x20, starting transfers between devices: 24.9 us -> 28.1 us  [shift(): lax.ppermute(value, axis, [(i, (i + step) % size) for i in range(size)])]
    ppermute x6, waiting for transfers between devices: 8.88 us -> 11.1 us  [split_shift(): return lax.ppermute(value, (axis, 'core'), pairs)]
  transfers between devices with their start and end apart: 26 -> 26, of which waited for: 14 -> 12; matrix products, arithmetic and copies ran while one was open for 1% -> 1% of each run, Pallas kernels for 6% -> 7%
where the time goes in v6:
time: 120 us
  blocking collectives  37.9 us (32%)
  starting transfers between devices  33.5 us (28%)
  waiting for transfers between devices  25.3 us (21%)
  Pallas kernels  19.2 us (16%)
  between operations  1.7 us (1%)
    ppermute x20, starting transfers between devices, shift(): lax.ppermute(value, axis, [(i, (i + step) % size) for i in range(size)])  28.1 us
    all_to_all x2, blocking collectives, spread(): return lax.all_to_all(copies, axes, 0, 0, tiled=True)  25.5 us
    ppermute x20, waiting for transfers between devices, shift(): lax.ppermute(value, axis, [(i, (i + step) % size) for i in range(size)])  14.1 us
    all_to_all x1, blocking collectives, sum_over_all(): part = lax.all_to_all(pieces, ('y', 'x'), 0, 0, tiled=True).sum(0)  12.4 us
    ppermute x6, waiting for transfers between devices, split_shift(): return lax.ppermute(value, (axis, 'core'), pairs)  11.1 us
    pallas_call x1, Pallas kernels, orthonormalize(): pl.pallas_call(lambda *refs: factor_kernel(*refs, scale=math.sqrt(vertex_...  8.78 us
    pallas_call x2, Pallas kernels, multiply(): pl.pallas_call(lambda *refs: multiply_kernel(*refs, places=places, first=...  6.19 us
    ppermute x6, starting transfers between devices, split_shift(): return lax.ppermute(value, (axis, 'core'), pairs)  5.39 us
  transfers between devices with their start and end apart: 26, of which 12 were waited for; matrix products, arithmetic and copies ran while one was open for 1% of the time, Pallas kernels for 7%

profile of v6, /device:TPU:2, one launch (start us, length us, event | category | flops | bytes accessed | tf_op | source)
XLA Modules:
  0.0 120.1 jit_solution(11471812624028225627)
XLA Ops:
  0.6 0.1 collective-permute-start
  0.7 0.9 slice_bitcast_fusion.2
  1.6 0.7 collective-permute-done
  2.3 2.0 %collective-permute-start.12 = (bf16[2,128,256]{2,1,0:T(8,128)(2,1)S(1)}, bf16[2,128,256]{2,1,0:T(8,128)(2,1)S(1)}, u32[]{:S(2)}, u32[]{:S(2)}) collective-permute-start(bf16[2,128,256]{2,1,0:T(8,128)(2,1)S(1)} %pad_maximum_fusion.7), channel_id=1, source_target_pairs={{0,32},{1,225},{32,64},{33,1},{64,96},{65,33},{96,128},{97,65},{12... | collective-permute-start | bytes 393224 | tf_op jit(solution)/shard_map/ppermute | solution.py:286
  4.3 1.7 %collective-permute-start.1 = (bf16[2,128,256]{2,1,0:T(8,128)(2,1)S(1)}, bf16[2,128,256]{2,1,0:T(8,128)(2,1)S(1)}, u32[]{:S(2)}, u32[]{:S(2)}) collective-permute-start(bf16[2,128,256]{2,1,0:T(8,128)(2,1)S(1)} %pad_maximum_fusion.6), channel_id=1, source_target_pairs={{0,8},{1,25},{8,16},{9,1},{16,24},{17,9},{24,0},{25,17},{2,10},{3,... | collective-permute-start | bytes 393224 | tf_op jit(solution)/shard_map/ppermute | solution.py:286
  6.0 5.2 %collective-permute-done.12 = bf16[2,128,256]{2,1,0:T(8,128)(2,1)S(1)} collective-permute-done((bf16[2,128,256]{2,1,0:T(8,128)(2,1)S(1)}, bf16[2,128,256]{2,1,0:T(8,128)(2,1)S(1)}, u32[]{:S(2)}, u32[]{:S(2)}) %collective-permute-start.12) | collective-permute-done | bytes 131104 | tf_op jit(solution)/shard_map/ppermute | solution.py:286
  11.2 1.7 %collective-permute-start.3 = (bf16[1,128,256]{2,1,0:T(8,128)(2,1)S(1)}, bf16[1,128,256]{2,1,0:T(8,128)(2,1)S(1)}, u32[]{:S(2)}, u32[]{:S(2)}) collective-permute-start(bf16[1,128,256]{2,1,0:T(8,128)(2,1)S(1)} %get-tuple-element.32), channel_id=1, source_target_pairs={{0,8},{1,25},{8,16},{9,1},{16,24},{17,9},{24,0},{25,17},{2,10},{3,... | collective-permute-start | bytes 196616 | tf_op jit(solution)/shard_map/ppermute | solution.py:286
  12.9 3.2 %collective-permute-start.2 = (bf16[1,128,256]{2,1,0:T(8,128)(2,1)S(1)}, bf16[1,128,256]{2,1,0:T(8,128)(2,1)S(1)}, u32[]{:S(2)}, u32[]{:S(2)}) collective-permute-start(bf16[1,128,256]{2,1,0:T(8,128)(2,1)S(1)} %get-tuple-element.31), channel_id=1, source_target_pairs={{0,1},{1,0},{2,3},{3,2},{4,5},{5,4},{6,7},{7,6},{8,9},{9,8},{10,11... | collective-permute-start | bytes 196616 | tf_op jit(solution)/shard_map/ppermute | solution.py:22
  16.1 1.3 %collective-permute-done.13 = bf16[2,128,256]{2,1,0:T(8,128)(2,1)S(1)} collective-permute-done((bf16[2,128,256]{2,1,0:T(8,128)(2,1)S(1)}, bf16[2,128,256]{2,1,0:T(8,128)(2,1)S(1)}, u32[]{:S(2)}, u32[]{:S(2)}) %collective-permute-start.13) | collective-permute-done | bytes 131104 | tf_op jit(solution)/shard_map/ppermute | solution.py:286
  17.5 3.3 %collective-permute-start.8 = (bf16[4,128,256]{2,1,0:T(8,128)(2,1)S(1)}, bf16[4,128,256]{2,1,0:T(8,128)(2,1)S(1)}, u32[]{:S(2)}, u32[]{:S(2)}) collective-permute-start(bf16[4,128,256]{2,1,0:T(8,128)(2,1)S(1)} %pad_maximum_fusion.refs_2_), channel_id=1, source_target_pairs={{0,224},{32,0},{64,32},{96,64},{128,96},{160,128},{192,160},{224,1... | collective-permute-start | bytes 786440 | tf_op jit(solution)/shard_map/ppermute | solution.py:22
  20.8 3.9 %collective-permute-done.14 = bf16[2,128,256]{2,1,0:T(8,128)(2,1)S(1)} collective-permute-done((bf16[2,128,256]{2,1,0:T(8,128)(2,1)S(1)}, bf16[2,128,256]{2,1,0:T(8,128)(2,1)S(1)}, u32[]{:S(2)}, u32[]{:S(2)}) %collective-permute-start.14) | collective-permute-done | bytes 131104 | tf_op jit(solution)/shard_map/ppermute | solution.py:286
  24.7 0.1 collective-permute-start.15
  24.8 0.1 collective-permute-start.16
  24.9 1.7 %collective-permute-done.8.refs_4_ = bf16[4,128,256]{2,1,0:T(8,128)(2,1)S(1)} collective-permute-done((bf16[4,128,256]{2,1,0:T(8,128)(2,1)S(1)}, bf16[4,128,256]{2,1,0:T(8,128)(2,1)S(1)}, u32[]{:S(2)}, u32[]{:S(2)}) %collective-permute-start.8) | collective-permute-done | bytes 262176 | tf_op jit(solution)/shard_map/ppermute | solution.py:22
  26.6 3.0 %collective-permute-start.9 = (bf16[4,128,256]{2,1,0:T(8,128)(2,1)S(1)}, bf16[4,128,256]{2,1,0:T(8,128)(2,1)S(1)}, u32[]{:S(2)}, u32[]{:S(2)}) collective-permute-start(bf16[4,128,256]{2,1,0:T(8,128)(2,1)S(1)} %collective-permute-done.8.refs_4_), channel_id=1, source_target_pairs={{0,224},{32,0},{64,32},{96,64},{128,96},{160,128},{192,160},{224,1... | collective-permute-start | bytes 786440 | tf_op jit(solution)/shard_map/ppermute | solution.py:22
  29.6 0.7 collective-permute-done.16
  30.4 1.9 %collective-permute-start.17 = (bf16[8,128,256]{2,1,0:T(8,128)(2,1)S(1)}, bf16[8,128,256]{2,1,0:T(8,128)(2,1)S(1)}, u32[]{:S(2)}, u32[]{:S(2)}) collective-permute-start(bf16[8,128,256]{2,1,0:T(8,128)(2,1)S(1)} %slice_dynamic-update-slice_fusion.refs_9_), channel_id=1, source_target_pairs={{0,8},{8,16},{16,24},{24,0},{1,9},{9,17},{17,25},{25,1},{2,10},{10... | collective-permute-start | bytes 1572872 | tf_op jit(solution)/shard_map/ppermute | solution.py:22
  32.3 1.5 %collective-permute-start.19 = (bf16[8,128,256]{2,1,0:T(8,128)(2,1)S(1)}, bf16[8,128,256]{2,1,0:T(8,128)(2,1)S(1)}, u32[]{:S(2)}, u32[]{:S(2)}) collective-permute-start(bf16[8,128,256]{2,1,0:T(8,128)(2,1)S(1)} %slice_dynamic-update-slice_fusion.refs_9_), channel_id=1, source_target_pairs={{0,24},{8,0},{16,8},{24,16},{1,25},{9,1},{17,9},{25,17},{2,26},{10... | collective-permute-start | bytes 1572872 | tf_op jit(solution)/shard_map/ppermute | solution.py:22
  33.7 1.3 %collective-permute-done.9.refs_6_ = bf16[4,128,256]{2,1,0:T(8,128)(2,1)S(1)} collective-permute-done((bf16[4,128,256]{2,1,0:T(8,128)(2,1)S(1)}, bf16[4,128,256]{2,1,0:T(8,128)(2,1)S(1)}, u32[]{:S(2)}, u32[]{:S(2)}) %collective-permute-start.9) | collective-permute-done | bytes 262176 | tf_op jit(solution)/shard_map/ppermute | solution.py:22
  35.1 2.4 %collective-permute-start.10 = (bf16[4,128,256]{2,1,0:T(8,128)(2,1)S(1)}, bf16[4,128,256]{2,1,0:T(8,128)(2,1)S(1)}, u32[]{:S(2)}, u32[]{:S(2)}) collective-permute-start(bf16[4,128,256]{2,1,0:T(8,128)(2,1)S(1)} %collective-permute-done.9.refs_6_), channel_id=1, source_target_pairs={{0,224},{32,0},{64,32},{96,64},{128,96},{160,128},{192,160},{224,1... | collective-permute-start | bytes 786440 | tf_op jit(solution)/shard_map/ppermute | solution.py:22
  38.2 4.3 %prepare.1 = (bf16[224,128,128]{2,1,0:T(8,128)(2,1)S(1)}, s32[256]{0:T(256)S(1)}, s32[256]{0:T(256)S(1)}, s32[2]{0:T(128)S(1)}, bf16[16,128]{1,0:T(8,128)(2,1)}) custom-call(s32[224]{0:T(256)S(1)} %fusion.9.entries_ref, bf16[224,128,128]{2,1,0:T(8,128)(2,1)} %bitcast.24), custom_call_target="tpu_custom_call" | custom-call | bytes 29360128 | tf_op jit(solution)/shard_map/prepare/pallas_call | solution.py:95
  42.5 0.2 collective-permute-done.10.refs_8_
  42.7 3.1 %collective-permute-start.11 = (bf16[2,128,256]{2,1,0:T(8,128)(2,1)S(1)}, bf16[2,128,256]{2,1,0:T(8,128)(2,1)S(1)}, u32[]{:S(2)}, u32[]{:S(2)}) collective-permute-start(bf16[2,128,256]{2,1,0:T(8,128)(2,1)S(1)} %slice.139), channel_id=1, source_target_pairs={{0,224},{32,0},{64,32},{96,64},{128,96},{160,128},{192,160},{224,1... | collective-permute-start | bytes 393224 | tf_op jit(solution)/shard_map/ppermute | solution.py:22
  45.8 0.1 collective-permute-start.7
  45.9 1.1 collective-permute-start.18
  47.0 2.3 %collective-permute-start.20 = (bf16[4,128,256]{2,1,0:T(8,128)(2,1)S(1)}, bf16[4,128,256]{2,1,0:T(8,128)(2,1)S(1)}, u32[]{:S(2)}, u32[]{:S(2)}) collective-permute-start(bf16[4,128,256]{2,1,0:T(8,128)(2,1)S(1)} %slice.148), channel_id=1, source_target_pairs={{0,24},{8,0},{16,8},{24,16},{1,25},{9,1},{17,9},{25,17},{2,26},{10... | collective-permute-start | bytes 786440 | tf_op jit(solution)/shard_map/ppermute | solution.py:22
  49.4 4.2 %multiply_first.1.refs_7_ = f32[2176,256]{1,0:T(8,128)S(1)} custom-call(s32[256]{0:T(256)S(1)} %get-tuple-element.14.refs_0_, s32[2]{0:T(128)S(1)} %get-tuple-element.12.refs_1_, bf16[4,128,256]{2,1,0:T(8,128)(2,1)S(1)} %pad_maximum_fusion.refs_2_, bf16[4,128,256]{2,1,0:T(8,128)(2,1)S(1)} %collective-permute-done.4.refs_3_, ...), custom_call_target="tpu_custom_call" | custom-call | flops 6000000000 | tf_op jit(solution)/shard_map/multiply_first/pallas_call | solution.py:125
  53.6 0.0 collective-permute-done.18.refs_4_
  53.6 2.0 %multiply_rest.1 = (f32[1032,256]{1,0:T(8,128)S(1)}, f32[1024,256]{1,0:T(8,128)S(1)}, f32[8,256]{1,0:T(8,128)S(1)}) custom-call(s32[256]{0:T(256)S(1)} %get-tuple-element.11.refs_0_, s32[2]{0:T(128)S(1)} %get-tuple-element.12.refs_1_, bf16[2,128,256]{2,1,0:T(8,128)(2,1)S(1)} %collective-permute-done.7.refs_2_, ...), custom_call_target="tpu_custom_call" | custom-call | flops 1000000000 | tf_op jit(solution)/shard_map/multiply_rest/pallas_call | solution.py:125
  55.6 0.1 collective-permute-start.21
  55.7 2.7 %collective-permute-done.21 = f32[1032,256]{1,0:T(8,128)S(1)} collective-permute-done((f32[1032,256]{1,0:T(8,128)S(1)}, f32[1032,256]{1,0:T(8,128)S(1)}, u32[]{:S(2)}, u32[]{:S(2)}) %collective-permute-start.21) | collective-permute-done | bytes 1056800 | tf_op jit(solution)/shard_map/ppermute | solution.py:22
  58.4 0.1 slice_add_fusion
  58.6 0.1 fusion
  58.6 0.1 fusion.20
  58.8 0.1 pad_maximum_fusion.3
  58.9 2.0 %collective-permute-start.23 = (f16[272,256]{1,0:T(8,128)(2,1)S(1)}, f16[272,256]{1,0:T(8,128)(2,1)S(1)}, u32[]{:S(2)}, u32[]{:S(2)}) collective-permute-start(f16[272,256]{1,0:T(8,128)(2,1)S(1)} %get-tuple-element.34), channel_id=1, source_target_pairs={{0,2},{2,4},{4,6},{6,0},{1,3},{3,5},{5,7},{7,1},{8,10},{10,12},{12... | collective-permute-start | bytes 417800 | tf_op jit(solution)/shard_map/ppermute | solution.py:22
  60.9 0.1 collective-permute-start.24
  61.0 3.9 %collective-permute-start.22 = (f16[272,256]{1,0:T(8,128)(2,1)S(1)}, f16[272,256]{1,0:T(8,128)(2,1)S(1)}, u32[]{:S(2)}, u32[]{:S(2)}) collective-permute-start(f16[272,256]{1,0:T(8,128)(2,1)S(1)} %get-tuple-element.33), channel_id=1, source_target_pairs={{0,4},{2,6},{4,0},{6,2},{1,5},{3,7},{5,1},{7,3},{8,12},{10,14},{12... | collective-permute-start | bytes 417800 | tf_op jit(solution)/shard_map/ppermute | solution.py:22
  64.9 2.2 %collective-permute-done.24 = f16[272,256]{1,0:T(8,128)(2,1)S(1)} collective-permute-done((f16[272,256]{1,0:T(8,128)(2,1)S(1)}, f16[272,256]{1,0:T(8,128)(2,1)S(1)}, u32[]{:S(2)}, u32[]{:S(2)}) %collective-permute-start.24) | collective-permute-done | bytes 139296 | tf_op jit(solution)/shard_map/ppermute | solution.py:22
  67.2 4.1 %collective-permute-done.22 = f16[272,256]{1,0:T(8,128)(2,1)S(1)} collective-permute-done((f16[272,256]{1,0:T(8,128)(2,1)S(1)}, f16[272,256]{1,0:T(8,128)(2,1)S(1)}, u32[]{:S(2)}, u32[]{:S(2)}) %collective-permute-start.22) | collective-permute-done | bytes 139296 | tf_op jit(solution)/shard_map/ppermute | solution.py:22
  71.3 0.1 fusion.2.refs_1_
  71.4 0.6 fusion.23
  72.1 12.4 %all_to_all.15 = f32[16,24,128]{2,1,0:T(8,128)S(1)} all-to-all(f32[16,24,128]{2,1,0:T(8,128)S(1)} %bitcast.25), channel_id=1, replica_groups=mesh['z'=8,'y'=4,'x'=4,'core'=2] {'y','x'}, dimensions={0} | all-to-all | bytes 393216 | tf_op jit(solution)/shard_map/all_to_all | solution.py:275
  84.5 0.1 collective-permute-start.25
  84.6 1.2 collective-permute-done.25
  85.8 14.1 %all_to_all.16 = f32[8,24,128]{2,1,0:T(8,128)S(1)} all-to-all(f32[8,24,128]{2,1,0:T(8,128)S(1)} %broadcast_in_dim.31), channel_id=1, replica_groups=mesh['z'=8,'y'=4,'x'=4,'core'=2] {'z'}, dimensions={0} | all-to-all | bytes 196608 | tf_op jit(solution)/shard_map/all_to_all | solution.py:268
  100.0 11.3 %all_to_all.17 = f32[16,24,128]{2,1,0:T(8,128)S(1)} all-to-all(f32[16,24,128]{2,1,0:T(8,128)S(1)} %broadcast_in_dim.32), channel_id=1, replica_groups=mesh['z'=8,'y'=4,'x'=4,'core'=2] {'y','x'}, dimensions={0} | all-to-all | bytes 393216 | tf_op jit(solution)/shard_map/all_to_all | solution.py:268
  111.3 8.8 %orthonormalize.1 = (f32[256,256]{1,0:T(8,128)}, f32[256,256]{1,0:T(8,128)}) custom-call(f32[384,128]{1,0:T(8,128)S(1)} %bitcast.23, f32[256,256]{1,0:T(8,128)S(1)} %fusion.2.refs_1_), custom_call_target="tpu_custom_call" | custom-call | tf_op jit(solution)/shard_map/orthonormalize/pallas_call | solution.py:255
  (63 shorter events, 0.6 us)
Async XLA Ops:
  0.6 1.6 %collective-permute-start = (bf16[256,256]{1,0:T(8,128)(2,1)}, bf16[256,256]{1,0:T(8,128)(2,1)S(1)}, u32[]{:S(2)}, u32[]{:S(2)}) collective-permute-start(bf16[256,256]{1,0:T(8,128)(2,1)} %param.10), channel_id=1, source_target_pairs={{0,1},{1,0},{2,3},{3,2},{4,5},{5,4},{6,7},{7,6},{8,9},{9,8},{10,11... | collective-permute-start | bytes 393224 | tf_op jit(solution)/shard_map/ppermute | solution.py:22
  2.3 22.5 %copy-start = (bf16[256,256]{1,0:T(8,128)(2,1)S(1)}, bf16[256,256]{1,0:T(8,128)(2,1)}, u32[]{:S(2)}) copy-start(bf16[256,256]{1,0:T(8,128)(2,1)} %param.10) | copy-start | bytes 393220
  2.3 8.9 %collective-permute-start.12 = (bf16[2,128,256]{2,1,0:T(8,128)(2,1)S(1)}, bf16[2,128,256]{2,1,0:T(8,128)(2,1)S(1)}, u32[]{:S(2)}, u32[]{:S(2)}) collective-permute-start(bf16[2,128,256]{2,1,0:T(8,128)(2,1)S(1)} %pad_maximum_fusion.7), channel_id=1, source_target_pairs={{0,32},{1,225},{32,64},{33,1},{64,96},{65,33},{96,128},{97,65},{12... | collective-permute-start | bytes 393224 | tf_op jit(solution)/shard_map/ppermute | solution.py:286
  4.3 6.9 %collective-permute-start.1 = (bf16[2,128,256]{2,1,0:T(8,128)(2,1)S(1)}, bf16[2,128,256]{2,1,0:T(8,128)(2,1)S(1)}, u32[]{:S(2)}, u32[]{:S(2)}) collective-permute-start(bf16[2,128,256]{2,1,0:T(8,128)(2,1)S(1)} %pad_maximum_fusion.6), channel_id=1, source_target_pairs={{0,8},{1,25},{8,16},{9,1},{16,24},{17,9},{24,0},{25,17},{2,10},{3,... | collective-permute-start | bytes 393224 | tf_op jit(solution)/shard_map/ppermute | solution.py:286
  11.2 6.2 %collective-permute-start.13 = (bf16[2,128,256]{2,1,0:T(8,128)(2,1)S(1)}, bf16[2,128,256]{2,1,0:T(8,128)(2,1)S(1)}, u32[]{:S(2)}, u32[]{:S(2)}) collective-permute-start(bf16[2,128,256]{2,1,0:T(8,128)(2,1)S(1)} %collective-permute-done.12), channel_id=1, source_target_pairs={{0,32},{1,225},{32,64},{33,1},{64,96},{65,33},{96,128},{97,65},{12... | collective-permute-start | bytes 393224 | tf_op jit(solution)/shard_map/ppermute | solution.py:286
  11.2 6.2 %collective-permute-start.3 = (bf16[1,128,256]{2,1,0:T(8,128)(2,1)S(1)}, bf16[1,128,256]{2,1,0:T(8,128)(2,1)S(1)}, u32[]{:S(2)}, u32[]{:S(2)}) collective-permute-start(bf16[1,128,256]{2,1,0:T(8,128)(2,1)S(1)} %get-tuple-element.32), channel_id=1, source_target_pairs={{0,8},{1,25},{8,16},{9,1},{16,24},{17,9},{24,0},{25,17},{2,10},{3,... | collective-permute-start | bytes 196616 | tf_op jit(solution)/shard_map/ppermute | solution.py:286
  12.9 4.5 %collective-permute-start.2 = (bf16[1,128,256]{2,1,0:T(8,128)(2,1)S(1)}, bf16[1,128,256]{2,1,0:T(8,128)(2,1)S(1)}, u32[]{:S(2)}, u32[]{:S(2)}) collective-permute-start(bf16[1,128,256]{2,1,0:T(8,128)(2,1)S(1)} %get-tuple-element.31), channel_id=1, source_target_pairs={{0,1},{1,0},{2,3},{3,2},{4,5},{5,4},{6,7},{7,6},{8,9},{9,8},{10,11... | collective-permute-start | bytes 196616 | tf_op jit(solution)/shard_map/ppermute | solution.py:22
  17.4 7.3 %collective-permute-start.14 = (bf16[2,128,256]{2,1,0:T(8,128)(2,1)S(1)}, bf16[2,128,256]{2,1,0:T(8,128)(2,1)S(1)}, u32[]{:S(2)}, u32[]{:S(2)}) collective-permute-start(bf16[2,128,256]{2,1,0:T(8,128)(2,1)S(1)} %collective-permute-done.13), channel_id=1, source_target_pairs={{0,32},{1,225},{32,64},{33,1},{64,96},{65,33},{96,128},{97,65},{12... | collective-permute-start | bytes 393224 | tf_op jit(solution)/shard_map/ppermute | solution.py:286
  17.5 20.7 %copy-start.2 = (s32[1,1,224]{2,1,0:T(1,128)S(1)}, s32[1,1,224]{2,1,0:T(1,128)}, u32[]{:S(2)}) copy-start(s32[1,1,224]{2,1,0:T(1,128)} %param.8) | copy-start | bytes 2692
  17.5 20.7 %copy-start.3 = (s32[1,1,224]{2,1,0:T(1,128)S(1)}, s32[1,1,224]{2,1,0:T(1,128)}, u32[]{:S(2)}) copy-start(s32[1,1,224]{2,1,0:T(1,128)} %param.7) | copy-start | bytes 2692
  17.5 9.1 %collective-permute-start.8 = (bf16[4,128,256]{2,1,0:T(8,128)(2,1)S(1)}, bf16[4,128,256]{2,1,0:T(8,128)(2,1)S(1)}, u32[]{:S(2)}, u32[]{:S(2)}) collective-permute-start(bf16[4,128,256]{2,1,0:T(8,128)(2,1)S(1)} %pad_maximum_fusion.refs_2_), channel_id=1, source_target_pairs={{0,224},{32,0},{64,32},{96,64},{128,96},{160,128},{192,160},{224,1... | collective-permute-start | bytes 786440 | tf_op jit(solution)/shard_map/ppermute | solution.py:22
  20.8 8.8 %collective-permute-start.4 = (bf16[4,128,256]{2,1,0:T(8,128)(2,1)S(1)}, bf16[4,128,256]{2,1,0:T(8,128)(2,1)S(1)}, u32[]{:S(2)}, u32[]{:S(2)}) collective-permute-start(bf16[4,128,256]{2,1,0:T(8,128)(2,1)S(1)} %pad_maximum_fusion.refs_2_), channel_id=1, source_target_pairs={{0,32},{32,64},{64,96},{96,128},{128,160},{160,192},{192,224},{224... | collective-permute-start | bytes 786440 | tf_op jit(solution)/shard_map/ppermute | solution.py:22
  24.7 4.9 %collective-permute-start.15 = (bf16[3,128,256]{2,1,0:T(8,128)(2,1)S(1)}, bf16[3,128,256]{2,1,0:T(8,128)(2,1)S(1)}, u32[]{:S(2)}, u32[]{:S(2)}) collective-permute-start(bf16[3,128,256]{2,1,0:T(8,128)(2,1)S(1)} %pad_maximum_fusion.4), channel_id=1, source_target_pairs={{0,1},{1,0},{2,3},{3,2},{4,5},{5,4},{6,7},{7,6},{8,9},{9,8},{10,11... | collective-permute-start | bytes 589832 | tf_op jit(solution)/shard_map/ppermute | solution.py:22
  24.8 5.6 %collective-permute-start.16 = (bf16[1,128,256]{2,1,0:T(8,128)(2,1)S(1)}, bf16[1,128,256]{2,1,0:T(8,128)(2,1)S(1)}, u32[]{:S(2)}, u32[]{:S(2)}) collective-permute-start(bf16[1,128,256]{2,1,0:T(8,128)(2,1)S(1)} %get-tuple-element.25), channel_id=1, source_target_pairs={{0,32},{1,225},{32,64},{33,1},{64,96},{65,33},{96,128},{97,65},{12... | collective-permute-start | bytes 196616 | tf_op jit(solution)/shard_map/ppermute | solution.py:286
  26.6 8.4 %collective-permute-start.9 = (bf16[4,128,256]{2,1,0:T(8,128)(2,1)S(1)}, bf16[4,128,256]{2,1,0:T(8,128)(2,1)S(1)}, u32[]{:S(2)}, u32[]{:S(2)}) collective-permute-start(bf16[4,128,256]{2,1,0:T(8,128)(2,1)S(1)} %collective-permute-done.8.refs_4_), channel_id=1, source_target_pairs={{0,224},{32,0},{64,32},{96,64},{128,96},{160,128},{192,160},{224,1... | collective-permute-start | bytes 786440 | tf_op jit(solution)/shard_map/ppermute | solution.py:22
  29.6 7.8 %collective-permute-start.5 = (bf16[4,128,256]{2,1,0:T(8,128)(2,1)S(1)}, bf16[4,128,256]{2,1,0:T(8,128)(2,1)S(1)}, u32[]{:S(2)}, u32[]{:S(2)}) collective-permute-start(bf16[4,128,256]{2,1,0:T(8,128)(2,1)S(1)} %collective-permute-done.4.refs_3_), channel_id=1, source_target_pairs={{0,32},{32,64},{64,96},{96,128},{128,160},{160,192},{192,224},{224... | collective-permute-start | bytes 786440 | tf_op jit(solution)/shard_map/ppermute | solution.py:22
  30.4 15.5 %collective-permute-start.17 = (bf16[8,128,256]{2,1,0:T(8,128)(2,1)S(1)}, bf16[8,128,256]{2,1,0:T(8,128)(2,1)S(1)}, u32[]{:S(2)}, u32[]{:S(2)}) collective-permute-start(bf16[8,128,256]{2,1,0:T(8,128)(2,1)S(1)} %slice_dynamic-update-slice_fusion.refs_9_), channel_id=1, source_target_pairs={{0,8},{8,16},{16,24},{24,0},{1,9},{9,17},{17,25},{25,1},{2,10},{10... | collective-permute-start | bytes 1572872 | tf_op jit(solution)/shard_map/ppermute | solution.py:22
  32.3 14.7 %collective-permute-start.19 = (bf16[8,128,256]{2,1,0:T(8,128)(2,1)S(1)}, bf16[8,128,256]{2,1,0:T(8,128)(2,1)S(1)}, u32[]{:S(2)}, u32[]{:S(2)}) collective-permute-start(bf16[8,128,256]{2,1,0:T(8,128)(2,1)S(1)} %slice_dynamic-update-slice_fusion.refs_9_), channel_id=1, source_target_pairs={{0,24},{8,0},{16,8},{24,16},{1,25},{9,1},{17,9},{25,17},{2,26},{10... | collective-permute-start | bytes 1572872 | tf_op jit(solution)/shard_map/ppermute | solution.py:22
  35.1 7.6 %collective-permute-start.10 = (bf16[4,128,256]{2,1,0:T(8,128)(2,1)S(1)}, bf16[4,128,256]{2,1,0:T(8,128)(2,1)S(1)}, u32[]{:S(2)}, u32[]{:S(2)}) collective-permute-start(bf16[4,128,256]{2,1,0:T(8,128)(2,1)S(1)} %collective-permute-done.9.refs_6_), channel_id=1, source_target_pairs={{0,224},{32,0},{64,32},{96,64},{128,96},{160,128},{192,160},{224,1... | collective-permute-start | bytes 786440 | tf_op jit(solution)/shard_map/ppermute | solution.py:22
  37.5 8.3 %collective-permute-start.6 = (bf16[4,128,256]{2,1,0:T(8,128)(2,1)S(1)}, bf16[4,128,256]{2,1,0:T(8,128)(2,1)S(1)}, u32[]{:S(2)}, u32[]{:S(2)}) collective-permute-start(bf16[4,128,256]{2,1,0:T(8,128)(2,1)S(1)} %collective-permute-done.5.refs_5_), channel_id=1, source_target_pairs={{0,32},{32,64},{64,96},{96,128},{128,160},{160,192},{192,224},{224... | collective-permute-start | bytes 786440 | tf_op jit(solution)/shard_map/ppermute | solution.py:22
  42.7 10.8 %collective-permute-start.11 = (bf16[2,128,256]{2,1,0:T(8,128)(2,1)S(1)}, bf16[2,128,256]{2,1,0:T(8,128)(2,1)S(1)}, u32[]{:S(2)}, u32[]{:S(2)}) collective-permute-start(bf16[2,128,256]{2,1,0:T(8,128)(2,1)S(1)} %slice.139), channel_id=1, source_target_pairs={{0,224},{32,0},{64,32},{96,64},{128,96},{160,128},{192,160},{224,1... | collective-permute-start | bytes 393224 | tf_op jit(solution)/shard_map/ppermute | solution.py:22
  45.8 7.7 %collective-permute-start.7 = (bf16[2,128,256]{2,1,0:T(8,128)(2,1)S(1)}, bf16[2,128,256]{2,1,0:T(8,128)(2,1)S(1)}, u32[]{:S(2)}, u32[]{:S(2)}) collective-permute-start(bf16[2,128,256]{2,1,0:T(8,128)(2,1)S(1)} %slice.138), channel_id=1, source_target_pairs={{0,32},{32,64},{64,96},{96,128},{128,160},{160,192},{192,224},{224... | collective-permute-start | bytes 393224 | tf_op jit(solution)/shard_map/ppermute | solution.py:22
  45.9 7.7 %collective-permute-start.18 = (bf16[4,128,256]{2,1,0:T(8,128)(2,1)S(1)}, bf16[4,128,256]{2,1,0:T(8,128)(2,1)S(1)}, u32[]{:S(2)}, u32[]{:S(2)}) collective-permute-start(bf16[4,128,256]{2,1,0:T(8,128)(2,1)S(1)} %slice.147), channel_id=1, source_target_pairs={{0,8},{8,16},{16,24},{24,0},{1,9},{9,17},{17,25},{25,1},{2,10},{10... | collective-permute-start | bytes 786440 | tf_op jit(solution)/shard_map/ppermute | solution.py:22
  47.0 6.6 %collective-permute-start.20 = (bf16[4,128,256]{2,1,0:T(8,128)(2,1)S(1)}, bf16[4,128,256]{2,1,0:T(8,128)(2,1)S(1)}, u32[]{:S(2)}, u32[]{:S(2)}) collective-permute-start(bf16[4,128,256]{2,1,0:T(8,128)(2,1)S(1)} %slice.148), channel_id=1, source_target_pairs={{0,24},{8,0},{16,8},{24,16},{1,25},{9,1},{17,9},{25,17},{2,26},{10... | collective-permute-start | bytes 786440 | tf_op jit(solution)/shard_map/ppermute | solution.py:22
  55.6 2.8 %collective-permute-start.21 = (f32[1032,256]{1,0:T(8,128)S(1)}, f32[1032,256]{1,0:T(8,128)S(1)}, u32[]{:S(2)}, u32[]{:S(2)}) collective-permute-start(f32[1032,256]{1,0:T(8,128)S(1)} %get-tuple-element.16), channel_id=1, source_target_pairs={{0,1},{1,0},{2,3},{3,2},{4,5},{5,4},{6,7},{7,6},{8,9},{9,8},{10,11... | collective-permute-start | bytes 3170312 | tf_op jit(solution)/shard_map/ppermute | solution.py:22
  58.7 12.6 %copy-start.1 = (f32[256]{0:T(256)S(1)}, f32[256]{0:T(256)}, u32[]{:S(2)}) copy-start(f32[256]{0:T(256)} %param.11) | copy-start | bytes 3076
  58.9 6.0 %collective-permute-start.23 = (f16[272,256]{1,0:T(8,128)(2,1)S(1)}, f16[272,256]{1,0:T(8,128)(2,1)S(1)}, u32[]{:S(2)}, u32[]{:S(2)}) collective-permute-start(f16[272,256]{1,0:T(8,128)(2,1)S(1)} %get-tuple-element.34), channel_id=1, source_target_pairs={{0,2},{2,4},{4,6},{6,0},{1,3},{3,5},{5,7},{7,1},{8,10},{10,12},{12... | collective-permute-start | bytes 417800 | tf_op jit(solution)/shard_map/ppermute | solution.py:22
  60.9 6.2 %collective-permute-start.24 = (f16[272,256]{1,0:T(8,128)(2,1)S(1)}, f16[272,256]{1,0:T(8,128)(2,1)S(1)}, u32[]{:S(2)}, u32[]{:S(2)}) collective-permute-start(f16[272,256]{1,0:T(8,128)(2,1)S(1)} %get-tuple-element.35), channel_id=1, source_target_pairs={{0,6},{2,0},{4,2},{6,4},{1,7},{3,1},{5,3},{7,5},{8,14},{10,8},{12,... | collective-permute-start | bytes 417800 | tf_op jit(solution)/shard_map/ppermute | solution.py:22
  61.0 10.3 %collective-permute-start.22 = (f16[272,256]{1,0:T(8,128)(2,1)S(1)}, f16[272,256]{1,0:T(8,128)(2,1)S(1)}, u32[]{:S(2)}, u32[]{:S(2)}) collective-permute-start(f16[272,256]{1,0:T(8,128)(2,1)S(1)} %get-tuple-element.33), channel_id=1, source_target_pairs={{0,4},{2,6},{4,0},{6,2},{1,5},{3,7},{5,1},{7,3},{8,12},{10,14},{12... | collective-permute-start | bytes 417800 | tf_op jit(solution)/shard_map/ppermute | solution.py:22
  84.5 1.3 %collective-permute-start.25 = (f32[24,128]{1,0:T(8,128)S(1)}, f32[24,128]{1,0:T(8,128)S(1)}, u32[]{:S(2)}, u32[]{:S(2)}) collective-permute-start(f32[24,128]{1,0:T(8,128)S(1)} %reduce_sum.18), channel_id=1, source_target_pairs={{0,1},{1,0},{2,3},{3,2},{4,5},{5,4},{6,7},{7,6},{8,9},{9,8},{10,11... | collective-permute-start | bytes 36872 | tf_op jit(solution)/shard_map/ppermute | solution.py:22
